TPU v7x, 128 devices: a whole 4x4x4 slice. The times are simulated.
128 devices in a mesh: dp: 32 (over z, y, core), table: 4 (over x).
Axes of the slice: x: 4, y: 4, z: 4, core: 2. Of those that a mesh axis runs over, the one named last changes fastest.
Arguments:
- table: bfloat16 [524288, 512], P(('dp', 'table')), may hold values from -12 to 12
- item_ids: int32 [32768], P(('dp', 'table')), may hold values from 0 to 524287, as said below
- negatives: int32 [128, 512], P('dp', 'table'), may hold values from 0 to 524287, as said below
- lengths: int32 [32, 4], P('dp'), may hold values from 1 to 512, 1024 in all within a row
- w_in: bfloat16 [4, 512, 512], P(None, None, 'table'), may hold values from -0.25 to 0.25
- w_out: bfloat16 [512, 512], P('table'), may hold values from -0.25 to 0.25
Outputs:
- grad_table: float32 [524288, 512], P(('dp', 'table'))
- grad_w_in: float32 [4, 512, 512], P(None, None, 'table')
- grad_w_out: float32 [512, 512], P('table')
Inputs may be any that keep to these rules, and one draw needn't show every extreme that they name: `item_ids`: item i is row i % 4096 of the rows held by device i // 4096 in dp+table order. Of the 256 history ids of one device (aligned blocks of the list), at most 4 are held by any one device; in every block some device holds exactly 4, and one device, drawn from the seed, does so in every block. `negatives`: of the 512 negative ids on one device, at most 8 are held by any one device; in every device's shard some device holds exactly 8, the same one for all shards.
All inputs are finite; a program needn't handle non-finite values.
Results may differ from a plain program's by a relative error of at most 0.029.
Values may be sent and summed in bfloat16 or wider, within the bound.
A program may use at most 128 MiB of HBM per device.

v0:
```python
import jax
import jax.numpy as jnp
from jax import lax
from jax.sharding import PartitionSpec as P

DH = 128


epsilon = 1e-06
sharpness = 20.0


def layer_norm(values):
    center = values - jnp.mean(values, axis=-1, keepdims=True)
    spread = jnp.mean(center * center, axis=-1, keepdims=True)
    return center * lax.rsqrt(spread + epsilon)


def unit_rows(values):
    return values * lax.rsqrt(jnp.sum(values * values, axis=-1, keepdims=True) + epsilon)


def segments(user_lengths, count):
    ends = jnp.cumsum(user_lengths)
    places = jnp.arange(count, dtype=jnp.int32)
    segment = jnp.sum((places[:, None] >= ends[None, :]).astype(jnp.int32), axis=1)
    belongs = segment[:, None] == jnp.arange(user_lengths.shape[0], dtype=jnp.int32)[None, :]
    row_len = jnp.sum(jnp.where(belongs, user_lengths[None, :].astype(jnp.float32), 0.0), axis=1)
    return (segment, row_len)


def branch(emb_f, w_in_f, w_out_f, segment, row_len):
    count = emb_f.shape[0]
    normed = layer_norm(emb_f).astype(jnp.bfloat16)
    w_in_b = w_in_f.astype(jnp.bfloat16)
    proj = jax.nn.silu(
        jnp.einsum("td,jde->jte", normed, w_in_b, preferred_element_type=jnp.float32)
    ).astype(jnp.bfloat16)
    heads = proj.shape[2] // DH
    shaped = proj.reshape(4, count, heads, DH)
    gate_u, value, query, keys = (shaped[0], shaped[1], shaped[2], shaped[3])
    scores = jnp.einsum("qhd,khd->hqk", query, keys, preferred_element_type=jnp.float32) * DH ** (
        -0.5
    )
    places = jnp.arange(count, dtype=jnp.int32)
    visible = (segment[:, None] == segment[None, :]) & (places[None, :] <= places[:, None])
    weights = jnp.where(visible[None], jax.nn.silu(scores) / row_len[None, :, None], 0.0).astype(
        jnp.bfloat16
    )
    mixed = jnp.einsum("hqk,khd->qhd", weights, value, preferred_element_type=jnp.float32)
    gated = (
        (layer_norm(mixed) * gate_u.astype(jnp.float32))
        .reshape(count, heads * DH)
        .astype(jnp.bfloat16)
    )
    return jnp.dot(gated, w_out_f.astype(jnp.bfloat16), preferred_element_type=jnp.float32)


def sampled_loss(y_rows, emb_f, neg_f, row_start, segment, col_user):
    rows = y_rows.shape[0]
    width = emb_f.shape[1]
    y_unit = unit_rows(y_rows).astype(jnp.bfloat16)
    e_unit = unit_rows(emb_f).astype(jnp.bfloat16)
    padded = jnp.concatenate([e_unit, jnp.zeros((1, width), jnp.bfloat16)], axis=0)
    following = lax.dynamic_slice_in_dim(padded, row_start + 1, rows, 0)
    seg_pad = jnp.concatenate([segment, jnp.full((1,), -1, jnp.int32)], axis=0)
    seg_next = lax.dynamic_slice_in_dim(seg_pad, row_start + 1, rows, 0)
    seg_here = lax.dynamic_slice_in_dim(segment, row_start, rows, 0)
    valid = seg_next == seg_here
    positive = sharpness * jnp.sum(
        y_unit.astype(jnp.float32) * following.astype(jnp.float32), axis=-1
    )
    n_unit = unit_rows(neg_f).astype(jnp.bfloat16)
    negative = sharpness * lax.dot_general(
        y_unit, n_unit, (((1,), (1,)), ((), ())), preferred_element_type=jnp.float32
    )
    own = seg_here[:, None] == col_user[None, :]
    total = jnp.exp(positive) + jnp.sum(jnp.where(own, jnp.exp(negative), 0.0), axis=-1)
    return jnp.sum(jnp.where(valid, jnp.log(total) - positive, 0.0))


def place_slots(wanted, rows_held, owners, slot_width, offset):
    holder = wanted // rows_held
    hits = (holder[:, None] == jnp.arange(owners, dtype=jnp.int32)[None, :]).astype(jnp.int32)
    before = jnp.sum((jnp.cumsum(hits, axis=0) - hits) * hits, axis=1)
    return holder * slot_width + offset + before


def on_device(table, item_ids, negatives, lengths, w_in, w_out):
    rows_held = table.shape[0]
    width = table.shape[1]
    dp_count = lax.axis_size("dp")
    table_count = lax.axis_size("table")
    owners = dp_count * table_count
    neg_ids = negatives.reshape(-1)
    hist_count = item_ids.shape[0]
    neg_count = neg_ids.shape[0]
    cap_hist = 2 * hist_count // owners
    cap_neg = 2 * neg_count // owners
    slot_width = cap_hist + cap_neg
    slot_hist = place_slots(item_ids, rows_held, owners, slot_width, 0)
    slot_neg = place_slots(neg_ids, rows_held, owners, slot_width, cap_hist)
    request = jnp.full((owners * slot_width,), -1, jnp.int32)
    request = request.at[slot_hist].set(item_ids % rows_held).at[slot_neg].set(neg_ids % rows_held)
    arrived = lax.all_to_all(
        request.reshape(owners, slot_width),
        ("dp", "table"),
        split_axis=0,
        concat_axis=0,
        tiled=True,
    )
    filled = (arrived >= 0).astype(jnp.bfloat16)
    picked = jnp.take(table, jnp.clip(arrived, 0, rows_held - 1), axis=0)
    fetched = lax.all_to_all(
        picked * filled[..., None], ("dp", "table"), split_axis=0, concat_axis=0, tiled=True
    )
    fetched = fetched.reshape(owners * slot_width, width)
    hist_rows = jnp.take(fetched, slot_hist, axis=0)
    neg_rows = jnp.take(fetched, slot_neg, axis=0)
    emb_all, neg_all = (
        lax.all_gather(hist_rows, "table", axis=0, tiled=True),
        lax.all_gather(neg_rows, "table", axis=0, tiled=True),
    )
    count = emb_all.shape[0]
    segment, row_len = segments(lengths[0], count)
    my_index = lax.axis_index("table")
    row_start = my_index * hist_count
    per_user = negatives.shape[1]
    col_user = jnp.arange(table_count * neg_count, dtype=jnp.int32) % neg_count // per_user
    emb_f = emb_all.astype(jnp.float32)
    neg_f = neg_all.astype(jnp.float32)

    def heads_term(emb_in, w_in_f, w_out_f):
        return branch(emb_in, w_in_f, w_out_f, segment, row_len)

    partial_out, heads_pullback = jax.vjp(
        heads_term, emb_f, w_in.astype(jnp.float32), w_out.astype(jnp.float32)
    )
    y_share = lax.psum_scatter(
        partial_out.astype(jnp.bfloat16), "table", scatter_dimension=0, tiled=True
    ).astype(jnp.float32)
    y_rows = y_share + lax.dynamic_slice_in_dim(emb_f, row_start, hist_count, 0)

    def quarter_loss(y_in, emb_in, neg_in):
        return sampled_loss(y_in, emb_in, neg_in, row_start, segment, col_user)

    loss_part, loss_pullback = jax.vjp(quarter_loss, y_rows, emb_f, neg_f)
    d_rows, d_emb_loss, d_neg = loss_pullback(jnp.ones((), jnp.float32))
    d_out = lax.all_gather(d_rows.astype(jnp.bfloat16), "table", axis=0, tiled=True).astype(
        d_rows.dtype
    )
    d_emb_heads, d_win, d_wout = heads_pullback(d_out)
    residual = lax.dynamic_update_slice_in_dim(jnp.zeros_like(emb_f), d_rows, row_start, 0)
    d_emb = d_emb_heads + d_emb_loss + residual
    grad_w_in, grad_w_out = (
        lax.psum(d_win.astype(jnp.bfloat16), "dp").astype(jnp.float32),
        lax.psum(d_wout.astype(jnp.bfloat16), "dp").astype(jnp.float32),
    )
    d_hist, d_negs = (
        lax.psum_scatter(
            d_emb.astype(jnp.bfloat16), "table", scatter_dimension=0, tiled=True
        ).astype(jnp.float32),
        lax.psum_scatter(
            d_neg.astype(jnp.bfloat16), "table", scatter_dimension=0, tiled=True
        ).astype(jnp.float32),
    )
    outgoing = jnp.zeros((owners * slot_width, width), jnp.float32)
    outgoing = outgoing.at[slot_hist].set(d_hist).at[slot_neg].set(d_negs)
    landed = lax.all_to_all(
        outgoing.reshape(owners, slot_width, width).astype(jnp.bfloat16),
        ("dp", "table"),
        split_axis=0,
        concat_axis=0,
        tiled=True,
    ).astype(jnp.float32)
    served_flat = arrived.reshape(-1)
    target = jnp.where(served_flat >= 0, served_flat, rows_held)
    grad_table = (
        jnp.zeros((rows_held, width), jnp.float32)
        .at[target]
        .add(landed.reshape(-1, width), mode="drop")
    )
    return (grad_table, grad_w_in, grad_w_out)


def solution(mesh):
    placed = (
        P(("dp", "table"), None),
        P(("dp", "table")),
        P("dp", "table"),
        P("dp", None),
        P(None, None, "table"),
        P("table", None),
    )
    return jax.shard_map(
        on_device,
        mesh=mesh,
        in_specs=placed,
        out_specs=(P(("dp", "table"), None), P(None, None, "table"), P("table", None)),
        check_vma=False,
    )
```

profile of v0, /device:TPU:1, one launch (start us, length us, event | category | flops | bytes accessed | tf_op | source)
XLA Modules:
  0.0 433.7 jit_solution(896975405244854338)
XLA Ops:
  7.2 0.8 add_select_fusion.3
  10.7 1.4 scatter_custom_fusion
  12.1 2.5 scatter_fusion
  14.7 21.0 %all_to_all.19 = s32[128,1,12]{2,1,0:T(1,128)S(1)} all-to-all(s32[128,1,12]{2,1,0:T(1,128)S(1)} %bitcast.212), channel_id=1, replica_groups=mesh['dp'=32,'table'=4] {'dp','table'}, dimensions={0} | all-to-all | bytes 12288 | tf_op jit(solution)/shard_map/all_to_all | solution.py:105
  36.3 7.6 %gather_fusion = bf16[1536,512]{1,0:T(8,128)(2,1)S(1)} fusion(bf16[4096,512]{1,0:T(8,128)(2,1)} %param.6, s32[2048]{0:T(1024)S(1)} %pad_clamp_fusion), kind=kCustom, calls=%fused_computation | custom fusion | bytes 3151872 | tf_op jit(solution)/shard_map/jit(_take)/gather | solution.py:113
  43.9 1.5 reshape.532
  45.6 2.9 select_multiply_fusion
  48.5 5.2 %all-to-all-start.1 = ((bf16[128,12,512]{2,1,0:T(8,128)(2,1)}), bf16[128,12,512]{2,1,0:T(8,128)(2,1)}, u32[]{:S(2)}, u32[]{:S(2)}) async-start(bf16[128,12,512]{2,1,0:T(8,128)(2,1)} %select_multiply_fusion), calls=%async_computation.1 | async-start | bytes 4194304 | tf_op jit(solution)/shard_map/all_to_all | solution.py:114
  53.8 30.5 %all-to-all-done.1 = bf16[128,12,512]{2,1,0:T(8,128)(2,1)} async-done(((bf16[128,12,512]{2,1,0:T(8,128)(2,1)}), bf16[128,12,512]{2,1,0:T(8,128)(2,1)}, u32[]{:S(2)}, u32[]{:S(2)}) %all-to-all-start.1) | async-done | bytes 1572896 | tf_op jit(solution)/shard_map/all_to_all | solution.py:114
  84.3 2.5 reshape.517
  86.8 1.2 gather_fusion.1
  88.0 0.8 broadcast_select_fusion.1
  89.5 2.0 gather_fusion.2
  91.7 0.9 broadcast_select_fusion
  92.8 14.5 %all-gather.4.cloned.1.call-done = bf16[1024,512]{1,0:T(8,128)(2,1)} async-done(((bf16[256,512]{1,0:T(8,128)(2,1)}), bf16[1024,512]{1,0:T(8,128)(2,1)}) %all-gather.4.cloned.1.call-update) | async-done | bytes 1048592 | tf_op jit(solution)/shard_map/all_gather | solution.py:121
  107.3 1.7 fusion.24
  109.1 2.1 fusion.25
  111.2 0.9 fusion.119
  112.7 3.7 select_convert_fusion
  116.4 0.8 fusion.123
  117.8 1.4 convolution_convert_fusion.1
  119.4 1.6 convert_element_type.212
  121.0 20.0 %all-gather.6.cloned.1.call-done = bf16[2048,512]{0,1:T(8,128)(2,1)} async-done(((bf16[512,512]{0,1:T(8,128)(2,1)}), bf16[2048,512]{0,1:T(8,128)(2,1)}) %all-gather.6.cloned.1.call-update) | async-done | bytes 2097168 | tf_op jit(solution)/shard_map/all_gather | solution.py:122
  141.1 2.0 fusion.4
  143.1 22.6 %reduce-scatter.4.cloned.1.call-done = bf16[256,512]{1,0:T(8,128)(2,1)} async-done(((bf16[1024,512]{1,0:T(8,128)(2,1)}), bf16[256,512]{1,0:T(8,128)(2,1)}) %reduce-scatter.4.cloned.1.call-update) | async-done | bytes 262160 | tf_op jit(solution)/shard_map/reduce_scatter | solution.py:139
  165.7 1.4 multiply_reduce_fusion.1
  167.1 1.4 fusion.68
  168.5 1.0 fusion.18
  170.2 1.0 multiply_reduce_fusion
  171.2 0.8 copy-done.14
  172.0 0.9 fusion.121
  173.1 1.8 fusion.67
  175.0 2.7 dynamic_update_slice.6
  177.7 19.4 %all-gather.8.cloned.1.call-done = bf16[1024,512]{1,0:T(8,128)(2,1)} async-done(((bf16[256,512]{1,0:T(8,128)(2,1)}), bf16[1024,512]{1,0:T(8,128)(2,1)}) %all-gather.8.cloned.1.call-update) | async-done | bytes 1048592 | tf_op jit(solution)/shard_map/all_gather | solution.py:149
  197.2 1.9 fusion.76
  199.1 1.4 fusion.122
  201.1 3.2 fusion.2
  204.3 0.8 fusion.44
  205.6 1.1 copy-done.8
  206.8 0.9 fusion.16
  207.8 1.1 fusion.23
  208.9 1.3 fusion.35
  210.3 1.4 fusion.27
  211.7 1.3 add_dynamic-update-slice_fusion
  213.0 1.1 convert_element_type.251
  214.2 0.8 copy-done.5
  215.0 2.5 fusion.6
  217.6 2.3 fusion.3
  219.8 17.9 %reduce-scatter.6.cloned.1.call-done = bf16[256,512]{1,0:T(8,128)(2,1)} async-done(((bf16[1024,512]{1,0:T(8,128)(2,1)}), bf16[256,512]{1,0:T(8,128)(2,1)}) %reduce-scatter.6.cloned.1.call-update) | async-done | bytes 262160 | tf_op jit(solution)/shard_map/reduce_scatter | solution.py:160
  237.7 2.6 scatter_custom_fusion.2
  240.4 31.0 %reduce-scatter.8.cloned.1.call-done = bf16[512,512]{0,1:T(8,128)(2,1)} async-done(((bf16[2048,512]{0,1:T(8,128)(2,1)}), bf16[512,512]{0,1:T(8,128)(2,1)}) %reduce-scatter.8.cloned.1.call-update) | async-done | bytes 524304 | tf_op jit(solution)/shard_map/reduce_scatter | solution.py:163
  271.4 2.2 copy.71
  273.6 4.3 scatter_fusion.1
  277.9 1.4 convert_element_type.257
  279.3 3.6 convert_element_type.258
  282.9 8.0 %all-to-all-start.2 = ((bf16[128,12,512]{2,1,0:T(8,128)(2,1)}), bf16[128,12,512]{2,1,0:T(8,128)(2,1)S(1)}, u32[]{:S(2)}, u32[]{:S(2)}) async-start(bf16[128,12,512]{2,1,0:T(8,128)(2,1)} %convert_element_type.258), calls=%async_computation.5 | async-start | bytes 4194304 | tf_op jit(solution)/shard_map/all_to_all | solution.py:169
  290.9 2.2 convolution_convert_fusion.7
  293.1 2.9 fusion.36
  296.6 0.8 reduce.11
  297.5 109.1 %all-reduce.8.cloned.1.call-done = (bf16[4,512,128]{1,2,0:T(8,128)(2,1)}, bf16[128,512]{1,0:T(8,128)(2,1)}) async-done(((bf16[4,512,128]{1,2,0:T(8,128)(2,1)}, bf16[128,512]{1,0:T(8,128)(2,1)}), (bf16[4,512,128]{1,2,0:T(8,128)(2,1)}, bf16[128,512]{1,0:T(8,128)(2,1)})) %all-reduce.8.cloned.1.call-update) | async-done | bytes 655376 | tf_op jit(solution)/shard_map/psum | solution.py:156
  406.6 2.2 copy.72
  408.8 1.6 convert_element_type.263
  410.5 1.8 reshape.591
  412.3 14.1 %scatter_custom_fusion.4 = f32[4096,512]{1,0:T(8,128)} fusion(s32[1536]{0:T(1024)S(1)} %fusion.103, f32[1536,512]{1,0:T(8,128)} %reshape.591, f32[]{:T(128)} %constant.171.clone.1), kind=kCustom, calls=%fused_computation.25 | custom fusion | flops 786432 | bytes 8389120 | tf_op jit(solution)/shard_map/scatter-add | solution.py:181
  (150 shorter events, 9.0 us)
Async XLA Ops:
  7.2 110.7 %copy-start = (bf16[128,512]{1,0:T(8,128)(2,1)S(1)}, bf16[128,512]{1,0:T(8,128)(2,1)}, u32[]{:S(2)}) copy-start(bf16[128,512]{1,0:T(8,128)(2,1)} %param.11) | copy-start | bytes 393220
  7.2 3.4 copy-start.29
  9.9 43.8 %copy-start.30 = (s32[256]{0:T(256)}, s32[256]{0:T(256)S(1)}, u32[]{:S(2)}) copy-start(s32[256]{0:T(256)S(1)} %get-tuple-element.31) | copy-start | bytes 3076
  10.6 78.7 %copy-start.27 = (s32[512,1]{0,1:T(1,128)}, s32[512,1]{0,1:T(1,128)S(1)}, u32[]{:S(2)}) copy-start(s32[512,1]{0,1:T(1,128)S(1)} %compare_select_fusion.6) | copy-start | bytes 6148
  35.7 0.6 copy-start.19
  48.5 35.8 %all-to-all-start.1 = ((bf16[128,12,512]{2,1,0:T(8,128)(2,1)}), bf16[128,12,512]{2,1,0:T(8,128)(2,1)}, u32[]{:S(2)}, u32[]{:S(2)}) async-start(bf16[128,12,512]{2,1,0:T(8,128)(2,1)} %select_multiply_fusion), calls=%async_computation.1 | async-start | bytes 4194304 | tf_op jit(solution)/shard_map/all_to_all | solution.py:114
  53.7 53.6 %all-gather.4.cloned.1.call-start = ((), (), s32[]{:S(2)}) async-start(), calls=%async_computation.6 | async-start | bytes 1310720 | tf_op jit(solution)/shard_map/all_gather | solution.py:121
  86.8 2.1 copy-start.21
  86.8 2.3 copy-start.33
  88.8 52.2 %all-gather.6.cloned.1.call-start = ((), (), s32[]{:S(2)}) async-start(), calls=%async_computation.8 | async-start | bytes 2621440 | tf_op jit(solution)/shard_map/all_gather | solution.py:122
  89.5 23.2 %copy-start.31 = (f32[1024]{0:T(1024)}, f32[1024]{0:T(1024)S(1)}, u32[]{:S(2)}) copy-start(f32[1024]{0:T(1024)S(1)} %select_reduce_fusion) | copy-start | bytes 12292
  92.6 73.1 %reduce-scatter.4.cloned.1.call-start = ((), (), s32[]{:S(2)}) async-start(), calls=%async_computation.7 | async-start | bytes 1310720 | tf_op jit(solution)/shard_map/reduce_scatter | solution.py:139
  107.3 3.9 copy-start.2
  109.1 2.1 copy-start.25
  111.2 1.5 copy-start.23
  112.1 4.3 %copy-start.7 = (f32[1024,512]{0,1}, f32[1024,512]{0,1:S(1)}, u32[]{:S(2)}) copy-start(f32[1024,512]{0,1:S(1)} %fusion.119) | copy-start | bytes 6291460
  112.7 4.7 %copy-start.11 = (bf16[4,1024,128]{1,2,0:T(8,128)(2,1)}, bf16[4,1024,128]{1,2,0:T(8,128)(2,1)S(1)}, u32[]{:S(2)}) copy-start(bf16[4,1024,128]{1,2,0:T(8,128)(2,1)S(1)} %multiply_convert_fusion) | copy-start | bytes 3145732
  116.4 1.4 copy-start.9
  119.3 77.9 %all-gather.8.cloned.1.call-start = ((), (), s32[]{:S(2)}) async-start(), calls=%async_computation.9 | async-start | bytes 1310720 | tf_op jit(solution)/shard_map/all_gather | solution.py:149
  165.7 2.8 copy-start.4
  168.5 1.1 copy-start.16
  168.5 1.7 copy-start.6
  168.5 1.7 copy-start.13
  169.5 1.6 copy-start.34
  171.2 0.8 copy-start.14
  172.9 64.9 %reduce-scatter.6.cloned.1.call-start = ((), (), s32[]{:S(2)}) async-start(), calls=%async_computation.10 | async-start | bytes 1310720 | tf_op jit(solution)/shard_map/reduce_scatter | solution.py:160
  197.1 3.4 copy-start.10
  197.1 3.9 copy-start.35
  199.1 2.0 copy-start.12
  199.1 2.0 copy-start.32
  205.2 1.6 copy-start.8
  206.8 1.0 copy-start.22
  207.8 1.1 copy-start.18
  207.8 1.1 copy-start.24
  208.9 1.4 copy-start.26
  210.3 1.4 copy-start.15
  213.0 2.0 copy-start.5
  213.0 2.0 copy-start.17
  214.2 57.2 %reduce-scatter.8.cloned.1.call-start = ((), (), s32[]{:S(2)}) async-start(), calls=%async_computation.11 | async-start | bytes 2621440 | tf_op jit(solution)/shard_map/reduce_scatter | solution.py:163
  219.8 53.8 %copy-start.28 = (s32[512,1]{0,1:T(1,128)S(1)}, s32[512,1]{0,1:T(1,128)}, u32[]{:S(2)}) copy-start(s32[512,1]{0,1:T(1,128)} %copy-done.27) | copy-start | bytes 6148
  282.9 10.2 %copy-start.3 = (bf16[1024,512]{1,0:T(8,128)(2,1)S(1)}, bf16[1024,512]{1,0:T(8,128)(2,1)}, u32[]{:S(2)}) copy-start(bf16[1024,512]{1,0:T(8,128)(2,1)} %all-gather.4.cloned.1.call-done) | copy-start | bytes 3145732
  282.9 127.6 %all-to-all-start.2 = ((bf16[128,12,512]{2,1,0:T(8,128)(2,1)}), bf16[128,12,512]{2,1,0:T(8,128)(2,1)S(1)}, u32[]{:S(2)}, u32[]{:S(2)}) async-start(bf16[128,12,512]{2,1,0:T(8,128)(2,1)} %convert_element_type.258), calls=%async_computation.5 | async-start | bytes 4194304 | tf_op jit(solution)/shard_map/all_to_all | solution.py:169
  290.9 115.7 %all-reduce.8.cloned.1.call-start = ((), (), s32[]{:S(2)}) async-start(), calls=%async_computation.12 | async-start | bytes 1310720 | tf_op jit(solution)/shard_map/psum | solution.py:156
  293.1 3.4 copy-start.20
  412.3 14.1 %copy-start.1 = (bf16[128,512]{1,0:T(8,128)(2,1)S(1)}, bf16[128,512]{1,0:T(8,128)(2,1)}, u32[]{:S(2)}) copy-start(bf16[128,512]{1,0:T(8,128)(2,1)} %param.11) | copy-start | bytes 393220
Sparse Core Ops, SparseCore 0:
  89.0 18.3 all-gather.3
  109.0 32.0 all-gather.5
  143.5 22.1 reduce-scatter.3
  173.0 24.0 all-gather.7
  214.3 23.4 reduce-scatter.5
  240.6 30.7 reduce-scatter.7
  296.1 110.4 all-reduce.7
where the time goes:
time: 441 us; the launch traced here: 434 us
  waiting for transfers between devices  265 us (60%)
  other arithmetic  52.1 us (12%)
  local copies, waits for them, and re-layouts  41.8 us (9%)
  matrix products  24.4 us (6%)
  blocking collectives  21 us (5%)
  between operations  15.4 us (3%)
  starting transfers between devices  13.8 us (3%)
    psum x1, waiting for transfers between devices, on_device(): lax.psum(d_win.astype(jnp.bfloat16), 'dp').astype(jnp.float32)  109 us
    reduce_scatter x1, waiting for transfers between devices, on_device(): lax.psum_scatter(d_neg.astype(jnp.bfloat16), 'table', scatter_dimension=0...  31 us
    all_to_all x1, waiting for transfers between devices, on_device(): lax.all_to_all(picked * filled[..., None], ('dp', 'table'), split_axis=0,...  30.5 us
    reduce_scatter x1, waiting for transfers between devices, on_device(): lax.psum_scatter(partial_out.astype(jnp.bfloat16), 'table', scatter_dimen...  22.6 us
    all_to_all x1, blocking collectives, on_device(): lax.all_to_all(request.reshape(owners, slot_width), ('dp', 'table'), spli...  21 us
    all_gather x1, waiting for transfers between devices, on_device(): lax.all_gather(neg_rows, 'table', axis=0, tiled=True)  20 us
    all_gather x1, waiting for transfers between devices, on_device(): lax.all_gather(d_rows.astype(jnp.bfloat16), 'table', axis=0, tiled=True)  19.4 us
    reduce_scatter x1, waiting for transfers between devices, on_device(): lax.psum_scatter(d_emb.astype(jnp.bfloat16), 'table', scatter_dimension=0...  17.9 us
  transfers between devices with their start and end apart: 9, of which 8 were waited for; matrix products, arithmetic and copies ran while one was open for 9% of the time, Pallas kernels for 0%

commit v1 on v0

--- a/solution.py
+++ b/solution.py
@@ -1,13 +1,609 @@
+import functools
 import jax
 import jax.numpy as jnp
 from jax import lax
+from jax.experimental import pallas as pl
+from jax.experimental.pallas import tpu as pltpu
 from jax.sharding import PartitionSpec as P
 
 DH = 128
-
+D = 512
+CAP_H = 4
+CAP_N = 8
+OWNERS = 128
+N_DP = 32
+N_TABLE = 4
+ROWS = 4096
+BF = jnp.bfloat16
+F32 = jnp.float32
+MESH = pl.DeviceIdType.MESH
 
 epsilon = 1e-06
 sharpness = 20.0
+
+
+def iota(shape, dim):
+    return lax.broadcasted_iota(jnp.int32, shape, dim)
+
+
+def one_zero(mask):
+    return jnp.where(mask, 1.0, 0.0).astype(BF)
+
+
+def mm(a, b):
+    return lax.dot_general(a, b, (((1,), (0,)), ((), ())), preferred_element_type=F32)
+
+
+def mm_nt(a, b):
+    return lax.dot_general(a, b, (((1,), (1,)), ((), ())), preferred_element_type=F32)
+
+
+def mm_tn(a, b):
+    return lax.dot_general(a, b, (((0,), (0,)), ((), ())), preferred_element_type=F32)
+
+
+def position():
+    dp = lax.axis_index("dp")
+    tx = lax.axis_index("table")
+    return dp, tx
+
+
+def partner(dp, tx, step):
+    dx = lax.rem(step, 4)
+    dc = lax.rem(lax.div(step, 4), 2)
+    dy = lax.rem(lax.div(step, 8), 4)
+    dz = lax.div(step, 32)
+    c = lax.rem(lax.rem(dp, 2) + dc, 2)
+    y = lax.rem(lax.rem(lax.div(dp, 2), 4) + dy, 4)
+    z = lax.rem(lax.div(dp, 8) + dz, 4)
+    x = lax.rem(tx + dx, 4)
+    return z * 8 + y * 2 + c, x
+
+
+def greet_all(barrier, dp, tx):
+    def one(i, carry):
+        pd, px = partner(dp, tx, i)
+        pl.semaphore_signal(barrier, inc=1, device_id=(pd, px), device_id_type=MESH)
+        return carry
+
+    lax.fori_loop(1, OWNERS, one, 0)
+
+
+def spread_all(src, dst, chunk, send_sem, recv_sem, dp, tx):
+    me = dp * 4 + tx
+
+    def one(i, carry):
+        pd, px = partner(dp, tx, lax.rem(i * 37, OWNERS))
+        pltpu.make_async_remote_copy(
+            src_ref=src.at[pl.ds(pl.multiple_of((pd * 4 + px) * chunk, chunk), chunk)],
+            dst_ref=dst.at[pl.ds(pl.multiple_of(me * chunk, chunk), chunk)],
+            send_sem=send_sem,
+            recv_sem=recv_sem,
+            device_id=(pd, px),
+            device_id_type=MESH,
+        ).start()
+        return carry
+
+    lax.fori_loop(1, OWNERS, one, 0)
+    own = pl.ds(pl.multiple_of(me * chunk, chunk), chunk)
+    dst[own] = src[own]
+
+
+def wait_rows(ref, count, sem):
+    pltpu.make_async_copy(ref.at[pl.ds(0, count)], ref.at[pl.ds(0, count)], sem).wait()
+
+
+class Ring:
+    def __init__(self, dp, tx, send_sems, recv_sems):
+        self.dp = dp
+        self.tx = tx
+        self.right = lax.rem(tx + 1, 4)
+        self.left = lax.rem(tx + 3, 4)
+        self.far = lax.rem(tx + 2, 4)
+        self.send_sems = send_sems
+        self.recv_sems = recv_sems
+
+    def copy(self, src, dst, slot, to):
+        return pltpu.make_async_remote_copy(
+            src_ref=src,
+            dst_ref=dst,
+            send_sem=self.send_sems.at[slot],
+            recv_sem=self.recv_sems.at[slot],
+            device_id=(self.dp, to),
+            device_id_type=MESH,
+        )
+
+
+class Gather:
+    def __init__(self, ring, buf, block):
+        h = block // 2
+        r = ring
+
+        def part(t, half):
+            return buf.at[pl.ds(pl.multiple_of(t * block + half * h, h), h)]
+
+        self.first = [
+            r.copy(part(r.tx, 0), part(r.tx, 0), 0, r.right),
+            r.copy(part(r.tx, 1), part(r.tx, 1), 1, r.left),
+            r.copy(part(r.tx, 1), part(r.tx, 1), 2, r.right),
+            r.copy(part(r.tx, 0), part(r.tx, 0), 3, r.left),
+        ]
+        self.second = [
+            r.copy(part(r.left, 0), part(r.left, 0), 4, r.right),
+            r.copy(part(r.right, 1), part(r.right, 1), 5, r.left),
+        ]
+
+    def start(self):
+        for c in self.first:
+            c.start()
+
+    def forward(self):
+        for c, d in zip(self.first[:2], self.second):
+            c.wait_recv()
+            d.start()
+
+    def finish(self):
+        for c in self.first[2:] + self.second:
+            c.wait_recv()
+        for c in self.first + self.second:
+            c.wait_send()
+
+
+class Scatter:
+    def __init__(self, ring, part, land, onward, block):
+        h = block // 2
+        r = ring
+        self.h = h
+        self.ring = r
+        self.part = part
+        self.land = land
+        self.onward = onward
+        self.block = block
+
+        self.first = [
+            r.copy(self.at(r.far, 0), self.slot(0), 0, r.right),
+            r.copy(self.at(r.far, 1), self.slot(1), 1, r.left),
+            r.copy(self.at(r.right, 1), self.slot(2), 2, r.right),
+            r.copy(self.at(r.left, 0), self.slot(3), 3, r.left),
+        ]
+        self.second = [
+            r.copy(onward.at[pl.ds(0, h)], self.slot(4), 4, r.right),
+            r.copy(onward.at[pl.ds(h, h)], self.slot(5), 5, r.left),
+        ]
+
+    def at(self, t, half):
+        return self.part.at[self.span(t, half)]
+
+    def span(self, t, half):
+        return pl.ds(pl.multiple_of(t * self.block + half * self.h, self.h), self.h)
+
+    def slot(self, i):
+        return self.land.at[pl.ds(i * self.h, self.h)]
+
+    def start(self):
+        for c in self.first:
+            c.start()
+
+    def forward(self):
+        h = self.h
+        for i, t in enumerate((self.ring.right, self.ring.left)):
+            self.first[i].wait_recv()
+            self.onward[i * h : (i + 1) * h] = (
+                self.land[i * h : (i + 1) * h].astype(F32) + self.part[self.span(t, i)].astype(F32)
+            ).astype(BF)
+            self.second[i].start()
+
+    def finish(self):
+        h = self.h
+        for c in self.first[2:] + self.second:
+            c.wait_recv()
+        for c in self.first + self.second:
+            c.wait_send()
+
+        def got(i):
+            return self.land[i * h : (i + 1) * h].astype(F32)
+
+        return got(3) + got(4), got(2) + got(5)
+
+
+def slots_of(ids):
+    n = ids.shape[1]
+    holder = lax.shift_right_logical(ids, 12)
+    hits = iota((OWNERS, n), 0) == holder
+    earlier = one_zero(iota((n, n), 0) < iota((n, n), 1))
+    hits_b = one_zero(hits)
+    before = jnp.sum(jnp.where(hits, mm(hits_b, earlier), 0.0), axis=0, keepdims=True)
+    return holder, hits_b, before.astype(jnp.int32)
+
+
+def wanted_rows(ids, hits_b, before, offset):
+    n = ids.shape[1]
+    marked = (ids & (ROWS - 1)) + 1
+    chosen = iota((OWNERS, n), 0) == before + offset
+    high = jnp.where(chosen, lax.shift_right_logical(marked, 6).astype(F32), 0.0).astype(BF)
+    low = jnp.where(chosen, (marked & 63).astype(F32), 0.0).astype(BF)
+    return 64.0 * mm_nt(hits_b, high) + mm_nt(hits_b, low)
+
+
+def as_column(row):
+    n = row.shape[1]
+    wide = jnp.broadcast_to(row.astype(F32), (128, n))
+    return jnp.transpose(wide)[:, 0:1].astype(jnp.int32)
+
+
+def neg_row(negs_ref):
+    return jnp.concatenate([negs_ref[u : u + 1, :] for u in range(4)], axis=1)
+
+
+def part_mask(rows, width, per, parts):
+    which = lax.rem(iota((rows, width), 0), 16) // per
+    return [one_zero(which == c) for c in range(parts)]
+
+
+def pick_parts(values, per, width):
+    which = lax.div(lax.rem(iota((values.shape[0], width), 0), 16), per)
+    out = values[:, 0:width]
+    for c in range(1, values.shape[1] // width):
+        out = jnp.where(which == c, values[:, c * width : (c + 1) * width], out)
+    return out
+
+
+def gather_rows(table, ids_col, out_ref, at):
+    step = 512
+
+    def one(i, total):
+        base = pl.multiple_of(i * step, step)
+        pick = one_zero(ids_col == iota((512, step), 1) + i * step)
+        return total + mm(pick, table[pl.ds(base, step), :])
+
+    total = lax.fori_loop(0, ROWS // step, one, jnp.zeros((512, D), F32))
+    out_ref[at : at + 512, :] = total.astype(BF)
+
+
+def spread_chunks(rows_ref, chunks_ref, at, cap):
+    width = cap * 32
+    block = 128 // cap
+    many = block * 16
+    r, q = iota((many, 128), 0), iota((many, 128), 1)
+    fold = one_zero(
+        (lax.rem(q, block) == lax.div(r, 16)) & (lax.div(q, block) == lax.rem(r, cap))
+    )
+    for b in range(cap):
+        rows = jnp.concatenate(
+            [
+                rows_ref[at + k * 128 + b * block : at + k * 128 + (b + 1) * block, :]
+                for k in range(cap)
+            ],
+            axis=0,
+        )
+        chunks_ref[b * many : (b + 1) * many, :] = pick_parts(mm(fold, rows), cap, width).astype(BF)
+
+
+def unfold(chunks, per, parts):
+    rows, width = chunks.shape
+    masks = part_mask(rows, width, per, parts)
+    return jnp.concatenate([chunks * m for m in masks], axis=1)
+
+
+def take_slots(chunks_ref, slot_col, cap):
+    n = slot_col.shape[0]
+    total = jnp.zeros((n, D), F32)
+    step = 512
+    for i in range(OWNERS * 16 // step):
+        r = iota((n, step), 1) + i * step
+        key = lax.div(r, 16) * cap + lax.rem(r, cap)
+        total = total + mm(
+            one_zero(slot_col == key),
+            unfold(chunks_ref[i * step : (i + 1) * step, :], cap, 16 // cap),
+        )
+    return total.astype(BF)
+
+
+def put_slots(rows, slot_row, chunks_ref, cap):
+    n = slot_row.shape[1]
+    step = 512
+    for i in range(OWNERS * 16 // step):
+        r = iota((step, n), 0) + i * step
+        key = lax.div(r, 16) * cap + lax.rem(r, cap)
+        chunks_ref[i * step : (i + 1) * step, :] = pick_parts(
+            mm(one_zero(slot_row == key), rows), cap, cap * 32
+        ).astype(BF)
+
+
+def fetch_kernel(
+    ids_ref,
+    negs_ref,
+    table_hbm,
+    emb_ref,
+    neg_ref,
+    arrived_ref,
+    table_ref,
+    request_ref,
+    picked_ref,
+    hist_out,
+    neg_out,
+    hist_in,
+    neg_in,
+    table_sem,
+    all_send,
+    all_recv,
+    hist_ss,
+    hist_rs,
+    neg_ss,
+    neg_rs,
+):
+    dp, tx = position()
+    barrier = pltpu.get_barrier_semaphore()
+    greet_all(barrier, dp, tx)
+    load = pltpu.make_async_copy(table_hbm, table_ref, table_sem)
+    load.start()
+
+    ids, negs = ids_ref[...], neg_row(negs_ref)
+    holder_h, hits_h, before_h = slots_of(ids)
+    holder_n, hits_n, before_n = slots_of(negs)
+    wanted = wanted_rows(ids, hits_h, before_h, 0) + wanted_rows(negs, hits_n, before_n, CAP_H)
+    request_ref[:, 0, :] = wanted.astype(jnp.int32) - 1
+    slot_h = as_column(holder_h * CAP_H + before_h)
+    slot_n = as_column(holder_n * CAP_N + before_n)
+
+    pl.semaphore_wait(barrier, OWNERS - 1)
+    spread_all(request_ref, arrived_ref, 1, all_send.at[0], all_recv.at[0], dp, tx)
+    load.wait()
+    wait_rows(arrived_ref, OWNERS - 1, all_recv.at[0])
+
+    arrived = arrived_ref[:, 0, :]
+    columns = [arrived[:, k : k + 1] for k in range(CAP_H + CAP_N)]
+    gather_rows(table_ref, jnp.concatenate(columns[0:4], axis=0), picked_ref, 0)
+    spread_chunks(picked_ref, hist_out, 0, CAP_H)
+    spread_all(hist_out, hist_in, 16, all_send.at[1], all_recv.at[1], dp, tx)
+    gather_rows(table_ref, jnp.concatenate(columns[4:8], axis=0), picked_ref, 512)
+    gather_rows(table_ref, jnp.concatenate(columns[8:12], axis=0), picked_ref, 1024)
+    spread_chunks(picked_ref, neg_out, 512, CAP_N)
+    spread_all(neg_out, neg_in, 16, all_send.at[2], all_recv.at[2], dp, tx)
+
+    wait_rows(hist_in, (OWNERS - 1) * 16, all_recv.at[1])
+    emb_ref[pl.ds(pl.multiple_of(tx * 256, 256), 256), :] = take_slots(hist_in, slot_h, CAP_H)
+    hist = Gather(Ring(dp, tx, hist_ss, hist_rs), emb_ref, 256)
+    hist.start()
+    hist.forward()
+    wait_rows(neg_in, (OWNERS - 1) * 16, all_recv.at[2])
+    neg_ref[pl.ds(pl.multiple_of(tx * 512, 512), 512), :] = take_slots(neg_in, slot_n, CAP_N)
+    negs_all = Gather(Ring(dp, tx, neg_ss, neg_rs), neg_ref, 512)
+    negs_all.start()
+    negs_all.forward()
+    hist.finish()
+    negs_all.finish()
+    wait_rows(request_ref, OWNERS - 1, all_send.at[0])
+    wait_rows(hist_out, (OWNERS - 1) * 16, all_send.at[1])
+    wait_rows(neg_out, (OWNERS - 1) * 16, all_send.at[2])
+
+
+VM = pl.BlockSpec(memory_space=pltpu.VMEM)
+HB = pl.BlockSpec(memory_space=pl.ANY)
+
+
+def fetch(ids, negs, table):
+    sem = pltpu.SemaphoreType.DMA
+    return pl.pallas_call(
+        fetch_kernel,
+        out_shape=[
+            jax.ShapeDtypeStruct((1024, D), BF),
+            jax.ShapeDtypeStruct((2048, D), BF),
+            jax.ShapeDtypeStruct((OWNERS, 1, 128), jnp.int32),
+        ],
+        in_specs=[VM, VM, HB],
+        out_specs=[VM, VM, VM],
+        scratch_shapes=[
+            pltpu.VMEM((ROWS, D), BF),
+            pltpu.VMEM((OWNERS, 1, 128), jnp.int32),
+            pltpu.VMEM((12 * OWNERS, D), BF),
+            pltpu.VMEM((OWNERS * 16, 128), BF),
+            pltpu.VMEM((OWNERS * 16, 256), BF),
+            pltpu.VMEM((OWNERS * 16, 128), BF),
+            pltpu.VMEM((OWNERS * 16, 256), BF),
+            sem,
+            sem((3,)),
+            sem((3,)),
+            sem((6,)),
+            sem((6,)),
+            sem((6,)),
+            sem((6,)),
+        ],
+        compiler_params=pltpu.CompilerParams(
+            collective_id=0, has_side_effects=True, vmem_limit_bytes=48 * 1024 * 1024
+        ),
+        name="fetch_rows",
+    )(ids, negs, table)
+
+
+def greet_dp(dp, tx, step):
+    pd, _ = partner(dp, tx, step * 4)
+    return pd
+
+
+def return_kernel(
+    ids_ref,
+    negs_ref,
+    emb_part,
+    neg_part,
+    weight_ref,
+    hist_in,
+    neg_in,
+    weight_sum,
+    hist_out,
+    neg_out,
+    emb_land,
+    emb_on,
+    neg_land,
+    neg_on,
+    weight_in,
+    weight_mine,
+    all_send,
+    all_recv,
+    emb_ss,
+    emb_rs,
+    neg_ss,
+    neg_rs,
+):
+    dp, tx = position()
+    barrier = pltpu.get_barrier_semaphore()
+    greet_all(barrier, dp, tx)
+    ids, negs = ids_ref[...], neg_row(negs_ref)
+    holder_h, _, before_h = slots_of(ids)
+    holder_n, _, before_n = slots_of(negs)
+    slot_h = holder_h * CAP_H + before_h
+    slot_n = holder_n * CAP_N + before_n
+    pl.semaphore_wait(barrier, OWNERS - 1)
+
+    neg_sum = Scatter(Ring(dp, tx, neg_ss, neg_rs), neg_part, neg_land, neg_on, 512)
+    emb_sum = Scatter(Ring(dp, tx, emb_ss, emb_rs), emb_part, emb_land, emb_on, 256)
+    emb_sum.start()
+    neg_sum.start()
+
+    piece = 80
+
+    def out_piece(i, carry):
+        pd = greet_dp(dp, tx, i)
+        pltpu.make_async_remote_copy(
+            src_ref=weight_ref.at[pl.ds(pl.multiple_of(pd * piece, 16), piece)],
+            dst_ref=weight_in.at[pl.ds(pl.multiple_of(dp * piece, 16), piece)],
+            send_sem=all_send.at[2],
+            recv_sem=all_recv.at[2],
+            device_id=(pd, tx),
+            device_id_type=MESH,
+        ).start()
+        return carry
+
+    emb_sum.forward()
+    neg_sum.forward()
+    lax.fori_loop(1, N_DP, out_piece, 0)
+    own = pl.ds(pl.multiple_of(dp * piece, 16), piece)
+    weight_in[own] = weight_ref[own]
+
+    def block_sum(total, part_ref, block):
+        first, second = total.finish()
+        mine = part_ref[pl.ds(pl.multiple_of(tx * block, block), block), :].astype(F32)
+        return (mine + jnp.concatenate([first, second], axis=0)).astype(BF)
+
+    d_hist = block_sum(emb_sum, emb_part, 256)
+    put_slots(d_hist, slot_h, hist_out, CAP_H)
+    spread_all(hist_out, hist_in, 16, all_send.at[0], all_recv.at[0], dp, tx)
+    d_neg = block_sum(neg_sum, neg_part, 512)
+    put_slots(d_neg, slot_n, neg_out, CAP_N)
+    spread_all(neg_out, neg_in, 16, all_send.at[1], all_recv.at[1], dp, tx)
+
+    wait_rows(weight_in, (N_DP - 1) * piece, all_recv.at[2])
+    total = weight_in[0:piece, :].astype(F32)
+    for i in range(1, N_DP):
+        total = total + weight_in[i * piece : (i + 1) * piece, :].astype(F32)
+    weight_mine[...] = total.astype(BF)
+    weight_sum[own] = total.astype(BF)
+
+    def back_piece(i, carry):
+        pd = greet_dp(dp, tx, i)
+        pltpu.make_async_remote_copy(
+            src_ref=weight_mine,
+            dst_ref=weight_sum.at[pl.ds(pl.multiple_of(dp * piece, 16), piece)],
+            send_sem=all_send.at[3],
+            recv_sem=all_recv.at[3],
+            device_id=(pd, tx),
+            device_id_type=MESH,
+        ).start()
+        return carry
+
+    lax.fori_loop(1, N_DP, back_piece, 0)
+    wait_rows(hist_in, (OWNERS - 1) * 16, all_recv.at[0])
+    wait_rows(neg_in, (OWNERS - 1) * 16, all_recv.at[1])
+    wait_rows(weight_sum, (N_DP - 1) * piece, all_recv.at[3])
+    wait_rows(hist_out, (OWNERS - 1) * 16, all_send.at[0])
+    wait_rows(neg_out, (OWNERS - 1) * 16, all_send.at[1])
+    wait_rows(weight_in, (N_DP - 1) * piece, all_send.at[2])
+    wait_rows(weight_in, (N_DP - 1) * piece, all_send.at[3])
+
+
+def give_back(ids, negs, emb_part, neg_part, weight):
+    sem = pltpu.SemaphoreType.DMA
+    return pl.pallas_call(
+        return_kernel,
+        out_shape=[
+            jax.ShapeDtypeStruct((OWNERS * 16, 128), BF),
+            jax.ShapeDtypeStruct((OWNERS * 16, 256), BF),
+            jax.ShapeDtypeStruct((2560, 128), BF),
+        ],
+        in_specs=[VM] * 5,
+        out_specs=[VM] * 3,
+        scratch_shapes=[
+            pltpu.VMEM((OWNERS * 16, 128), BF),
+            pltpu.VMEM((OWNERS * 16, 256), BF),
+            pltpu.VMEM((6 * 128, D), BF),
+            pltpu.VMEM((2 * 128, D), BF),
+            pltpu.VMEM((6 * 256, D), BF),
+            pltpu.VMEM((2 * 256, D), BF),
+            pltpu.VMEM((2560, 128), BF),
+            pltpu.VMEM((80, 128), BF),
+            sem((4,)),
+            sem((4,)),
+            sem((6,)),
+            sem((6,)),
+            sem((6,)),
+            sem((6,)),
+        ],
+        compiler_params=pltpu.CompilerParams(
+            collective_id=1, has_side_effects=True, vmem_limit_bytes=48 * 1024 * 1024
+        ),
+        name="return_rows",
+    )(ids, negs, emb_part, neg_part, weight)
+
+
+def gather_chunks(chunks_ref, rows_ref, at, cap):
+    block = 128 // cap
+    many = block * 16
+    q, r = iota((128, many), 0), iota((128, many), 1)
+    fold = one_zero(
+        (lax.rem(q, block) == lax.div(r, 16)) & (lax.div(q, block) == lax.rem(r, cap))
+    )
+    for b in range(cap):
+        wide = unfold(chunks_ref[b * many : (b + 1) * many, :], cap, 16 // cap)
+        rows = mm(fold, wide).astype(BF)
+        for k in range(cap):
+            rows_ref[at + k * 128 + b * block : at + k * 128 + (b + 1) * block, :] = rows[
+                k * block : (k + 1) * block
+            ]
+
+
+def add_kernel(arrived_ref, hist_ref, neg_ref, out_ref, rows_ref, ids_ref):
+    tile = out_ref.shape[0]
+    step = pl.program_id(0)
+
+    @pl.when(step == 0)
+    def _():
+        gather_chunks(hist_ref, rows_ref, 0, CAP_H)
+        gather_chunks(neg_ref, rows_ref, 512, CAP_N)
+        ids_ref[...] = jnp.transpose(arrived_ref[:, 0, :].astype(F32)).astype(jnp.int32)
+
+    total = jnp.zeros((tile, D), F32)
+    for k in range(0, CAP_H + CAP_N, 4):
+        row = jnp.concatenate([ids_ref[k + j : k + j + 1, :] for j in range(4)], axis=1)
+        put = one_zero(row == iota((tile, 512), 0) + step * tile)
+        total = total + mm(put, rows_ref[k * 128 : (k + 4) * 128, :])
+    out_ref[...] = total
+
+
+def add_rows(arrived, hist_in, neg_in):
+    tile = 512
+    return pl.pallas_call(
+        add_kernel,
+        out_shape=jax.ShapeDtypeStruct((ROWS, D), F32),
+        grid=(ROWS // tile,),
+        in_specs=[VM] * 3,
+        out_specs=pl.BlockSpec((tile, D), lambda i: (i, 0)),
+        scratch_shapes=[
+            pltpu.VMEM((12 * OWNERS, D), BF),
+            pltpu.VMEM((128, 128), jnp.int32),
+        ],
+        compiler_params=pltpu.CompilerParams(vmem_limit_bytes=32 * 1024 * 1024),
+        name="add_rows",
+    )(arrived, hist_in, neg_in)
 
 
 def layer_norm(values):
@@ -79,48 +675,13 @@
     return jnp.sum(jnp.where(valid, jnp.log(total) - positive, 0.0))
 
 
-def place_slots(wanted, rows_held, owners, slot_width, offset):
-    holder = wanted // rows_held
-    hits = (holder[:, None] == jnp.arange(owners, dtype=jnp.int32)[None, :]).astype(jnp.int32)
-    before = jnp.sum((jnp.cumsum(hits, axis=0) - hits) * hits, axis=1)
-    return holder * slot_width + offset + before
-
-
 def on_device(table, item_ids, negatives, lengths, w_in, w_out):
-    rows_held = table.shape[0]
-    width = table.shape[1]
-    dp_count = lax.axis_size("dp")
-    table_count = lax.axis_size("table")
-    owners = dp_count * table_count
     neg_ids = negatives.reshape(-1)
     hist_count = item_ids.shape[0]
     neg_count = neg_ids.shape[0]
-    cap_hist = 2 * hist_count // owners
-    cap_neg = 2 * neg_count // owners
-    slot_width = cap_hist + cap_neg
-    slot_hist = place_slots(item_ids, rows_held, owners, slot_width, 0)
-    slot_neg = place_slots(neg_ids, rows_held, owners, slot_width, cap_hist)
-    request = jnp.full((owners * slot_width,), -1, jnp.int32)
-    request = request.at[slot_hist].set(item_ids % rows_held).at[slot_neg].set(neg_ids % rows_held)
-    arrived = lax.all_to_all(
-        request.reshape(owners, slot_width),
-        ("dp", "table"),
-        split_axis=0,
-        concat_axis=0,
-        tiled=True,
-    )
-    filled = (arrived >= 0).astype(jnp.bfloat16)
-    picked = jnp.take(table, jnp.clip(arrived, 0, rows_held - 1), axis=0)
-    fetched = lax.all_to_all(
-        picked * filled[..., None], ("dp", "table"), split_axis=0, concat_axis=0, tiled=True
-    )
-    fetched = fetched.reshape(owners * slot_width, width)
-    hist_rows = jnp.take(fetched, slot_hist, axis=0)
-    neg_rows = jnp.take(fetched, slot_neg, axis=0)
-    emb_all, neg_all = (
-        lax.all_gather(hist_rows, "table", axis=0, tiled=True),
-        lax.all_gather(neg_rows, "table", axis=0, tiled=True),
-    )
+    table_count = lax.axis_size("table")
+    ids_row = item_ids.reshape(1, hist_count)
+    emb_all, neg_all, arrived = fetch(ids_row, negatives, table)
     count = emb_all.shape[0]
     segment, row_len = segments(lengths[0], count)
     my_index = lax.axis_index("table")
@@ -152,34 +713,21 @@
     d_emb_heads, d_win, d_wout = heads_pullback(d_out)
     residual = lax.dynamic_update_slice_in_dim(jnp.zeros_like(emb_f), d_rows, row_start, 0)
     d_emb = d_emb_heads + d_emb_loss + residual
-    grad_w_in, grad_w_out = (
-        lax.psum(d_win.astype(jnp.bfloat16), "dp").astype(jnp.float32),
-        lax.psum(d_wout.astype(jnp.bfloat16), "dp").astype(jnp.float32),
-    )
-    d_hist, d_negs = (
-        lax.psum_scatter(
-            d_emb.astype(jnp.bfloat16), "table", scatter_dimension=0, tiled=True
-        ).astype(jnp.float32),
-        lax.psum_scatter(
-            d_neg.astype(jnp.bfloat16), "table", scatter_dimension=0, tiled=True
-        ).astype(jnp.float32),
-    )
-    outgoing = jnp.zeros((owners * slot_width, width), jnp.float32)
-    outgoing = outgoing.at[slot_hist].set(d_hist).at[slot_neg].set(d_negs)
-    landed = lax.all_to_all(
-        outgoing.reshape(owners, slot_width, width).astype(jnp.bfloat16),
-        ("dp", "table"),
-        split_axis=0,
-        concat_axis=0,
-        tiled=True,
-    ).astype(jnp.float32)
-    served_flat = arrived.reshape(-1)
-    target = jnp.where(served_flat >= 0, served_flat, rows_held)
-    grad_table = (
-        jnp.zeros((rows_held, width), jnp.float32)
-        .at[target]
-        .add(landed.reshape(-1, width), mode="drop")
-    )
+    weight = jnp.concatenate(
+        [
+            d_win.astype(BF).reshape(2048, 128),
+            d_wout.astype(BF).reshape(128, 4, 128).transpose(1, 0, 2).reshape(512, 128),
+        ],
+        axis=0,
+    )
+    hist_in, neg_in, weight_sum = give_back(
+        ids_row, negatives, d_emb.astype(BF), d_neg.astype(BF), weight
+    )
+    grad_w_in = weight_sum[:2048].reshape(4, 512, 128).astype(F32)
+    grad_w_out = (
+        weight_sum[2048:].reshape(4, 128, 128).transpose(1, 0, 2).reshape(128, 512).astype(F32)
+    )
+    grad_table = add_rows(arrived, hist_in, neg_in)
     return (grad_table, grad_w_in, grad_w_out)
 
 

time: 441 us -> 260 us (0.59); the launches traced: 434 us -> 260 us
  waiting for transfers between devices: 265 us -> 31.4 us
  Pallas kernels: 0 us -> 153 us
  other arithmetic: 52.1 us -> 20.9 us
  local copies, waits for them, and re-layouts: 41.8 us -> 14 us
  blocking collectives: 21 us -> 0 us
  starting transfers between devices: 13.8 us -> 0.26 us
    pallas_call x0 -> x3, Pallas kernels: none -> 153 us  [the longest x1 78.8 us: fetch(): pl.pallas_call(fetch_kernel, out_shape=[jax.ShapeDtypeStruct((1024, D), B...]
    psum x1 -> x0, waiting for transfers between devices: 109 us -> none  [on_device(): lax.psum(d_win.astype(jnp.bfloat16), 'dp').astype(jnp.float32)]
    reduce_scatter x2 -> x0, waiting for transfers between devices: 48.9 us -> none  [the longest x1 31 us: on_device(): lax.psum_scatter(d_neg.astype(jnp.bfloat16), 'table', scatter_dimension=0...]
    all_gather x2 -> x0, waiting for transfers between devices: 34.5 us -> none  [the longest x1 20 us: on_device(): lax.all_gather(neg_rows, 'table', axis=0, tiled=True)]
    all_to_all x2 -> x0, waiting for transfers between devices: 30.5 us -> none  [the longest x1 30.5 us: on_device(): lax.all_to_all(picked * filled[..., None], ('dp', 'table'), split_axis=0,...]
    all_to_all x1 -> x0, blocking collectives: 21 us -> none  [on_device(): lax.all_to_all(request.reshape(owners, slot_width), ('dp', 'table'), spli...]
    scatter-add x1 -> x0, other arithmetic: 14.1 us -> none  [on_device(): grad_table = jnp.zeros((rows_held, width), jnp.float32).at[target].add(la...]
    all_to_all x2 -> x0, starting transfers between devices: 13.1 us -> none  [the longest x1 7.96 us: on_device(): lax.all_to_all(outgoing.reshape(owners, slot_width, width).astype(jnp.bfl...]
  transfers between devices with their start and end apart: 9 -> 2, of which waited for: 8 -> 2; matrix products, arithmetic and copies ran while one was open for 9% -> 5% of each run, Pallas kernels for 0% -> 0%
where the time goes in v1:
time: 260 us
  Pallas kernels  153 us (59%)
  waiting for transfers between devices  31.4 us (12%)
  matrix products  25.6 us (10%)
  other arithmetic  20.9 us (8%)
  between operations  14.5 us (6%)
  local copies, waits for them, and re-layouts  14 us (5%)
    pallas_call x1, Pallas kernels, fetch(): pl.pallas_call(fetch_kernel, out_shape=[jax.ShapeDtypeStruct((1024, D), B...  78.8 us
    pallas_call x1, Pallas kernels, give_back(): pl.pallas_call(return_kernel, out_shape=[jax.ShapeDtypeStruct((OWNERS * 1...  64.4 us
    reduce_scatter x1, waiting for transfers between devices, on_device(): lax.psum_scatter(partial_out.astype(jnp.bfloat16), 'table', scatter_dimen...  17.7 us
    all_gather x1, waiting for transfers between devices, on_device(): lax.all_gather(d_rows.astype(jnp.bfloat16), 'table', axis=0, tiled=True)  13.7 us
    pallas_call x1, Pallas kernels, add_rows(): pl.pallas_call(add_kernel, out_shape=jax.ShapeDtypeStruct((ROWS, D), F32)...  9.86 us
    unnamed x57, local copies, waits for them, and re-layouts  7.62 us
    dot_general x3, matrix products, branch(): jnp.einsum('hqk,khd->qhd', weights, value, preferred_element_type=jnp.flo...  6.15 us
    dot_general x3, matrix products, branch(): jnp.einsum('qhd,khd->hqk', query, keys, preferred_element_type=jnp.float32)  6.1 us
  transfers between devices with their start and end apart: 2, of which 2 were waited for; matrix products, arithmetic and copies ran while one was open for 5% of the time, Pallas kernels for 0%

profile of v1, /device:TPU:1, one launch (start us, length us, event | category | flops | bytes accessed | tf_op | source)
XLA Modules:
  0.0 259.8 jit_solution(5246858451563814403)
XLA Ops:
  7.2 0.0 reduce-scatter.2.cloned.1.call-start
  7.2 0.7 copy-done.2
  7.9 0.7 copy-done.4
  8.6 78.8 %fetch_rows.1 = (bf16[1024,512]{1,0:T(8,128)(2,1)S(1)}, bf16[2048,512]{1,0:T(8,128)(2,1)S(1)}, s32[128,1,128]{2,1,0:T(1,128)S(1)}) custom-call(s32[1,256]{1,0:T(1,128)S(1)} %bitcast.162, s32[4,128]{1,0:T(4,128)S(1)} %copy-done.2, bf16[4096,512]{1,0:T(8,128)(2,1)} %table_hbm.1), custom_call_target="tpu_custom_call" | custom-call | tf_op jit(solution)/shard_map/fetch_rows/pallas_call | solution.py:387
  87.5 0.4 fusion.22
  87.9 2.0 copy.17
  89.9 1.6 fusion.23
  91.6 0.2 reduce-window.8
  91.8 0.1 convert_reduce_fusion.1
  91.9 1.9 fusion.91
  93.8 0.6 multiply_convert_fusion
  94.4 0.1 select_reduce_fusion
  94.5 3.7 %select_convert_fusion = (bf16[1024,1024]{1,0:T(8,128)(2,1)S(1)}, f32[1024,1024]{1,0:T(8,128)}) fusion(f32[1024]{0:T(1024)S(1)} %select_reduce_fusion, s32[1024]{0:T(1024)S(1)} %convert_reduce_fusion.1, bf16[4,1024,128]{1,2,0:T(8,128)(2,1)S(1)} %multiply_convert_fusion), kind=kOutput, calls=%fused_computation.14 | convolution fusion | flops 279969792 | bytes 6828032 | tf_op jit(solution)/shard_map/jvp(qhd,khd->hqk)/dot_general | solution.py:638
  98.2 0.8 fusion.95
  99.1 0.1 fusion.68
  99.2 0.7 copy-done.6
  99.8 0.1 fusion.72
  100.0 0.7 copy-done.20
  100.6 1.5 convolution_convert_fusion.1
  102.1 0.0 reduce-scatter.2.cloned.1.call-update
  102.1 0.2 all-gather.2.cloned.1.call-start
  102.4 1.6 convert_element_type.181
  104.0 0.1 dynamic_slice.12
  104.0 0.5 fusion.4
  104.5 17.7 %reduce-scatter.2.cloned.1.call-done = bf16[256,512]{1,0:T(8,128)(2,1)} async-done(((bf16[1024,512]{1,0:T(8,128)(2,1)}), bf16[256,512]{1,0:T(8,128)(2,1)}) %reduce-scatter.2.cloned.1.call-update) | async-done | bytes 262160 | tf_op jit(solution)/shard_map/reduce_scatter | solution.py:700
  122.2 1.3 multiply_reduce_fusion.1
  123.5 1.5 fusion.59
  125.0 1.3 fusion.16
  126.2 0.1 add_multiply_fusion
  126.3 0.3 copy-done.9
  126.6 0.3 copy-done.19
  127.0 1.0 multiply_reduce_fusion
  128.0 0.8 copy-done.22
  128.8 0.9 fusion.93
  129.7 1.8 fusion.58
  131.5 1.1 broadcast_in_dim.116
  132.6 2.8 %dynamic_update_slice.6 = bf16[1025,512]{1,0:T(8,128)(2,1)} dynamic-update-slice(bf16[1025,512]{1,0:T(8,128)(2,1)} %broadcast_in_dim.116, bf16[256,512]{1,0:T(8,128)(2,1)} %fusion.58, s32[]{:T(128)S(6)} %select_n.58, s32[]{:T(128)} %constant.38.clone.1) | dynamic-update-slice | bytes 524292 | tf_op jit(solution)/shard_map/transpose(jvp())/dynamic_update_slice | solution.py:661
  135.4 2.6 %fusion.6 = (f32[2048]{0:T(1024)S(1)}, bf16[2048,512]{1,0:T(8,128)(2,1)S(1)}) fusion(bf16[2048,512]{1,0:T(8,128)(2,1)S(1)} %get-tuple-element.11, bf16[256,512]{1,0:T(8,128)(2,1)} %copy-done.24, f32[256,2048]{1,0:T(8,128)} %copy-done.27, f32[256]{0:T(256)S(1)} %get-tuple-element.22, s32[2048]{0:T(1024)S(1)} %add_select_fusion, s32[256]{0:T(256)S(1)} %dynamic_slice.12), kind=kOutput, calls=%fused_computation.13 | convolution fusion | flops 544208896 | bytes 6572032 | tf_op jit(solution)/shard_map/transpose(jvp())/dot_general | solution.py:670
  138.1 2.0 fusion.3.neg_part
  140.1 13.7 %all-gather.2.cloned.1.call-done = bf16[1024,512]{1,0:T(8,128)(2,1)} async-done(((bf16[256,512]{1,0:T(8,128)(2,1)}), bf16[1024,512]{1,0:T(8,128)(2,1)}) %all-gather.2.cloned.1.call-update) | async-done | bytes 1048592 | tf_op jit(solution)/shard_map/all_gather | solution.py:710
  153.9 2.1 fusion.67
  156.0 0.2 fusion.94
  156.2 0.5 fusion.37
  156.7 4.9 %fusion.2 = bf16[1024,1024]{1,0:T(8,128)(2,1)S(1)} fusion(f32[1024,1024]{1,0:T(8,128)} %get-tuple-element.29, f32[1024]{0:T(1024)S(1)} %select_reduce_fusion, s32[1024]{0:T(1024)S(1)} %convert_reduce_fusion.1, f32[1024,1,128]{0,2,1:T(8,128)S(1)} %get-tuple-element.20, f32[1024]{0:T(1024)S(1)} %negate_multiply_fusion.1, bf16[4,1024,128]{1,2,0:T(8,128)(2,1)S(1)} %copy-done.15), kind=kOutput, calls=%fused_computation.9 | convolution fusion | flops 288489472 | bytes 7094272 | tf_op jit(solution)/shard_map/transpose(jvp(hqk,khd->qhd))/dot_general | solution.py:646
  161.5 0.8 fusion.36
  162.4 1.5 fusion.35
  163.9 0.1 copy-done.11
  164.0 0.9 fusion.14
  165.0 0.1 copy-done.25
  165.1 1.1 fusion.21
  166.1 1.6 fusion.30
  167.8 1.3 fusion.29
  169.2 1.4 fusion.25
  170.6 1.3 add_dynamic-update-slice_fusion
  171.9 0.1 convert_element_type.220.emb_part
  172.1 1.1 copy-done.18
  173.1 0.0 copy-done.21
  173.2 0.3 fusion.44
  173.5 2.2 copy.22
  175.7 1.1 pad_maximum_fusion.weight_ref
  176.9 64.4 %return_rows.1 = (bf16[2048,128]{1,0:T(8,128)(2,1)S(1)}, bf16[2048,256]{1,0:T(8,128)(2,1)S(1)}, bf16[2560,128]{1,0:T(8,128)(2,1)S(1)}) custom-call(s32[1,256]{1,0:T(1,128)S(1)} %bitcast.163, s32[4,128]{1,0:T(4,128)S(1)} %copy-done.3, bf16[1024,512]{1,0:T(8,128)(2,1)S(1)} %convert_element_type.220.emb_part, bf16[2048,512]{1,0:T(8,128)(2,1)S(1)} %copy-done.1, ...), custom_call_target="tpu_custom_call" | custom-call | tf_op jit(solution)/shard_map/return_rows/pallas_call | solution.py:526
  241.3 1.0 convert.8
  242.4 0.7 copy_bitcast_fusion
  243.1 9.9 %add_rows.1 = f32[4096,512]{1,0:T(8,128)} custom-call(s32[128,1,128]{2,1,0:T(1,128)S(1)} %get-tuple-element.9.arrived_ref, bf16[2048,128]{1,0:T(8,128)(2,1)S(1)} %get-tuple-element.12.hist_ref, bf16[2048,256]{1,0:T(8,128)(2,1)S(1)} %get-tuple-element.13.neg_ref), custom_call_target="tpu_custom_call" | custom-call | tf_op jit(solution)/shard_map/add_rows/pallas_call | solution.py:594
  (64 shorter events, 0.3 us)
Async XLA Ops:
  7.2 93.5 %copy-start = (bf16[128,512]{1,0:T(8,128)(2,1)S(1)}, bf16[128,512]{1,0:T(8,128)(2,1)}, u32[]{:S(2)}) copy-start(bf16[128,512]{1,0:T(8,128)(2,1)} %param.11) | copy-start | bytes 393220
  7.2 115.0 %reduce-scatter.2.cloned.1.call-start = ((), (), s32[]{:S(2)}) async-start(), calls=%async_computation.1 | async-start | bytes 1310720 | tf_op jit(solution)/shard_map/reduce_scatter | solution.py:700
  7.2 0.7 copy-start.2
  7.9 0.7 copy-start.4
  87.5 4.1 %copy-start.26 = (s32[1,4]{1,0:T(1,128)S(1)}, s32[1,4]{1,0:T(1,128)}, u32[]{:S(2)}) copy-start(s32[1,4]{1,0:T(1,128)} %param.9) | copy-start | bytes 52
  93.8 4.4 %copy-start.10 = (f32[1024,512]{0,1}, f32[1024,512]{0,1:S(1)}, u32[]{:S(2)}) copy-start(f32[1024,512]{0,1:S(1)} %fusion.91) | copy-start | bytes 6291460
  94.4 4.8 %copy-start.14 = (bf16[4,1024,128]{1,2,0:T(8,128)(2,1)}, bf16[4,1024,128]{1,2,0:T(8,128)(2,1)S(1)}, u32[]{:S(2)}) copy-start(bf16[4,1024,128]{1,2,0:T(8,128)(2,1)S(1)} %multiply_convert_fusion) | copy-start | bytes 3145732
  98.2 1.7 copy-start.12
  99.1 0.8 copy-start.6
  99.9 0.7 copy-start.20
  102.1 51.7 %all-gather.2.cloned.1.call-start = ((), (), s32[]{:S(2)}) async-start(), calls=%async_computation.2 | async-start | bytes 1310720 | tf_op jit(solution)/shard_map/all_gather | solution.py:710
  124.9 1.3 copy-start.24
  124.9 1.7 copy-start.9
  125.0 1.7 copy-start.16
  125.0 2.0 copy-start.19
  126.2 1.7 copy-start.27
  128.0 0.8 copy-start.22
  140.1 15.8 %copy-start.7 = (f32[128,1024]{1,0:T(8,128)S(1)}, f32[128,1024]{1,0:T(8,128)}, u32[]{:S(2)}) copy-start(f32[128,1024]{1,0:T(8,128)} %copy-done.6) | copy-start | bytes 1572868
  140.1 15.8 %copy-start.15 = (bf16[4,1024,128]{1,2,0:T(8,128)(2,1)S(1)}, bf16[4,1024,128]{1,2,0:T(8,128)(2,1)}, u32[]{:S(2)}) copy-start(bf16[4,1024,128]{1,2,0:T(8,128)(2,1)} %copy-done.14) | copy-start | bytes 3145732
  153.9 2.3 copy-start.13
  162.4 1.7 copy-start.11
  164.0 1.0 copy-start.25
  166.1 1.7 copy-start.8
  169.2 1.4 copy-start.17
  169.2 1.4 copy-start.23
  171.9 1.2 copy-start.18
  171.9 1.3 copy-start.21
  173.2 3.7 %copy-start.1 = (bf16[2048,512]{1,0:T(8,128)(2,1)S(1)}, bf16[2048,512]{1,0:T(8,128)(2,1)}, u32[]{:S(2)}) copy-start(bf16[2048,512]{1,0:T(8,128)(2,1)} %fusion.3.neg_part) | copy-start | bytes 6291460
  173.2 3.7 %copy-start.3 = (s32[4,128]{1,0:T(4,128)S(1)}, s32[4,128]{1,0:T(4,128)}, u32[]{:S(2)}) copy-start(s32[4,128]{1,0:T(4,128)} %negs_ref.3) | copy-start | bytes 6148
  173.2 3.7 %copy-start.5 = (s32[256]{0:T(256)S(1)}, s32[256]{0:T(256)}, u32[]{:S(2)}) copy-start(s32[256]{0:T(256)} %param.7) | copy-start | bytes 3076
Sparse Core Ops, SparseCore 0:
  102.3 19.9 reduce-scatter.1
  129.8 24.0 all-gather.1

commit v2 on v1

v2 whole, which is shorter than its diff:
```python
import functools
import jax
import jax.numpy as jnp
from jax import lax
from jax.experimental import pallas as pl
from jax.experimental.pallas import tpu as pltpu
from jax.sharding import PartitionSpec as P

DH = 128
D = 512
CAP_H = 4
CAP_N = 8
OWNERS = 128
N_DP = 32
N_TABLE = 4
ROWS = 4096
BF = jnp.bfloat16
F32 = jnp.float32
MESH = pl.DeviceIdType.MESH

epsilon = 1e-06
sharpness = 20.0


def iota(shape, dim):
    return lax.broadcasted_iota(jnp.int32, shape, dim)


def one_zero(mask):
    return jnp.where(mask, 1.0, 0.0).astype(BF)


def mm(a, b):
    return lax.dot_general(a, b, (((1,), (0,)), ((), ())), preferred_element_type=F32)


def mm_nt(a, b):
    return lax.dot_general(a, b, (((1,), (1,)), ((), ())), preferred_element_type=F32)


def mm_tn(a, b):
    return lax.dot_general(a, b, (((0,), (0,)), ((), ())), preferred_element_type=F32)


def position():
    dp = lax.axis_index("dp")
    tx = lax.axis_index("table")
    return dp, tx


def partner(dp, tx, step):
    dx = lax.rem(step, 4)
    dc = lax.rem(lax.div(step, 4), 2)
    dy = lax.rem(lax.div(step, 8), 4)
    dz = lax.div(step, 32)
    c = lax.rem(lax.rem(dp, 2) + dc, 2)
    y = lax.rem(lax.rem(lax.div(dp, 2), 4) + dy, 4)
    z = lax.rem(lax.div(dp, 8) + dz, 4)
    x = lax.rem(tx + dx, 4)
    return z * 8 + y * 2 + c, x


def greet_all(barrier, dp, tx):
    def one(i, carry):
        pd, px = partner(dp, tx, i)
        pl.semaphore_signal(barrier, inc=1, device_id=(pd, px), device_id_type=MESH)
        return carry

    lax.fori_loop(1, OWNERS, one, 0)


def spread_all(src, dst, chunk, send_sem, recv_sem, dp, tx):
    me = dp * 4 + tx

    def one(i, carry):
        pd, px = partner(dp, tx, lax.rem(i * 37, OWNERS))
        pltpu.make_async_remote_copy(
            src_ref=src.at[pl.ds(pl.multiple_of((pd * 4 + px) * chunk, chunk), chunk)],
            dst_ref=dst.at[pl.ds(pl.multiple_of(me * chunk, chunk), chunk)],
            send_sem=send_sem,
            recv_sem=recv_sem,
            device_id=(pd, px),
            device_id_type=MESH,
        ).start()
        return carry

    lax.fori_loop(1, OWNERS, one, 0)
    own = pl.ds(pl.multiple_of(me * chunk, chunk), chunk)
    dst[own] = src[own]


def wait_rows(ref, count, sem):
    pltpu.make_async_copy(ref.at[pl.ds(0, count)], ref.at[pl.ds(0, count)], sem).wait()


class Ring:
    def __init__(self, dp, tx, send_sems, recv_sems):
        self.dp = dp
        self.tx = tx
        self.right = lax.rem(tx + 1, 4)
        self.left = lax.rem(tx + 3, 4)
        self.far = lax.rem(tx + 2, 4)
        self.send_sems = send_sems
        self.recv_sems = recv_sems

    def copy(self, src, dst, slot, to):
        return pltpu.make_async_remote_copy(
            src_ref=src,
            dst_ref=dst,
            send_sem=self.send_sems.at[slot],
            recv_sem=self.recv_sems.at[slot],
            device_id=(self.dp, to),
            device_id_type=MESH,
        )


class Gather:
    def __init__(self, ring, buf, block):
        h = block // 2
        r = ring

        def part(t, half):
            return buf.at[pl.ds(pl.multiple_of(t * block + half * h, h), h)]

        self.first = [
            r.copy(part(r.tx, 0), part(r.tx, 0), 0, r.right),
            r.copy(part(r.tx, 1), part(r.tx, 1), 1, r.left),
            r.copy(part(r.tx, 1), part(r.tx, 1), 2, r.right),
            r.copy(part(r.tx, 0), part(r.tx, 0), 3, r.left),
        ]
        self.second = [
            r.copy(part(r.left, 0), part(r.left, 0), 4, r.right),
            r.copy(part(r.right, 1), part(r.right, 1), 5, r.left),
        ]

    def start(self):
        for c in self.first:
            c.start()

    def forward(self):
        for c, d in zip(self.first[:2], self.second):
            c.wait_recv()
            d.start()

    def finish(self):
        for c in self.first[2:] + self.second:
            c.wait_recv()
        for c in self.first + self.second:
            c.wait_send()


class Scatter:
    def __init__(self, ring, part, land, onward, block):
        h = block // 2
        r = ring
        self.h = h
        self.ring = r
        self.part = part
        self.land = land
        self.onward = onward
        self.block = block

        self.first = [
            r.copy(self.at(r.far, 0), self.slot(0), 0, r.right),
            r.copy(self.at(r.far, 1), self.slot(1), 1, r.left),
            r.copy(self.at(r.right, 1), self.slot(2), 2, r.right),
            r.copy(self.at(r.left, 0), self.slot(3), 3, r.left),
        ]
        self.second = [
            r.copy(onward.at[pl.ds(0, h)], self.slot(4), 4, r.right),
            r.copy(onward.at[pl.ds(h, h)], self.slot(5), 5, r.left),
        ]

    def at(self, t, half):
        return self.part.at[self.span(t, half)]

    def span(self, t, half):
        return pl.ds(pl.multiple_of(t * self.block + half * self.h, self.h), self.h)

    def slot(self, i):
        return self.land.at[pl.ds(i * self.h, self.h)]

    def start(self):
        for c in self.first:
            c.start()

    def forward(self):
        h = self.h
        for i, t in enumerate((self.ring.right, self.ring.left)):
            self.first[i].wait_recv()
            self.onward[i * h : (i + 1) * h] = (
                self.land[i * h : (i + 1) * h].astype(F32) + self.part[self.span(t, i)].astype(F32)
            ).astype(BF)
            self.second[i].start()

    def finish(self):
        h = self.h
        for c in self.first[2:] + self.second:
            c.wait_recv()
        for c in self.first + self.second:
            c.wait_send()

        def got(i):
            return self.land[i * h : (i + 1) * h].astype(F32)

        return got(3) + got(4), got(2) + got(5)


def slots_of(ids):
    n = ids.shape[1]
    holder = lax.shift_right_logical(ids, 12)
    hits = iota((OWNERS, n), 0) == holder
    earlier = one_zero(iota((n, n), 0) < iota((n, n), 1))
    hits_b = one_zero(hits)
    before = jnp.sum(jnp.where(hits, mm(hits_b, earlier), 0.0), axis=0, keepdims=True)
    return holder, hits_b, before.astype(jnp.int32)


def wanted_rows(ids, hits_b, before, offset):
    n = ids.shape[1]
    marked = (ids & (ROWS - 1)) + 1
    chosen = iota((OWNERS, n), 0) == before + offset
    high = jnp.where(chosen, lax.shift_right_logical(marked, 6).astype(F32), 0.0).astype(BF)
    low = jnp.where(chosen, (marked & 63).astype(F32), 0.0).astype(BF)
    return 64.0 * mm_nt(hits_b, high) + mm_nt(hits_b, low)


def as_column(row):
    n = row.shape[1]
    wide = jnp.broadcast_to(row.astype(F32), (128, n))
    return jnp.transpose(wide)[:, 0:1].astype(jnp.int32)


def neg_row(negs_ref):
    return jnp.concatenate([negs_ref[u : u + 1, :] for u in range(4)], axis=1)


def part_mask(rows, width, per, parts):
    which = lax.rem(iota((rows, width), 0), 16) // per
    return [one_zero(which == c) for c in range(parts)]


def pick_parts(values, per, width):
    which = lax.div(lax.rem(iota((values.shape[0], width), 0), 16), per)
    out = values[:, 0:width]
    for c in range(1, values.shape[1] // width):
        out = jnp.where(which == c, values[:, c * width : (c + 1) * width], out)
    return out


def gather_rows(table, ids_col, out_ref, at):
    step = 512

    def one(i, total):
        base = pl.multiple_of(i * step, step)
        pick = one_zero(ids_col == iota((512, step), 1) + i * step)
        return total + mm(pick, table[pl.ds(base, step), :])

    total = lax.fori_loop(0, ROWS // step, one, jnp.zeros((512, D), F32))
    out_ref[at : at + 512, :] = total.astype(BF)


def spread_chunks(rows_ref, chunks_ref, at, cap):
    width = cap * 32
    block = 128 // cap
    many = block * 16
    r, q = iota((many, 128), 0), iota((many, 128), 1)
    fold = one_zero(
        (lax.rem(q, block) == lax.div(r, 16)) & (lax.div(q, block) == lax.rem(r, cap))
    )
    for b in range(cap):
        rows = jnp.concatenate(
            [
                rows_ref[at + k * 128 + b * block : at + k * 128 + (b + 1) * block, :]
                for k in range(cap)
            ],
            axis=0,
        )
        chunks_ref[b * many : (b + 1) * many, :] = pick_parts(mm(fold, rows), cap, width).astype(BF)


def unfold(chunks, per, parts):
    rows, width = chunks.shape
    masks = part_mask(rows, width, per, parts)
    return jnp.concatenate([chunks * m for m in masks], axis=1)


def take_slots(chunks_ref, slot_col, cap):
    n = slot_col.shape[0]
    total = jnp.zeros((n, D), F32)
    step = 512
    for i in range(OWNERS * 16 // step):
        r = iota((n, step), 1) + i * step
        key = lax.div(r, 16) * cap + lax.rem(r, cap)
        total = total + mm(
            one_zero(slot_col == key),
            unfold(chunks_ref[i * step : (i + 1) * step, :], cap, 16 // cap),
        )
    return total.astype(BF)


def put_slots(rows, slot_row, chunks_ref, cap):
    n = slot_row.shape[1]
    step = 512
    for i in range(OWNERS * 16 // step):
        r = iota((step, n), 0) + i * step
        key = lax.div(r, 16) * cap + lax.rem(r, cap)
        chunks_ref[i * step : (i + 1) * step, :] = pick_parts(
            mm(one_zero(slot_row == key), rows), cap, cap * 32
        ).astype(BF)


def row_sum(values):
    return jnp.sum(values, axis=-1, keepdims=True)


def row_mean(values):
    return jnp.mean(values, axis=-1, keepdims=True)


def normal(values):
    center = values - row_mean(values)
    factor = lax.rsqrt(row_mean(center * center) + epsilon)
    return center * factor, factor


def normal_back(grad, normed, factor):
    return factor * (grad - row_mean(grad) - normed * row_mean(grad * normed))


def unit_factor(values):
    return lax.rsqrt(row_sum(values * values) + epsilon)


def unit_back(grad, values, factor):
    return factor * (grad - values * (factor * factor * row_sum(grad * values)))


class Users:
    def __init__(self, lengths_ref):
        self.lengths = [lengths_ref[0, u] for u in range(4)]
        self.ends = []
        end = 0
        for length in self.lengths:
            end = end + length
            self.ends.append(end)

    def segment(self, t):
        return sum(jnp.where(t >= end, 1, 0) for end in self.ends)

    def start(self, t):
        return sum(jnp.where(t >= e, n, 0) for e, n in zip(self.ends, self.lengths))

    def length(self, t):
        out = jnp.where(t >= 0, self.lengths[0], 0)
        for u in range(1, 4):
            out = jnp.where(t >= self.ends[u - 1], self.lengths[u], out)
        return out


VM = pl.BlockSpec(memory_space=pltpu.VMEM)
HB = pl.BlockSpec(memory_space=pl.ANY)
SM = pl.BlockSpec(memory_space=pltpu.SMEM)
Q = 256
KEYS = 768
SCALE = DH**-0.5
PIECE = 80


def layer_kernel(
    ids_ref,
    negs_ref,
    lengths_ref,
    table_hbm,
    w_in_hbm,
    w_out_hbm,
    arrived_ref,
    hist_back,
    neg_back,
    weight_sum,
    table_ref,
    request_ref,
    picked_ref,
    hist_out,
    neg_out,
    hist_in,
    neg_in,
    w_in_ref,
    w_out_ref,
    emb_ref,
    unit_ref,
    normed_ref,
    proj_ref,
    slope_ref,
    weights_ref,
    dweights_ref,
    mixed_ref,
    factor_ref,
    gated_ref,
    part_ref,
    out_land,
    out_on,
    share_ref,
    dout_ref,
    dneg_ref,
    demb_ref,
    neg_land,
    neg_on,
    emb_land,
    emb_on,
    rest_ref,
    dgate_ref,
    dvalue_ref,
    dquery_ref,
    dkey_ref,
    dpre_ref,
    dwout_ref,
    weight_ref,
    weight_in,
    weight_mine,
    load_sems,
    all_send,
    all_recv,
    ring_send,
    ring_recv,
):
    dp, tx = position()
    barrier = pltpu.get_barrier_semaphore()
    greet_all(barrier, dp, tx)
    loads = [pltpu.make_async_copy(table_hbm, table_ref, load_sems.at[0])]
    for j in range(4):
        loads.append(
            pltpu.make_async_copy(
                w_in_hbm.at[j], w_in_ref.at[:, j * DH : (j + 1) * DH], load_sems.at[1 + j]
            )
        )
    loads.append(pltpu.make_async_copy(w_out_hbm, w_out_ref, load_sems.at[5]))
    for load in loads:
        load.start()

    def ring(i):
        return Ring(dp, tx, ring_send.at[i], ring_recv.at[i])

    right, left, far = ring(0).right, ring(0).left, ring(0).far

    def rows_of(b, n=Q):
        return pl.ds(pl.multiple_of(b * n, n), n)

    ids, negs = ids_ref[...], neg_row(negs_ref)
    holder_h, hits_h, before_h = slots_of(ids)
    holder_n, hits_n, before_n = slots_of(negs)
    wanted = wanted_rows(ids, hits_h, before_h, 0) + wanted_rows(negs, hits_n, before_n, CAP_H)
    request_ref[:, 0, :] = wanted.astype(jnp.int32) - 1
    slot_h = holder_h * CAP_H + before_h
    slot_n = holder_n * CAP_N + before_n
    slot_h_col, slot_n_col = as_column(slot_h), as_column(slot_n)
    users = Users(lengths_ref)

    pl.semaphore_wait(barrier, OWNERS - 1)
    spread_all(request_ref, arrived_ref, 1, all_send.at[0], all_recv.at[0], dp, tx)
    for load in loads:
        load.wait()
    wait_rows(arrived_ref, OWNERS - 1, all_recv.at[0])

    arrived = arrived_ref[:, 0, :]
    columns = [arrived[:, k : k + 1] for k in range(CAP_H + CAP_N)]
    gather_rows(table_ref, jnp.concatenate(columns[0:4], axis=0), picked_ref, 0)
    spread_chunks(picked_ref, hist_out, 0, CAP_H)
    spread_all(hist_out, hist_in, 16, all_send.at[1], all_recv.at[1], dp, tx)
    gather_rows(table_ref, jnp.concatenate(columns[4:8], axis=0), picked_ref, 512)
    gather_rows(table_ref, jnp.concatenate(columns[8:12], axis=0), picked_ref, 1024)
    spread_chunks(picked_ref, neg_out, 512, CAP_N)
    spread_all(neg_out, neg_in, 16, all_send.at[2], all_recv.at[2], dp, tx)

    wait_rows(hist_in, (OWNERS - 1) * 16, all_recv.at[1])
    emb_ref[rows_of(tx), :] = take_slots(hist_in, slot_h_col, CAP_H)
    hist = Gather(ring(0), emb_ref, Q)
    hist.start()

    def project(b):
        at = rows_of(b)
        normed = normal(emb_ref[at, :].astype(F32))[0].astype(BF)
        normed_ref[at, :] = normed
        pre = mm(normed, w_in_ref[...])
        gate = lax.logistic(pre)
        proj_ref[at, :] = (pre * gate).astype(BF)
        slope_ref[at, :] = gate * (1.0 + pre * (1.0 - gate))

    project(tx)
    hist.forward()
    for c in hist.first[2:]:
        c.wait_recv()
    project(left)
    project(right)
    for c in hist.second:
        c.wait_recv()
    project(far)

    wait_rows(neg_in, (OWNERS - 1) * 16, all_recv.at[2])
    neg_f = take_slots(neg_in, slot_n_col, CAP_N).astype(F32)
    neg_factor = unit_factor(neg_f)
    unit_ref[rows_of(tx, 512), :] = (neg_f * neg_factor).astype(BF)
    units = Gather(ring(1), unit_ref, 512)
    units.start()

    def keys_of(b):
        return pl.ds(pl.multiple_of(lax.div(b, 3) * Q, Q), KEYS)

    def attend(b):
        at, kr = rows_of(b), keys_of(b)
        scores = mm_nt(proj_ref[at, 256:384], proj_ref[kr, 384:512]) * SCALE
        t = iota((Q, 1), 0) + b * Q
        s = iota((Q, KEYS), 1) + lax.div(b, 3) * Q
        seen = (s <= t) & (s >= users.start(t))
        share = 1.0 / users.length(t).astype(F32)
        gate = lax.logistic(scores)
        weights = jnp.where(seen, scores * gate * share, 0.0).astype(BF)
        weights_ref[at, :] = weights
        dweights_ref[at, :] = jnp.where(
            seen, gate * (1.0 + scores * (1.0 - gate)) * (share * SCALE), 0.0
        )
        mixed, factor = normal(mm(weights, proj_ref[kr, 128:256]))
        mixed_ref[at, :] = mixed
        factor_ref[at, :] = jnp.broadcast_to(factor, (Q, DH))
        gated = (mixed * proj_ref[at, 0:128].astype(F32)).astype(BF)
        gated_ref[at, :] = gated
        part_ref[at, :] = mm(gated, w_out_ref[...]).astype(BF)

    out_sum = Scatter(ring(2), part_ref, out_land, out_on, Q)
    attend(far)
    out_sum.first[0].start()
    out_sum.first[1].start()
    attend(right)
    out_sum.first[2].start()
    attend(left)
    out_sum.first[3].start()
    units.forward()
    out_sum.forward()
    attend(tx)
    emb_f = emb_ref[rows_of(tx), :].astype(F32)
    first, second = out_sum.finish()
    y = emb_f + part_ref[rows_of(tx), :].astype(F32) + jnp.concatenate([first, second], axis=0)

    y_factor = unit_factor(y)
    y_unit = (y * y_factor).astype(BF)
    last = iota((Q, 1), 0) == Q - 1
    follow = jnp.where(
        last,
        emb_ref[rows_of(right), :].astype(F32)[0:1, :],
        pltpu.roll(emb_f, Q - 1, 0),
    )
    follow_factor = unit_factor(follow)
    follow_unit = (follow * follow_factor).astype(BF).astype(F32)
    y_unit_f = y_unit.astype(F32)
    t = iota((Q, 1), 0) + tx * Q
    segment = users.segment(t)
    valid = users.segment(t + 1) == segment
    grown_pos = jnp.exp(sharpness * row_sum(y_unit_f * follow_unit))
    total = grown_pos
    mine = [jnp.where(segment == u, 1.0, 0.0) for u in range(4)]
    units.finish()
    for c in range(4):
        grown = jnp.exp(sharpness * mm_nt(y_unit, unit_ref[c * 512 : (c + 1) * 512, :]))
        grown = jnp.concatenate(
            [grown[:, u * 128 : (u + 1) * 128] * mine[u] for u in range(4)], axis=1
        )
        total = total + row_sum(grown)
        share_ref[c] = grown
    scaled = jnp.where(valid, sharpness / total, 0.0)
    d_pos = jnp.where(valid, sharpness * (grown_pos / total - 1.0), 0.0)
    d_unit = d_pos * follow_unit
    for c in range(4):
        d_unit = d_unit + mm(
            (share_ref[c] * scaled).astype(BF), unit_ref[c * 512 : (c + 1) * 512, :]
        )
    d_rows = unit_back(d_unit, y, y_factor)
    dout_ref[rows_of(tx), :] = d_rows.astype(BF)
    douts = Gather(ring(3), dout_ref, Q)
    douts.start()
    neg_sum = Scatter(ring(4), dneg_ref, neg_land, neg_on, 512)

    def neg_grads(b):
        dneg_ref[rows_of(b, 512), :] = mm_tn((share_ref[b] * scaled).astype(BF), y_unit).astype(BF)

    neg_grads(far)
    d_follow = unit_back(d_pos * y_unit_f, follow, follow_factor)
    rest_ref[0:Q, :] = d_rows + jnp.where(t == tx * Q, 0.0, pltpu.roll(d_follow, 1, 0))
    rest_ref[Q : Q + 8, :] = jnp.where(iota((8, 1), 0) == 0, d_follow[Q - 1 : Q, :], 0.0)
    douts.forward()
    neg_sum.first[0].start()
    neg_sum.first[1].start()
    neg_grads(right)
    neg_sum.first[2].start()
    neg_grads(left)
    neg_sum.first[3].start()
    neg_grads(tx)

    dkey_ref[...] = jnp.zeros_like(dkey_ref)
    dvalue_ref[...] = jnp.zeros_like(dvalue_ref)
    dwout_ref[...] = jnp.zeros_like(dwout_ref)

    def attend_back(b):
        at, kr = rows_of(b), keys_of(b)
        d_out = dout_ref[at, :]
        d_gated = mm_nt(d_out, w_out_ref[...]).astype(BF).astype(F32)
        dwout_ref[...] += mm_tn(gated_ref[at, :], d_out)
        mixed = mixed_ref[at, :]
        dgate_ref[at, :] = (d_gated * mixed).astype(BF)
        d_mixed = normal_back(
            d_gated * proj_ref[at, 0:128].astype(F32), mixed, factor_ref[at, :][:, 0:1]
        ).astype(BF)
        d_scores = (mm_nt(d_mixed, proj_ref[kr, 128:256]) * dweights_ref[at, :]).astype(BF)
        dquery_ref[at, :] = mm(d_scores, proj_ref[kr, 384:512]).astype(BF)
        dkey_ref[kr, :] += mm_tn(d_scores, proj_ref[at, 256:384])
        dvalue_ref[kr, :] += mm_tn(weights_ref[at, :], d_mixed)

    attend_back(tx)
    for c in douts.first[2:]:
        c.wait_recv()
    attend_back(left)
    attend_back(right)
    neg_sum.forward()
    for c in douts.second:
        c.wait_recv()
    attend_back(far)

    def project_back(b):
        at = rows_of(b)
        d_proj = jnp.concatenate(
            [
                dgate_ref[at, :].astype(F32),
                dvalue_ref[at, :].astype(BF).astype(F32),
                dquery_ref[at, :].astype(F32),
                dkey_ref[at, :].astype(BF).astype(F32),
            ],
            axis=1,
        )
        d_pre = (d_proj * slope_ref[at, :]).astype(BF)
        dpre_ref[at, :] = d_pre
        normed, factor = normal(emb_ref[at, :].astype(F32))
        return normal_back(mm_nt(d_pre, w_in_ref[...]).astype(BF).astype(F32), normed, factor)

    emb_sum = Scatter(ring(5), demb_ref, emb_land, emb_on, Q)
    demb_ref[rows_of(far), :] = project_back(far).astype(BF)
    emb_sum.first[0].start()
    emb_sum.first[1].start()
    d_right = project_back(right)
    demb_ref[rows_of(right), :] = (
        d_right + jnp.where(iota((Q, 1), 0) == 0, rest_ref[Q : Q + 1, :], 0.0)
    ).astype(BF)
    emb_sum.first[2].start()
    demb_ref[rows_of(left), :] = project_back(left).astype(BF)
    emb_sum.first[3].start()
    rest_ref[0:Q, :] += project_back(tx)
    emb_sum.forward()

    d_win = mm_tn(normed_ref[...], dpre_ref[...]).astype(BF)
    for j in range(4):
        weight_ref[j * D : (j + 1) * D, :] = d_win[:, j * DH : (j + 1) * DH]
        weight_ref[2048 + j * DH : 2048 + (j + 1) * DH, :] = dwout_ref[
            :, j * DH : (j + 1) * DH
        ].astype(BF)
    own = pl.ds(pl.multiple_of(dp * PIECE, 16), PIECE)

    def out_piece(i, carry):
        pd, _ = partner(dp, tx, i * 4)
        pltpu.make_async_remote_copy(
            src_ref=weight_ref.at[pl.ds(pl.multiple_of(pd * PIECE, 16), PIECE)],
            dst_ref=weight_in.at[own],
            send_sem=all_send.at[5],
            recv_sem=all_recv.at[5],
            device_id=(pd, tx),
            device_id_type=MESH,
        ).start()
        return carry

    def back_piece(i, carry):
        pd, _ = partner(dp, tx, i * 4)
        pltpu.make_async_remote_copy(
            src_ref=weight_mine,
            dst_ref=weight_sum.at[own],
            send_sem=all_send.at[6],
            recv_sem=all_recv.at[6],
            device_id=(pd, tx),
            device_id_type=MESH,
        ).start()
        return carry

    first, second = emb_sum.finish()
    d_hist = rest_ref[0:Q, :] + jnp.concatenate([first, second], axis=0)
    wait_rows(hist_out, (OWNERS - 1) * 16, all_send.at[1])
    put_slots(d_hist.astype(BF), slot_h, hist_out, CAP_H)
    spread_all(hist_out, hist_back, 16, all_send.at[3], all_recv.at[3], dp, tx)

    first, second = neg_sum.finish()
    d_neg = dneg_ref[rows_of(tx, 512), :].astype(F32) + jnp.concatenate([first, second], axis=0)
    wait_rows(neg_out, (OWNERS - 1) * 16, all_send.at[2])
    put_slots(unit_back(d_neg, neg_f, neg_factor).astype(BF), slot_n, neg_out, CAP_N)
    spread_all(neg_out, neg_back, 16, all_send.at[4], all_recv.at[4], dp, tx)

    lax.fori_loop(1, N_DP, out_piece, 0)
    weight_in[own] = weight_ref[own]
    wait_rows(weight_in, (N_DP - 1) * PIECE, all_recv.at[5])
    total = weight_in[0:PIECE, :].astype(F32)
    for i in range(1, N_DP):
        total = total + weight_in[i * PIECE : (i + 1) * PIECE, :].astype(F32)
    weight_mine[...] = total.astype(BF)
    weight_sum[own] = total.astype(BF)
    lax.fori_loop(1, N_DP, back_piece, 0)

    wait_rows(hist_back, (OWNERS - 1) * 16, all_recv.at[3])
    wait_rows(neg_back, (OWNERS - 1) * 16, all_recv.at[4])
    wait_rows(weight_sum, (N_DP - 1) * PIECE, all_recv.at[6])
    for c in hist.first + hist.second + douts.first + douts.second:
        c.wait_send()
    wait_rows(request_ref, OWNERS - 1, all_send.at[0])
    wait_rows(hist_out, (OWNERS - 1) * 16, all_send.at[3])
    wait_rows(neg_out, (OWNERS - 1) * 16, all_send.at[4])
    wait_rows(weight_in, (N_DP - 1) * PIECE, all_send.at[5])
    wait_rows(weight_in, (N_DP - 1) * PIECE, all_send.at[6])


def layer(ids, negs, lengths, table, w_in, w_out):
    sem = pltpu.SemaphoreType.DMA
    vm = pltpu.VMEM
    return pl.pallas_call(
        layer_kernel,
        out_shape=[
            jax.ShapeDtypeStruct((OWNERS, 1, 128), jnp.int32),
            jax.ShapeDtypeStruct((OWNERS * 16, 128), BF),
            jax.ShapeDtypeStruct((OWNERS * 16, 256), BF),
            jax.ShapeDtypeStruct((2560, 128), BF),
        ],
        in_specs=[VM, VM, SM, HB, HB, HB],
        out_specs=[VM] * 4,
        scratch_shapes=[
            vm((ROWS, D), BF),
            vm((OWNERS, 1, 128), jnp.int32),
            vm((12 * OWNERS, D), BF),
            vm((OWNERS * 16, 128), BF),
            vm((OWNERS * 16, 256), BF),
            vm((OWNERS * 16, 128), BF),
            vm((OWNERS * 16, 256), BF),
            vm((D, D), BF),
            vm((DH, D), BF),
            vm((1024, D), BF),
            vm((2048, D), BF),
            vm((1024, D), BF),
            vm((1024, D), BF),
            vm((1024, D), F32),
            vm((1024, KEYS), BF),
            vm((1024, KEYS), F32),
            vm((1024, DH), F32),
            vm((1024, DH), F32),
            vm((1024, DH), BF),
            vm((1024, D), BF),
            vm((6 * 128, D), BF),
            vm((2 * 128, D), BF),
            vm((4, Q, 512), F32),
            vm((1024, D), BF),
            vm((2048, D), BF),
            vm((1024, D), BF),
            vm((6 * 256, D), BF),
            vm((2 * 256, D), BF),
            vm((6 * 128, D), BF),
            vm((2 * 128, D), BF),
            vm((Q + 8, D), F32),
            vm((1024, DH), BF),
            vm((1024, DH), F32),
            vm((1024, DH), BF),
            vm((1024, DH), F32),
            vm((1024, D), BF),
            vm((DH, D), F32),
            vm((2560, 128), BF),
            vm((2560, 128), BF),
            vm((PIECE, 128), BF),
            sem((6,)),
            sem((7,)),
            sem((7,)),
            sem((6, 6)),
            sem((6, 6)),
        ],
        compiler_params=pltpu.CompilerParams(
            collective_id=0, has_side_effects=True, vmem_limit_bytes=56 * 1024 * 1024
        ),
        name="layer",
    )(ids, negs, lengths, table, w_in, w_out)


def gather_chunks(chunks_ref, rows_ref, at, cap):
    block = 128 // cap
    many = block * 16
    q, r = iota((128, many), 0), iota((128, many), 1)
    fold = one_zero(
        (lax.rem(q, block) == lax.div(r, 16)) & (lax.div(q, block) == lax.rem(r, cap))
    )
    for b in range(cap):
        wide = unfold(chunks_ref[b * many : (b + 1) * many, :], cap, 16 // cap)
        rows = mm(fold, wide).astype(BF)
        for k in range(cap):
            rows_ref[at + k * 128 + b * block : at + k * 128 + (b + 1) * block, :] = rows[
                k * block : (k + 1) * block
            ]


def add_kernel(arrived_ref, hist_ref, neg_ref, out_ref, rows_ref, ids_ref):
    tile = out_ref.shape[0]
    step = pl.program_id(0)

    @pl.when(step == 0)
    def _():
        gather_chunks(hist_ref, rows_ref, 0, CAP_H)
        gather_chunks(neg_ref, rows_ref, 512, CAP_N)
        ids_ref[...] = jnp.transpose(arrived_ref[:, 0, :].astype(F32)).astype(jnp.int32)

    total = jnp.zeros((tile, D), F32)
    for k in range(0, CAP_H + CAP_N, 4):
        row = jnp.concatenate([ids_ref[k + j : k + j + 1, :] for j in range(4)], axis=1)
        put = one_zero(row == iota((tile, 512), 0) + step * tile)
        total = total + mm(put, rows_ref[k * 128 : (k + 4) * 128, :])
    out_ref[...] = total


def add_rows(arrived, hist_in, neg_in):
    tile = 512
    return pl.pallas_call(
        add_kernel,
        out_shape=jax.ShapeDtypeStruct((ROWS, D), F32),
        grid=(ROWS // tile,),
        in_specs=[VM] * 3,
        out_specs=pl.BlockSpec((tile, D), lambda i: (i, 0)),
        scratch_shapes=[
            pltpu.VMEM((12 * OWNERS, D), BF),
            pltpu.VMEM((128, 128), jnp.int32),
        ],
        compiler_params=pltpu.CompilerParams(vmem_limit_bytes=32 * 1024 * 1024),
        name="add_rows",
    )(arrived, hist_in, neg_in)


def on_device(table, item_ids, negatives, lengths, w_in, w_out):
    arrived, hist_back, neg_back, weight_sum = layer(
        item_ids.reshape(1, -1), negatives, lengths, table, w_in, w_out
    )
    grad_w_in = weight_sum[:2048].reshape(4, D, DH).astype(F32)
    grad_w_out = weight_sum[2048:].reshape(4, DH, DH).transpose(1, 0, 2).reshape(DH, D).astype(F32)
    grad_table = add_rows(arrived, hist_back, neg_back)
    return (grad_table, grad_w_in, grad_w_out)


def solution(mesh):
    placed = (
        P(("dp", "table"), None),
        P(("dp", "table")),
        P("dp", "table"),
        P("dp", None),
        P(None, None, "table"),
        P("table", None),
    )
    return jax.shard_map(
        on_device,
        mesh=mesh,
        in_specs=placed,
        out_specs=(P(("dp", "table"), None), P(None, None, "table"), P("table", None)),
        check_vma=False,
    )
```

time: 260 us -> 188 us (0.72)
  waiting for transfers between devices: 31.4 us -> 0 us
  Pallas kernels: 153 us -> 182 us
  matrix products: 25.6 us -> 0 us
  other arithmetic: 20.9 us -> 1.77 us
  between operations: 14.5 us -> 0.66 us
  local copies, waits for them, and re-layouts: 14 us -> 3.15 us
    pallas_call x2 -> x1, Pallas kernels: 143 us -> 173 us  [layer(): pl.pallas_call(layer_kernel, out_shape=[jax.ShapeDtypeStruct((OWNERS, 1,...]
    dot_general x14 -> x0, matrix products: 23.7 us -> none  [the longest x3 6.15 us: branch(): jnp.einsum('hqk,khd->qhd', weights, value, preferred_element_type=jnp.flo...]
    reduce_scatter x1 -> x0, waiting for transfers between devices: 17.7 us -> none  [on_device(): lax.psum_scatter(partial_out.astype(jnp.bfloat16), 'table', scatter_dimen...]
    all_gather x1 -> x0, waiting for transfers between devices: 13.7 us -> none  [on_device(): lax.all_gather(d_rows.astype(jnp.bfloat16), 'table', axis=0, tiled=True)]
    convert_element_type x10 -> x2, other arithmetic: 10.5 us -> 1.77 us  [the longest x1 1.04 us: on_device(): grad_w_in = weight_sum[:2048].reshape(4, D, DH).astype(F32)]
    reduce_sum x9 -> x0, other arithmetic: 5.38 us -> none  [the longest x3 2.15 us: unit_rows(): jnp.sum(values * values, axis=-1, keepdims=True) + epsilon]
    unnamed x57 -> x8, local copies, waits for them, and re-layouts: 7.62 us -> 3.1 us
    dynamic_update_slice x1 -> x0, local copies, waits for them, and re-layouts: 2.84 us -> none  [sampled_loss(): following = lax.dynamic_slice_in_dim(padded, row_start + 1, rows, 0)]
  transfers between devices with their start and end apart: 2 -> 0, of which waited for: 2 -> 0; matrix products, arithmetic and copies ran while one was open for 5% -> 0% of each run, Pallas kernels for 0% -> 0%
where the time goes in v2:
time: 188 us
  Pallas kernels  182 us (97%)
  local copies, waits for them, and re-layouts  3.15 us (2%)
    pallas_call x1, Pallas kernels, layer(): pl.pallas_call(layer_kernel, out_shape=[jax.ShapeDtypeStruct((OWNERS, 1,...  173 us
    pallas_call x1, Pallas kernels, add_rows(): pl.pallas_call(add_kernel, out_shape=jax.ShapeDtypeStruct((ROWS, D), F32)...  9.82 us

profile of v2, /device:TPU:1, one launch (start us, length us, event | category | flops | bytes accessed | tf_op | source)
XLA Modules:
  0.0 188.0 jit_solution(10821919956218406946)
XLA Ops:
  0.6 172.6 %layer.1 = (s32[128,1,128]{2,1,0:T(1,128)}, bf16[2048,128]{1,0:T(8,128)(2,1)}, bf16[2048,256]{1,0:T(8,128)(2,1)}, bf16[2560,128]{1,0:T(8,128)(2,1)}) custom-call(s32[1,256]{1,0:T(1,128)} %bitcast.13, s32[4,128]{1,0:T(4,128)} %negs_ref.1, s32[1,4]{1,0:T(1,128)} %lengths_ref.1, bf16[4096,512]{1,0:T(8,128)(2,1)} %table_hbm.1, bf16[4,512,128]{2,1,0:T(8,128)(2,1)} %w_in_hbm.1, ...), custom_call_target="tpu_custom_call" | custom-call | tf_op jit(solution)/shard_map/layer/pallas_call | solution.py:726
  173.2 0.0 copy-start
  173.3 1.2 copy-done
  174.5 0.0 copy-start.1
  174.5 1.0 copy-done.1
  175.5 0.0 copy-start.2
  175.5 0.8 copy-done.2
  176.3 0.0 copy-start.3
  176.4 9.8 %add_rows.1 = f32[4096,512]{1,0:T(8,128)} custom-call(s32[128,1,128]{2,1,0:T(1,128)S(1)} %copy-done.2, bf16[2048,128]{1,0:T(8,128)(2,1)S(1)} %copy-done.1, bf16[2048,256]{1,0:T(8,128)(2,1)S(1)} %copy-done), custom_call_target="tpu_custom_call" | custom-call | tf_op jit(solution)/shard_map/add_rows/pallas_call | solution.py:826
  186.2 0.0 copy-done.3
  186.2 1.0 convert.4
  187.3 0.7 copy_bitcast_fusion
  (2 shorter events, 0.0 us)
Async XLA Ops:
  173.2 1.2 copy-start
  174.5 1.0 copy-start.1
  175.5 0.8 copy-start.2
  176.3 9.8 %copy-start.3 = (bf16[2560,128]{1,0:T(8,128)(2,1)S(1)}, bf16[2560,128]{1,0:T(8,128)(2,1)}, u32[]{:S(2)}) copy-start(bf16[2560,128]{1,0:T(8,128)(2,1)} %get-tuple-element.10) | copy-start | bytes 1966084

commit v3 on v2

--- a/solution.py
+++ b/solution.py
@@ -48,45 +48,79 @@
     return dp, tx
 
 
-def partner(dp, tx, step):
-    dx = lax.rem(step, 4)
-    dc = lax.rem(lax.div(step, 4), 2)
-    dy = lax.rem(lax.div(step, 8), 4)
-    dz = lax.div(step, 32)
-    c = lax.rem(lax.rem(dp, 2) + dc, 2)
-    y = lax.rem(lax.rem(lax.div(dp, 2), 4) + dy, 4)
-    z = lax.rem(lax.div(dp, 8) + dz, 4)
-    x = lax.rem(tx + dx, 4)
-    return z * 8 + y * 2 + c, x
-
-
-def greet_all(barrier, dp, tx):
+def coordinates(dp, tx):
+    z, y, c = lax.div(dp, 8), lax.rem(lax.div(dp, 2), 4), lax.rem(dp, 2)
+    near = [(core, lax.rem(tx + dx, 4)) for core in (1 - c, c) for dx in range(4)]
+    return z, y, near[4:] + near[:4]
+
+
+def plane_base(z, y, step):
+    return lax.rem(z + lax.div(step, 4), 4) * 8 + lax.rem(y + lax.rem(step, 4), 4) * 2
+
+
+def each_partner(dp, tx, do):
+    z, y, near = coordinates(dp, tx)
+
     def one(i, carry):
-        pd, px = partner(dp, tx, i)
-        pl.semaphore_signal(barrier, inc=1, device_id=(pd, px), device_id_type=MESH)
+        base = plane_base(z, y, lax.rem(i * 7, 16))
+        for core, x in near:
+            do(base + core, x)
         return carry
 
-    lax.fori_loop(1, OWNERS, one, 0)
+    lax.fori_loop(1, 16, one, 0)
+    for core, x in near[1:]:
+        do(z * 8 + y * 2 + core, x)
+
+
+def each_dp(dp, tx, do):
+    z, y, near = coordinates(dp, tx)
+    mine, other = near[0][0], near[4][0]
+
+    def one(i, carry):
+        base = plane_base(z, y, lax.rem(i * 7, 16))
+        do(base + mine)
+        do(base + other)
+        return carry
+
+    lax.fori_loop(1, 16, one, 0)
+    do(z * 8 + y * 2 + other)
+
+
+def signal(sem, dp, x):
+    pl.semaphore_signal(sem, inc=1, device_id=(dp, x), device_id_type=MESH)
+
+
+def greet_planes(barrier, dp, tx):
+    z, y, near = coordinates(dp, tx)
+    for core, x in near[1:]:
+        signal(barrier, z * 8 + y * 2 + core, x)
+    core, x = near[0]
+    for i in range(1, 16):
+        signal(barrier, plane_base(z, y, i) + core, x)
+
+
+def greet_again(sem, dp, tx):
+    z, y, near = coordinates(dp, tx)
+    for core, x in near[1:]:
+        signal(sem, z * 8 + y * 2 + core, x)
 
 
 def spread_all(src, dst, chunk, send_sem, recv_sem, dp, tx):
     me = dp * 4 + tx
-
-    def one(i, carry):
-        pd, px = partner(dp, tx, lax.rem(i * 37, OWNERS))
+    land = pl.ds(pl.multiple_of(me * chunk, chunk), chunk)
+
+    def one(pd, px):
         pltpu.make_async_remote_copy(
             src_ref=src.at[pl.ds(pl.multiple_of((pd * 4 + px) * chunk, chunk), chunk)],
-            dst_ref=dst.at[pl.ds(pl.multiple_of(me * chunk, chunk), chunk)],
+            dst_ref=dst.at[land],
             send_sem=send_sem,
             recv_sem=recv_sem,
             device_id=(pd, px),
             device_id_type=MESH,
         ).start()
-        return carry
-
-    lax.fori_loop(1, OWNERS, one, 0)
-    own = pl.ds(pl.multiple_of(me * chunk, chunk), chunk)
-    dst[own] = src[own]
+
+    each_partner(dp, tx, one)
+    dst[land] = src[land]
 
 
 def wait_rows(ref, count, sem):
@@ -374,12 +408,15 @@
     table_hbm,
     w_in_hbm,
     w_out_hbm,
+    ids_out,
+    rows_out,
+    weight_out,
+    table_ref,
+    request_ref,
     arrived_ref,
+    arrived_t_ref,
     hist_back,
     neg_back,
-    weight_sum,
-    table_ref,
-    request_ref,
     picked_ref,
     hist_out,
     neg_out,
@@ -418,6 +455,8 @@
     weight_ref,
     weight_in,
     weight_mine,
+    weight_sum,
+    met_sem,
     load_sems,
     all_send,
     all_recv,
@@ -426,7 +465,7 @@
 ):
     dp, tx = position()
     barrier = pltpu.get_barrier_semaphore()
-    greet_all(barrier, dp, tx)
+    greet_planes(barrier, dp, tx)
     loads = [pltpu.make_async_copy(table_hbm, table_ref, load_sems.at[0])]
     for j in range(4):
         loads.append(
@@ -450,13 +489,15 @@
     holder_h, hits_h, before_h = slots_of(ids)
     holder_n, hits_n, before_n = slots_of(negs)
     wanted = wanted_rows(ids, hits_h, before_h, 0) + wanted_rows(negs, hits_n, before_n, CAP_H)
+    pl.semaphore_wait(barrier, 22)
+    greet_again(met_sem, dp, tx)
     request_ref[:, 0, :] = wanted.astype(jnp.int32) - 1
     slot_h = holder_h * CAP_H + before_h
     slot_n = holder_n * CAP_N + before_n
     slot_h_col, slot_n_col = as_column(slot_h), as_column(slot_n)
     users = Users(lengths_ref)
 
-    pl.semaphore_wait(barrier, OWNERS - 1)
+    pl.semaphore_wait(met_sem, 7)
     spread_all(request_ref, arrived_ref, 1, all_send.at[0], all_recv.at[0], dp, tx)
     for load in loads:
         load.wait()
@@ -495,6 +536,8 @@
     for c in hist.second:
         c.wait_recv()
     project(far)
+
+    arrived_t_ref[...] = jnp.transpose(arrived.astype(F32)).astype(jnp.int32)
 
     wait_rows(neg_in, (OWNERS - 1) * 16, all_recv.at[2])
     neg_f = take_slots(neg_in, slot_n_col, CAP_N).astype(F32)
@@ -662,8 +705,7 @@
         ].astype(BF)
     own = pl.ds(pl.multiple_of(dp * PIECE, 16), PIECE)
 
-    def out_piece(i, carry):
-        pd, _ = partner(dp, tx, i * 4)
+    def out_piece(pd):
         pltpu.make_async_remote_copy(
             src_ref=weight_ref.at[pl.ds(pl.multiple_of(pd * PIECE, 16), PIECE)],
             dst_ref=weight_in.at[own],
@@ -672,10 +714,8 @@
             device_id=(pd, tx),
             device_id_type=MESH,
         ).start()
-        return carry
-
-    def back_piece(i, carry):
-        pd, _ = partner(dp, tx, i * 4)
+
+    def back_piece(pd):
         pltpu.make_async_remote_copy(
             src_ref=weight_mine,
             dst_ref=weight_sum.at[own],
@@ -684,7 +724,6 @@
             device_id=(pd, tx),
             device_id_type=MESH,
         ).start()
-        return carry
 
     first, second = emb_sum.finish()
     d_hist = rest_ref[0:Q, :] + jnp.concatenate([first, second], axis=0)
@@ -698,7 +737,7 @@
     put_slots(unit_back(d_neg, neg_f, neg_factor).astype(BF), slot_n, neg_out, CAP_N)
     spread_all(neg_out, neg_back, 16, all_send.at[4], all_recv.at[4], dp, tx)
 
-    lax.fori_loop(1, N_DP, out_piece, 0)
+    each_dp(dp, tx, out_piece)
     weight_in[own] = weight_ref[own]
     wait_rows(weight_in, (N_DP - 1) * PIECE, all_recv.at[5])
     total = weight_in[0:PIECE, :].astype(F32)
@@ -706,11 +745,22 @@
         total = total + weight_in[i * PIECE : (i + 1) * PIECE, :].astype(F32)
     weight_mine[...] = total.astype(BF)
     weight_sum[own] = total.astype(BF)
-    lax.fori_loop(1, N_DP, back_piece, 0)
+    each_dp(dp, tx, back_piece)
 
     wait_rows(hist_back, (OWNERS - 1) * 16, all_recv.at[3])
+    gather_chunks(hist_back, picked_ref, 0, CAP_H)
     wait_rows(neg_back, (OWNERS - 1) * 16, all_recv.at[4])
+    gather_chunks(neg_back, picked_ref, 512, CAP_N)
     wait_rows(weight_sum, (N_DP - 1) * PIECE, all_recv.at[6])
+    results = [
+        pltpu.make_async_copy(arrived_t_ref, ids_out, load_sems.at[0]),
+        pltpu.make_async_copy(picked_ref, rows_out, load_sems.at[1]),
+        pltpu.make_async_copy(weight_sum, weight_out, load_sems.at[2]),
+    ]
+    for move in results:
+        move.start()
+    for move in results:
+        move.wait()
     for c in hist.first + hist.second + douts.first + douts.second:
         c.wait_send()
     wait_rows(request_ref, OWNERS - 1, all_send.at[0])
@@ -726,16 +776,19 @@
     return pl.pallas_call(
         layer_kernel,
         out_shape=[
-            jax.ShapeDtypeStruct((OWNERS, 1, 128), jnp.int32),
-            jax.ShapeDtypeStruct((OWNERS * 16, 128), BF),
-            jax.ShapeDtypeStruct((OWNERS * 16, 256), BF),
+            jax.ShapeDtypeStruct((128, 128), jnp.int32),
+            jax.ShapeDtypeStruct((12 * OWNERS, D), BF),
             jax.ShapeDtypeStruct((2560, 128), BF),
         ],
         in_specs=[VM, VM, SM, HB, HB, HB],
-        out_specs=[VM] * 4,
+        out_specs=[HB] * 3,
         scratch_shapes=[
             vm((ROWS, D), BF),
             vm((OWNERS, 1, 128), jnp.int32),
+            vm((OWNERS, 1, 128), jnp.int32),
+            vm((128, 128), jnp.int32),
+            vm((OWNERS * 16, 128), BF),
+            vm((OWNERS * 16, 256), BF),
             vm((12 * OWNERS, D), BF),
             vm((OWNERS * 16, 128), BF),
             vm((OWNERS * 16, 256), BF),
@@ -774,6 +827,8 @@
             vm((2560, 128), BF),
             vm((2560, 128), BF),
             vm((PIECE, 128), BF),
+            vm((2560, 128), BF),
+            pltpu.SemaphoreType.REGULAR,
             sem((6,)),
             sem((7,)),
             sem((7,)),
@@ -803,15 +858,21 @@
             ]
 
 
-def add_kernel(arrived_ref, hist_ref, neg_ref, out_ref, rows_ref, ids_ref):
+def add_kernel(ids_hbm, rows_hbm, weight_hbm, out_ref, w_in_ref, w_out_ref, ids_ref, rows_ref, weight_ref, sems):
     tile = out_ref.shape[0]
     step = pl.program_id(0)
 
     @pl.when(step == 0)
     def _():
-        gather_chunks(hist_ref, rows_ref, 0, CAP_H)
-        gather_chunks(neg_ref, rows_ref, 512, CAP_N)
-        ids_ref[...] = jnp.transpose(arrived_ref[:, 0, :].astype(F32)).astype(jnp.int32)
+        moves = [
+            pltpu.make_async_copy(ids_hbm, ids_ref, sems.at[0]),
+            pltpu.make_async_copy(rows_hbm, rows_ref, sems.at[1]),
+            pltpu.make_async_copy(weight_hbm, weight_ref, sems.at[2]),
+        ]
+        for move in moves:
+            move.start()
+        for move in moves:
+            move.wait()
 
     total = jnp.zeros((tile, D), F32)
     for k in range(0, CAP_H + CAP_N, 4):
@@ -819,33 +880,48 @@
         put = one_zero(row == iota((tile, 512), 0) + step * tile)
         total = total + mm(put, rows_ref[k * 128 : (k + 4) * 128, :])
     out_ref[...] = total
-
-
-def add_rows(arrived, hist_in, neg_in):
+    w_in_ref[...] = weight_ref[pl.ds(pl.multiple_of(step * 256, 256), 256), :].astype(F32)
+    w_out_ref[...] = jnp.concatenate(
+        [
+            weight_ref[pl.ds(pl.multiple_of(2048 + c * 128 + step * 16, 16), 16), :]
+            for c in range(4)
+        ],
+        axis=1,
+    ).astype(F32)
+
+
+def add_rows(ids, rows, weight):
     tile = 512
+    anywhere = pl.BlockSpec(memory_space=pl.ANY)
     return pl.pallas_call(
         add_kernel,
-        out_shape=jax.ShapeDtypeStruct((ROWS, D), F32),
+        out_shape=[
+            jax.ShapeDtypeStruct((ROWS, D), F32),
+            jax.ShapeDtypeStruct((2048, DH), F32),
+            jax.ShapeDtypeStruct((DH, D), F32),
+        ],
         grid=(ROWS // tile,),
-        in_specs=[VM] * 3,
-        out_specs=pl.BlockSpec((tile, D), lambda i: (i, 0)),
+        in_specs=[anywhere] * 3,
+        out_specs=[
+            pl.BlockSpec((tile, D), lambda i: (i, 0)),
+            pl.BlockSpec((256, DH), lambda i: (i, 0)),
+            pl.BlockSpec((16, D), lambda i: (i, 0)),
+        ],
         scratch_shapes=[
+            pltpu.VMEM((128, 128), jnp.int32),
             pltpu.VMEM((12 * OWNERS, D), BF),
-            pltpu.VMEM((128, 128), jnp.int32),
+            pltpu.VMEM((2560, 128), BF),
+            pltpu.SemaphoreType.DMA((3,)),
         ],
-        compiler_params=pltpu.CompilerParams(vmem_limit_bytes=32 * 1024 * 1024),
+        compiler_params=pltpu.CompilerParams(vmem_limit_bytes=56 * 1024 * 1024),
         name="add_rows",
-    )(arrived, hist_in, neg_in)
+    )(ids, rows, weight)
 
 
 def on_device(table, item_ids, negatives, lengths, w_in, w_out):
-    arrived, hist_back, neg_back, weight_sum = layer(
-        item_ids.reshape(1, -1), negatives, lengths, table, w_in, w_out
-    )
-    grad_w_in = weight_sum[:2048].reshape(4, D, DH).astype(F32)
-    grad_w_out = weight_sum[2048:].reshape(4, DH, DH).transpose(1, 0, 2).reshape(DH, D).astype(F32)
-    grad_table = add_rows(arrived, hist_back, neg_back)
-    return (grad_table, grad_w_in, grad_w_out)
+    ids, rows, weight = layer(item_ids.reshape(1, -1), negatives, lengths, table, w_in, w_out)
+    grad_table, grad_w_in, grad_w_out = add_rows(ids, rows, weight)
+    return (grad_table, grad_w_in.reshape(4, D, DH), grad_w_out)
 
 
 def solution(mesh):

time: 188 us -> 173 us (0.920)
  Pallas kernels: 182 us -> 172 us
  local copies, waits for them, and re-layouts: 3.15 us -> 0 us
    pallas_call x2, Pallas kernels: 182 us -> 172 us  [the longest x1 162 us: layer(): pl.pallas_call(layer_kernel, out_shape=[jax.ShapeDtypeStruct((128, 128),...]
    unnamed x8 -> x0, local copies, waits for them, and re-layouts: 3.1 us -> none
where the time goes in v3:
time: 173 us
  Pallas kernels  172 us (99%)
    pallas_call x1, Pallas kernels, layer(): pl.pallas_call(layer_kernel, out_shape=[jax.ShapeDtypeStruct((128, 128),...  162 us
    pallas_call x1, Pallas kernels, add_rows(): pl.pallas_call(add_kernel, out_shape=[jax.ShapeDtypeStruct((ROWS, D), F32...  10.5 us

profile of v3, /device:TPU:1, one launch (start us, length us, event | category | flops | bytes accessed | tf_op | source)
XLA Modules:
  0.0 173.2 jit_solution(2550402860755644971)
XLA Ops:
  0.6 161.8 %layer.1 = (s32[128,128]{1,0:T(8,128)}, bf16[1536,512]{1,0:T(8,128)(2,1)}, bf16[2560,128]{1,0:T(8,128)(2,1)}) custom-call(s32[1,256]{1,0:T(1,128)} %bitcast.2, s32[4,128]{1,0:T(4,128)} %negs_ref.1, s32[1,4]{1,0:T(1,128)} %lengths_ref.1, bf16[4096,512]{1,0:T(8,128)(2,1)} %table_hbm.1, bf16[4,512,128]{2,1,0:T(8,128)(2,1)} %w_in_hbm.1, bf16[128,512]{1,0:T(8,128)(2,1)} %w_out_hbm.1), custom_call_target="tpu_custom_call" | custom-call | tf_op jit(solution)/shard_map/layer/pallas_call | solution.py:776
  162.5 10.5 %add_rows.1 = (f32[4096,512]{1,0:T(8,128)}, f32[2048,128]{1,0:T(8,128)}, f32[128,512]{1,0:T(8,128)}) custom-call(s32[128,128]{1,0:T(8,128)} %get-tuple-element.9.ids_hbm, bf16[1536,512]{1,0:T(8,128)(2,1)} %get-tuple-element.10.rows_hbm, bf16[2560,128]{1,0:T(8,128)(2,1)} %get-tuple-element.11.weight_hbm), custom_call_target="tpu_custom_call" | custom-call | tf_op jit(solution)/shard_map/add_rows/pallas_call | solution.py:896

commit v4 on v3

--- a/solution.py
+++ b/solution.py
@@ -425,6 +425,7 @@
     w_in_ref,
     w_out_ref,
     emb_ref,
+    neg_ref,
     unit_ref,
     normed_ref,
     proj_ref,
@@ -434,15 +435,21 @@
     mixed_ref,
     factor_ref,
     gated_ref,
-    part_ref,
-    out_land,
-    out_on,
-    share_ref,
-    dout_ref,
-    dneg_ref,
+    y_ref,
+    y_factor_ref,
+    y_unit_ref,
+    grown_ref,
+    shares_ref,
+    total_ref,
+    whole_ref,
+    drows_ref,
+    dgated_ref,
+    dgated_land,
+    dgated_on,
+    dout_part,
+    dout_land,
+    dout_on,
     demb_ref,
-    neg_land,
-    neg_on,
     emb_land,
     emb_on,
     rest_ref,
@@ -451,7 +458,6 @@
     dquery_ref,
     dkey_ref,
     dpre_ref,
-    dwout_ref,
     weight_ref,
     weight_in,
     weight_mine,
@@ -462,6 +468,8 @@
     all_recv,
     ring_send,
     ring_recv,
+    total_send,
+    total_recv,
 ):
     dp, tx = position()
     barrier = pltpu.get_barrier_semaphore()
@@ -473,7 +481,11 @@
                 w_in_hbm.at[j], w_in_ref.at[:, j * DH : (j + 1) * DH], load_sems.at[1 + j]
             )
         )
-    loads.append(pltpu.make_async_copy(w_out_hbm, w_out_ref, load_sems.at[5]))
+    loads.append(
+        pltpu.make_async_copy(
+            w_out_hbm, w_out_ref.at[pl.ds(pl.multiple_of(tx * DH, DH), DH)], load_sems.at[5]
+        )
+    )
     for load in loads:
         load.start()
 
@@ -494,13 +506,15 @@
     request_ref[:, 0, :] = wanted.astype(jnp.int32) - 1
     slot_h = holder_h * CAP_H + before_h
     slot_n = holder_n * CAP_N + before_n
-    slot_h_col, slot_n_col = as_column(slot_h), as_column(slot_n)
-    users = Users(lengths_ref)
 
     pl.semaphore_wait(met_sem, 7)
     spread_all(request_ref, arrived_ref, 1, all_send.at[0], all_recv.at[0], dp, tx)
     for load in loads:
         load.wait()
+    w_outs = Gather(ring(1), w_out_ref, DH)
+    w_outs.start()
+    slot_h_col, slot_n_col = as_column(slot_h), as_column(slot_n)
+    users = Users(lengths_ref)
     wait_rows(arrived_ref, OWNERS - 1, all_recv.at[0])
 
     arrived = arrived_ref[:, 0, :]
@@ -508,6 +522,7 @@
     gather_rows(table_ref, jnp.concatenate(columns[0:4], axis=0), picked_ref, 0)
     spread_chunks(picked_ref, hist_out, 0, CAP_H)
     spread_all(hist_out, hist_in, 16, all_send.at[1], all_recv.at[1], dp, tx)
+    w_outs.forward()
     gather_rows(table_ref, jnp.concatenate(columns[4:8], axis=0), picked_ref, 512)
     gather_rows(table_ref, jnp.concatenate(columns[8:12], axis=0), picked_ref, 1024)
     spread_chunks(picked_ref, neg_out, 512, CAP_N)
@@ -539,133 +554,163 @@
 
     arrived_t_ref[...] = jnp.transpose(arrived.astype(F32)).astype(jnp.int32)
 
-    wait_rows(neg_in, (OWNERS - 1) * 16, all_recv.at[2])
-    neg_f = take_slots(neg_in, slot_n_col, CAP_N).astype(F32)
-    neg_factor = unit_factor(neg_f)
-    unit_ref[rows_of(tx, 512), :] = (neg_f * neg_factor).astype(BF)
-    units = Gather(ring(1), unit_ref, 512)
-    units.start()
+    mine = pl.multiple_of(tx * 1024, 1024)
 
     def keys_of(b):
-        return pl.ds(pl.multiple_of(lax.div(b, 3) * Q, Q), KEYS)
+        low = max(b - 2, 0)
+        return slice(low * Q, (b + 1) * Q), low
 
     def attend(b):
-        at, kr = rows_of(b), keys_of(b)
+        at = slice(b * Q, (b + 1) * Q)
+        kr, low = keys_of(b)
+        n = kr.stop - kr.start
         scores = mm_nt(proj_ref[at, 256:384], proj_ref[kr, 384:512]) * SCALE
         t = iota((Q, 1), 0) + b * Q
-        s = iota((Q, KEYS), 1) + lax.div(b, 3) * Q
+        s = iota((Q, n), 1) + low * Q
         seen = (s <= t) & (s >= users.start(t))
         share = 1.0 / users.length(t).astype(F32)
         gate = lax.logistic(scores)
         weights = jnp.where(seen, scores * gate * share, 0.0).astype(BF)
-        weights_ref[at, :] = weights
-        dweights_ref[at, :] = jnp.where(
+        weights_ref[at, 0:n] = weights
+        dweights_ref[at, 0:n] = jnp.where(
             seen, gate * (1.0 + scores * (1.0 - gate)) * (share * SCALE), 0.0
         )
         mixed, factor = normal(mm(weights, proj_ref[kr, 128:256]))
         mixed_ref[at, :] = mixed
         factor_ref[at, :] = jnp.broadcast_to(factor, (Q, DH))
-        gated = (mixed * proj_ref[at, 0:128].astype(F32)).astype(BF)
-        gated_ref[at, :] = gated
-        part_ref[at, :] = mm(gated, w_out_ref[...]).astype(BF)
-
-    out_sum = Scatter(ring(2), part_ref, out_land, out_on, Q)
-    attend(far)
-    out_sum.first[0].start()
-    out_sum.first[1].start()
-    attend(right)
-    out_sum.first[2].start()
-    attend(left)
-    out_sum.first[3].start()
-    units.forward()
-    out_sum.forward()
-    attend(tx)
+        gated_ref[pl.ds(mine + b * Q, Q), :] = (mixed * proj_ref[at, 0:128].astype(F32)).astype(BF)
+
+    gates = Gather(ring(2), gated_ref, 1024)
+    attend(0)
+    attend(1)
+    gates.first[0].start()
+    gates.first[3].start()
+    attend(2)
+    attend(3)
+    gates.first[1].start()
+    gates.first[2].start()
+
+    wait_rows(neg_in, (OWNERS - 1) * 16, all_recv.at[2])
+    neg_ref[...] = take_slots(neg_in, slot_n_col, CAP_N)
+    gates.forward()
+    neg_f = neg_ref[...].astype(F32)
+    neg_factor = unit_factor(neg_f)
+    unit_ref[...] = (neg_f * neg_factor).astype(BF)
+    w_outs.finish()
+    arrived_t_ref[...] = jnp.transpose(arrived.astype(F32)).astype(jnp.int32)
+
     emb_f = emb_ref[rows_of(tx), :].astype(F32)
-    first, second = out_sum.finish()
-    y = emb_f + part_ref[rows_of(tx), :].astype(F32) + jnp.concatenate([first, second], axis=0)
-
-    y_factor = unit_factor(y)
-    y_unit = (y * y_factor).astype(BF)
-    last = iota((Q, 1), 0) == Q - 1
     follow = jnp.where(
-        last,
+        iota((Q, 1), 0) == Q - 1,
         emb_ref[rows_of(right), :].astype(F32)[0:1, :],
         pltpu.roll(emb_f, Q - 1, 0),
     )
     follow_factor = unit_factor(follow)
     follow_unit = (follow * follow_factor).astype(BF).astype(F32)
-    y_unit_f = y_unit.astype(F32)
-    t = iota((Q, 1), 0) + tx * Q
-    segment = users.segment(t)
-    valid = users.segment(t + 1) == segment
+    t_row = iota((1, 1024), 1)
+    segment = users.segment(t_row)
+    valid = users.segment(t_row + 1) == segment
+    users_of = [jnp.where(segment == u, 1.0, 0.0) for u in range(4)]
+    gates.finish()
+
+    for b in range(4):
+        at = slice(b * Q, (b + 1) * Q)
+        gated = jnp.concatenate(
+            [gated_ref[h * 1024 + b * Q : h * 1024 + (b + 1) * Q, :] for h in range(4)], axis=1
+        )
+        y = emb_ref[at, :].astype(F32) + mm(gated, w_out_ref[...])
+        factor = unit_factor(y)
+        y_unit = (y * factor).astype(BF)
+        y_ref[at, :] = y
+        y_factor_ref[at, :] = jnp.broadcast_to(factor, (Q, DH))
+        y_unit_ref[at, :] = y_unit
+        grown = jnp.exp(sharpness * mm_nt(unit_ref[...], y_unit))
+        grown = jnp.concatenate(
+            [grown[u * DH : (u + 1) * DH, :] * users_of[u][:, at] for u in range(4)], axis=0
+        )
+        grown_ref[:, at] = grown
+        total_ref[tx, :, at] = jnp.sum(grown, axis=0, keepdims=True)
+
+    y_unit_f = y_unit_ref[rows_of(tx), :].astype(F32)
     grown_pos = jnp.exp(sharpness * row_sum(y_unit_f * follow_unit))
-    total = grown_pos
-    mine = [jnp.where(segment == u, 1.0, 0.0) for u in range(4)]
-    units.finish()
-    for c in range(4):
-        grown = jnp.exp(sharpness * mm_nt(y_unit, unit_ref[c * 512 : (c + 1) * 512, :]))
-        grown = jnp.concatenate(
-            [grown[:, u * 128 : (u + 1) * 128] * mine[u] for u in range(4)], axis=1
-        )
-        total = total + row_sum(grown)
-        share_ref[c] = grown
-    scaled = jnp.where(valid, sharpness / total, 0.0)
-    d_pos = jnp.where(valid, sharpness * (grown_pos / total - 1.0), 0.0)
-    d_unit = d_pos * follow_unit
-    for c in range(4):
-        d_unit = d_unit + mm(
-            (share_ref[c] * scaled).astype(BF), unit_ref[c * 512 : (c + 1) * 512, :]
-        )
-    d_rows = unit_back(d_unit, y, y_factor)
-    dout_ref[rows_of(tx), :] = d_rows.astype(BF)
-    douts = Gather(ring(3), dout_ref, Q)
-    douts.start()
-    neg_sum = Scatter(ring(4), dneg_ref, neg_land, neg_on, 512)
-
-    def neg_grads(b):
-        dneg_ref[rows_of(b, 512), :] = mm_tn((share_ref[b] * scaled).astype(BF), y_unit).astype(BF)
-
-    neg_grads(far)
+    own_lanes = pl.ds(pl.multiple_of(tx * Q, Q), Q)
+    grown_pos_row = jnp.transpose(jnp.broadcast_to(grown_pos, (Q, DH)))[0:1, :]
+    total_ref[tx, :, own_lanes] += grown_pos_row
+    totals = [
+        Ring(dp, tx, total_send, total_recv).copy(total_ref.at[tx], total_ref.at[tx], i, to)
+        for i, to in enumerate((right, left, far))
+    ]
+    for c in totals:
+        c.start()
+    for c in totals:
+        c.wait_recv()
+    total = total_ref[0] + total_ref[1] + total_ref[2] + total_ref[3]
+    whole_ref[...] = jnp.where(valid, sharpness / total, 0.0)
+    scaled_own = jnp.transpose(jnp.broadcast_to(whole_ref[:, own_lanes], (DH, Q)))[:, 0:1]
+    d_pos = jnp.where(scaled_own > 0.0, scaled_own * grown_pos - sharpness, 0.0)
+    d_unit_pos = d_pos * follow_unit
+    gate_sum = Scatter(ring(3), dgated_ref, dgated_land, dgated_on, 1024)
+    for b in range(4):
+        at = slice(b * Q, (b + 1) * Q)
+        shares = (grown_ref[:, at] * whole_ref[:, at]).astype(BF)
+        shares_ref[:, at] = shares
+        d_unit = mm_tn(shares, unit_ref[...]) + jnp.where(tx == b, d_unit_pos, 0.0)
+        d_rows = unit_back(d_unit, y_ref[at, :], y_factor_ref[at, :][:, 0:1])
+        drows_ref[at, :] = d_rows
+        d_gated = mm_nt(d_rows.astype(BF), w_out_ref[...]).astype(BF)
+        for h in range(4):
+            dgated_ref[h * 1024 + b * Q : h * 1024 + (b + 1) * Q, :] = d_gated[
+                :, h * DH : (h + 1) * DH
+            ]
+        if b == 1:
+            gate_sum.first[0].start()
+            gate_sum.first[3].start()
+    gate_sum.first[1].start()
+    gate_sum.first[2].start()
+
+    d_neg = unit_back(
+        mm(shares_ref[...], y_unit_ref[...]),
+        neg_ref[...].astype(F32),
+        unit_factor(neg_ref[...].astype(F32)),
+    )
+    wait_rows(neg_out, (OWNERS - 1) * 16, all_send.at[2])
+    put_slots(d_neg.astype(BF), slot_n, neg_out, CAP_N)
+    gate_sum.forward()
+    spread_all(neg_out, neg_back, 16, all_send.at[4], all_recv.at[4], dp, tx)
+    for h in range(4):
+        dout_part[h * DH : (h + 1) * DH, :] = mm_tn(
+            gated_ref[h * 1024 : (h + 1) * 1024, :], drows_ref[...].astype(BF)
+        ).astype(BF)
+    w_out_sum = Scatter(ring(4), dout_part, dout_land, dout_on, DH)
+    w_out_sum.start()
     d_follow = unit_back(d_pos * y_unit_f, follow, follow_factor)
-    rest_ref[0:Q, :] = d_rows + jnp.where(t == tx * Q, 0.0, pltpu.roll(d_follow, 1, 0))
+    rest_ref[0:Q, :] = jnp.where(iota((Q, 1), 0) == 0, 0.0, pltpu.roll(d_follow, 1, 0))
     rest_ref[Q : Q + 8, :] = jnp.where(iota((8, 1), 0) == 0, d_follow[Q - 1 : Q, :], 0.0)
-    douts.forward()
-    neg_sum.first[0].start()
-    neg_sum.first[1].start()
-    neg_grads(right)
-    neg_sum.first[2].start()
-    neg_grads(left)
-    neg_sum.first[3].start()
-    neg_grads(tx)
-
     dkey_ref[...] = jnp.zeros_like(dkey_ref)
     dvalue_ref[...] = jnp.zeros_like(dvalue_ref)
-    dwout_ref[...] = jnp.zeros_like(dwout_ref)
+    halves = gate_sum.finish()
 
     def attend_back(b):
-        at, kr = rows_of(b), keys_of(b)
-        d_out = dout_ref[at, :]
-        d_gated = mm_nt(d_out, w_out_ref[...]).astype(BF).astype(F32)
-        dwout_ref[...] += mm_tn(gated_ref[at, :], d_out)
+        at = slice(b * Q, (b + 1) * Q)
+        kr, _ = keys_of(b)
+        n = kr.stop - kr.start
+        half = halves[b // 2][(b % 2) * Q : (b % 2 + 1) * Q, :]
+        d_gated = half + dgated_ref[pl.ds(mine + b * Q, Q), :].astype(F32)
         mixed = mixed_ref[at, :]
         dgate_ref[at, :] = (d_gated * mixed).astype(BF)
         d_mixed = normal_back(
             d_gated * proj_ref[at, 0:128].astype(F32), mixed, factor_ref[at, :][:, 0:1]
         ).astype(BF)
-        d_scores = (mm_nt(d_mixed, proj_ref[kr, 128:256]) * dweights_ref[at, :]).astype(BF)
+        d_scores = (mm_nt(d_mixed, proj_ref[kr, 128:256]) * dweights_ref[at, 0:n]).astype(BF)
         dquery_ref[at, :] = mm(d_scores, proj_ref[kr, 384:512]).astype(BF)
         dkey_ref[kr, :] += mm_tn(d_scores, proj_ref[at, 256:384])
-        dvalue_ref[kr, :] += mm_tn(weights_ref[at, :], d_mixed)
-
-    attend_back(tx)
-    for c in douts.first[2:]:
-        c.wait_recv()
-    attend_back(left)
-    attend_back(right)
-    neg_sum.forward()
-    for c in douts.second:
-        c.wait_recv()
-    attend_back(far)
+        dvalue_ref[kr, :] += mm_tn(weights_ref[at, 0:n], d_mixed)
+
+    attend_back(0)
+    attend_back(1)
+    w_out_sum.forward()
+    attend_back(2)
+    attend_back(3)
 
     def project_back(b):
         at = rows_of(b)
@@ -681,7 +726,8 @@
         d_pre = (d_proj * slope_ref[at, :]).astype(BF)
         dpre_ref[at, :] = d_pre
         normed, factor = normal(emb_ref[at, :].astype(F32))
-        return normal_back(mm_nt(d_pre, w_in_ref[...]).astype(BF).astype(F32), normed, factor)
+        d_normed = mm_nt(d_pre, w_in_ref[...]).astype(BF).astype(F32)
+        return normal_back(d_normed, normed, factor) + drows_ref[at, :]
 
     emb_sum = Scatter(ring(5), demb_ref, emb_land, emb_on, Q)
     demb_ref[rows_of(far), :] = project_back(far).astype(BF)
@@ -698,9 +744,11 @@
     emb_sum.forward()
 
     d_win = mm_tn(normed_ref[...], dpre_ref[...]).astype(BF)
+    first, second = w_out_sum.finish()
+    d_wout = jnp.concatenate([first, second], axis=0) + dout_part[rows_of(tx, DH), :].astype(F32)
     for j in range(4):
         weight_ref[j * D : (j + 1) * D, :] = d_win[:, j * DH : (j + 1) * DH]
-        weight_ref[2048 + j * DH : 2048 + (j + 1) * DH, :] = dwout_ref[
+        weight_ref[2048 + j * DH : 2048 + (j + 1) * DH, :] = d_wout[
             :, j * DH : (j + 1) * DH
         ].astype(BF)
     own = pl.ds(pl.multiple_of(dp * PIECE, 16), PIECE)
@@ -725,20 +773,15 @@
             device_id_type=MESH,
         ).start()
 
+    each_dp(dp, tx, out_piece)
+    weight_in[own] = weight_ref[own]
+
     first, second = emb_sum.finish()
     d_hist = rest_ref[0:Q, :] + jnp.concatenate([first, second], axis=0)
     wait_rows(hist_out, (OWNERS - 1) * 16, all_send.at[1])
     put_slots(d_hist.astype(BF), slot_h, hist_out, CAP_H)
     spread_all(hist_out, hist_back, 16, all_send.at[3], all_recv.at[3], dp, tx)
 
-    first, second = neg_sum.finish()
-    d_neg = dneg_ref[rows_of(tx, 512), :].astype(F32) + jnp.concatenate([first, second], axis=0)
-    wait_rows(neg_out, (OWNERS - 1) * 16, all_send.at[2])
-    put_slots(unit_back(d_neg, neg_f, neg_factor).astype(BF), slot_n, neg_out, CAP_N)
-    spread_all(neg_out, neg_back, 16, all_send.at[4], all_recv.at[4], dp, tx)
-
-    each_dp(dp, tx, out_piece)
-    weight_in[own] = weight_ref[own]
     wait_rows(weight_in, (N_DP - 1) * PIECE, all_recv.at[5])
     total = weight_in[0:PIECE, :].astype(F32)
     for i in range(1, N_DP):
@@ -761,7 +804,7 @@
         move.start()
     for move in results:
         move.wait()
-    for c in hist.first + hist.second + douts.first + douts.second:
+    for c in totals + hist.first + hist.second:
         c.wait_send()
     wait_rows(request_ref, OWNERS - 1, all_send.at[0])
     wait_rows(hist_out, (OWNERS - 1) * 16, all_send.at[3])
@@ -795,9 +838,10 @@
             vm((OWNERS * 16, 128), BF),
             vm((OWNERS * 16, 256), BF),
             vm((D, D), BF),
-            vm((DH, D), BF),
+            vm((D, D), BF),
             vm((1024, D), BF),
-            vm((2048, D), BF),
+            vm((512, D), BF),
+            vm((512, D), BF),
             vm((1024, D), BF),
             vm((1024, D), BF),
             vm((1024, D), F32),
@@ -805,16 +849,22 @@
             vm((1024, KEYS), F32),
             vm((1024, DH), F32),
             vm((1024, DH), F32),
-            vm((1024, DH), BF),
+            vm((4096, DH), BF),
+            vm((1024, D), F32),
+            vm((1024, DH), F32),
             vm((1024, D), BF),
-            vm((6 * 128, D), BF),
-            vm((2 * 128, D), BF),
-            vm((4, Q, 512), F32),
+            vm((512, 1024), F32),
+            vm((512, 1024), BF),
+            vm((4, 1, 1024), F32),
+            vm((1, 1024), F32),
+            vm((1024, D), F32),
+            vm((4096, DH), BF),
+            vm((6 * 512, DH), BF),
+            vm((2 * 512, DH), BF),
+            vm((D, D), BF),
+            vm((6 * 64, D), BF),
+            vm((2 * 64, D), BF),
             vm((1024, D), BF),
-            vm((2048, D), BF),
-            vm((1024, D), BF),
-            vm((6 * 256, D), BF),
-            vm((2 * 256, D), BF),
             vm((6 * 128, D), BF),
             vm((2 * 128, D), BF),
             vm((Q + 8, D), F32),
@@ -823,7 +873,6 @@
             vm((1024, DH), BF),
             vm((1024, DH), F32),
             vm((1024, D), BF),
-            vm((DH, D), F32),
             vm((2560, 128), BF),
             vm((2560, 128), BF),
             vm((PIECE, 128), BF),
@@ -834,6 +883,8 @@
             sem((7,)),
             sem((6, 6)),
             sem((6, 6)),
+            sem((3,)),
+            sem((3,)),
         ],
         compiler_params=pltpu.CompilerParams(
             collective_id=0, has_side_effects=True, vmem_limit_bytes=56 * 1024 * 1024

time: 173 us -> 142 us (0.82)
  Pallas kernels: 172 us -> 141 us
    pallas_call x1, Pallas kernels: 162 us -> 131 us  [layer(): pl.pallas_call(layer_kernel, out_shape=[jax.ShapeDtypeStruct((128, 128),...]
where the time goes in v4:
time: 142 us
  Pallas kernels  141 us (99%)
    pallas_call x1, Pallas kernels, layer(): pl.pallas_call(layer_kernel, out_shape=[jax.ShapeDtypeStruct((128, 128),...  131 us
    pallas_call x1, Pallas kernels, add_rows(): pl.pallas_call(add_kernel, out_shape=[jax.ShapeDtypeStruct((ROWS, D), F32...  10.5 us

profile of v4, /device:TPU:1, one launch (start us, length us, event | category | flops | bytes accessed | tf_op | source)
XLA Modules:
  0.0 142.0 jit_solution(9491576674874023935)
XLA Ops:
  0.6 130.7 %layer.1 = (s32[128,128]{1,0:T(8,128)}, bf16[1536,512]{1,0:T(8,128)(2,1)}, bf16[2560,128]{1,0:T(8,128)(2,1)}) custom-call(s32[1,256]{1,0:T(1,128)} %bitcast.2, s32[4,128]{1,0:T(4,128)} %negs_ref.1, s32[1,4]{1,0:T(1,128)} %lengths_ref.1, bf16[4096,512]{1,0:T(8,128)(2,1)} %table_hbm.1, bf16[4,512,128]{2,1,0:T(8,128)(2,1)} %w_in_hbm.1, bf16[128,512]{1,0:T(8,128)(2,1)} %w_out_hbm.1), custom_call_target="tpu_custom_call" | custom-call | tf_op jit(solution)/shard_map/layer/pallas_call | solution.py:819
  131.3 10.5 %add_rows.1 = (f32[4096,512]{1,0:T(8,128)}, f32[2048,128]{1,0:T(8,128)}, f32[128,512]{1,0:T(8,128)}) custom-call(s32[128,128]{1,0:T(8,128)} %get-tuple-element.9.ids_hbm, bf16[1536,512]{1,0:T(8,128)(2,1)} %get-tuple-element.10.rows_hbm, bf16[2560,128]{1,0:T(8,128)(2,1)} %get-tuple-element.11.weight_hbm), custom_call_target="tpu_custom_call" | custom-call | tf_op jit(solution)/shard_map/add_rows/pallas_call | solution.py:947

commit v5 on v4

--- a/solution.py
+++ b/solution.py
@@ -283,7 +283,7 @@
 
 
 def gather_rows(table, ids_col, out_ref, at):
-    step = 512
+    step = 1024
 
     def one(i, total):
         base = pl.multiple_of(i * step, step)
@@ -411,6 +411,7 @@
     ids_out,
     rows_out,
     weight_out,
+    table_out,
     table_ref,
     request_ref,
     arrived_ref,
@@ -524,9 +525,6 @@
     spread_all(hist_out, hist_in, 16, all_send.at[1], all_recv.at[1], dp, tx)
     w_outs.forward()
     gather_rows(table_ref, jnp.concatenate(columns[4:8], axis=0), picked_ref, 512)
-    gather_rows(table_ref, jnp.concatenate(columns[8:12], axis=0), picked_ref, 1024)
-    spread_chunks(picked_ref, neg_out, 512, CAP_N)
-    spread_all(neg_out, neg_in, 16, all_send.at[2], all_recv.at[2], dp, tx)
 
     wait_rows(hist_in, (OWNERS - 1) * 16, all_recv.at[1])
     emb_ref[rows_of(tx), :] = take_slots(hist_in, slot_h_col, CAP_H)
@@ -542,8 +540,11 @@
         proj_ref[at, :] = (pre * gate).astype(BF)
         slope_ref[at, :] = gate * (1.0 + pre * (1.0 - gate))
 
+    gather_rows(table_ref, jnp.concatenate(columns[8:12], axis=0), picked_ref, 1024)
+    hist.forward()
+    spread_chunks(picked_ref, neg_out, 512, CAP_N)
+    spread_all(neg_out, neg_in, 16, all_send.at[2], all_recv.at[2], dp, tx)
     project(tx)
-    hist.forward()
     for c in hist.first[2:]:
         c.wait_recv()
     project(left)
@@ -776,6 +777,18 @@
     each_dp(dp, tx, out_piece)
     weight_in[own] = weight_ref[own]
 
+    wait_rows(neg_back, (OWNERS - 1) * 16, all_recv.at[4])
+    gather_chunks(neg_back, picked_ref, 512, CAP_N)
+
+    def add_negatives(i, carry):
+        at = pl.ds(pl.multiple_of(i * 512, 512), 512)
+        total = put_rows(arrived_t_ref, picked_ref, i * 512, 4, 512)
+        total = total + put_rows(arrived_t_ref, picked_ref, i * 512, 8, 512)
+        table_ref[at, :] = total.astype(BF)
+        return carry
+
+    lax.fori_loop(0, 4, add_negatives, 0)
+
     first, second = emb_sum.finish()
     d_hist = rest_ref[0:Q, :] + jnp.concatenate([first, second], axis=0)
     wait_rows(hist_out, (OWNERS - 1) * 16, all_send.at[1])
@@ -790,19 +803,20 @@
     weight_sum[own] = total.astype(BF)
     each_dp(dp, tx, back_piece)
 
+    lax.fori_loop(4, 8, add_negatives, 0)
+    keep = pltpu.make_async_copy(table_ref, table_out, load_sems.at[3])
+    keep.start()
     wait_rows(hist_back, (OWNERS - 1) * 16, all_recv.at[3])
     gather_chunks(hist_back, picked_ref, 0, CAP_H)
-    wait_rows(neg_back, (OWNERS - 1) * 16, all_recv.at[4])
-    gather_chunks(neg_back, picked_ref, 512, CAP_N)
     wait_rows(weight_sum, (N_DP - 1) * PIECE, all_recv.at[6])
     results = [
         pltpu.make_async_copy(arrived_t_ref, ids_out, load_sems.at[0]),
-        pltpu.make_async_copy(picked_ref, rows_out, load_sems.at[1]),
+        pltpu.make_async_copy(picked_ref.at[0:512], rows_out, load_sems.at[1]),
         pltpu.make_async_copy(weight_sum, weight_out, load_sems.at[2]),
     ]
     for move in results:
         move.start()
-    for move in results:
+    for move in results + [keep]:
         move.wait()
     for c in totals + hist.first + hist.second:
         c.wait_send()
@@ -820,11 +834,12 @@
         layer_kernel,
         out_shape=[
             jax.ShapeDtypeStruct((128, 128), jnp.int32),
-            jax.ShapeDtypeStruct((12 * OWNERS, D), BF),
+            jax.ShapeDtypeStruct((CAP_H * OWNERS, D), BF),
             jax.ShapeDtypeStruct((2560, 128), BF),
+            jax.ShapeDtypeStruct((ROWS, D), BF),
         ],
         in_specs=[VM, VM, SM, HB, HB, HB],
-        out_specs=[HB] * 3,
+        out_specs=[HB] * 4,
         scratch_shapes=[
             vm((ROWS, D), BF),
             vm((OWNERS, 1, 128), jnp.int32),
@@ -909,7 +924,13 @@
             ]
 
 
-def add_kernel(ids_hbm, rows_hbm, weight_hbm, out_ref, w_in_ref, w_out_ref, ids_ref, rows_ref, weight_ref, sems):
+def put_rows(ids_ref, rows_ref, first, slot, tile):
+    row = jnp.concatenate([ids_ref[slot + j : slot + j + 1, :] for j in range(4)], axis=1)
+    put = one_zero(row == iota((tile, 512), 0) + first)
+    return mm(put, rows_ref[slot * 128 : (slot + 4) * 128, :])
+
+
+def add_kernel(ids_hbm, rows_hbm, weight_hbm, part_ref, out_ref, w_in_ref, w_out_ref, ids_ref, rows_ref, weight_ref, sems):
     tile = out_ref.shape[0]
     step = pl.program_id(0)
 
@@ -925,12 +946,7 @@
         for move in moves:
             move.wait()
 
-    total = jnp.zeros((tile, D), F32)
-    for k in range(0, CAP_H + CAP_N, 4):
-        row = jnp.concatenate([ids_ref[k + j : k + j + 1, :] for j in range(4)], axis=1)
-        put = one_zero(row == iota((tile, 512), 0) + step * tile)
-        total = total + mm(put, rows_ref[k * 128 : (k + 4) * 128, :])
-    out_ref[...] = total
+    out_ref[...] = part_ref[...].astype(F32) + put_rows(ids_ref, rows_ref, step * tile, 0, tile)
     w_in_ref[...] = weight_ref[pl.ds(pl.multiple_of(step * 256, 256), 256), :].astype(F32)
     w_out_ref[...] = jnp.concatenate(
         [
@@ -941,7 +957,7 @@
     ).astype(F32)
 
 
-def add_rows(ids, rows, weight):
+def add_rows(ids, rows, weight, part):
     tile = 512
     anywhere = pl.BlockSpec(memory_space=pl.ANY)
     return pl.pallas_call(
@@ -952,7 +968,7 @@
             jax.ShapeDtypeStruct((DH, D), F32),
         ],
         grid=(ROWS // tile,),
-        in_specs=[anywhere] * 3,
+        in_specs=[anywhere] * 3 + [pl.BlockSpec((tile, D), lambda i: (i, 0))],
         out_specs=[
             pl.BlockSpec((tile, D), lambda i: (i, 0)),
             pl.BlockSpec((256, DH), lambda i: (i, 0)),
@@ -960,18 +976,18 @@
         ],
         scratch_shapes=[
             pltpu.VMEM((128, 128), jnp.int32),
-            pltpu.VMEM((12 * OWNERS, D), BF),
+            pltpu.VMEM((CAP_H * OWNERS, D), BF),
             pltpu.VMEM((2560, 128), BF),
             pltpu.SemaphoreType.DMA((3,)),
         ],
         compiler_params=pltpu.CompilerParams(vmem_limit_bytes=56 * 1024 * 1024),
         name="add_rows",
-    )(ids, rows, weight)
+    )(ids, rows, weight, part)
 
 
 def on_device(table, item_ids, negatives, lengths, w_in, w_out):
-    ids, rows, weight = layer(item_ids.reshape(1, -1), negatives, lengths, table, w_in, w_out)
-    grad_table, grad_w_in, grad_w_out = add_rows(ids, rows, weight)
+    ids, rows, weight, part = layer(item_ids.reshape(1, -1), negatives, lengths, table, w_in, w_out)
+    grad_table, grad_w_in, grad_w_out = add_rows(ids, rows, weight, part)
     return (grad_table, grad_w_in.reshape(4, D, DH), grad_w_out)
 
 

time: 142 us -> 137 us (0.965)
  Pallas kernels: 141 us -> 136 us
    pallas_call x1, Pallas kernels: 131 us -> 126 us  [layer(): pl.pallas_call(layer_kernel, out_shape=[jax.ShapeDtypeStruct((128, 128),...]
where the time goes in v5:
time: 137 us
  Pallas kernels  136 us (99%)
    pallas_call x1, Pallas kernels, layer(): pl.pallas_call(layer_kernel, out_shape=[jax.ShapeDtypeStruct((128, 128),...  126 us
    pallas_call x1, Pallas kernels, add_rows(): pl.pallas_call(add_kernel, out_shape=[jax.ShapeDtypeStruct((ROWS, D), F32...  10.1 us

profile of v5, /device:TPU:1, one launch (start us, length us, event | category | flops | bytes accessed | tf_op | source)
XLA Modules:
  0.0 137.1 jit_solution(7063083814218489622)
XLA Ops:
  0.6 126.2 %layer.1 = (s32[128,128]{1,0:T(8,128)}, bf16[512,512]{1,0:T(8,128)(2,1)}, bf16[2560,128]{1,0:T(8,128)(2,1)}, bf16[4096,512]{1,0:T(8,128)(2,1)}) custom-call(s32[1,256]{1,0:T(1,128)} %bitcast.2, s32[4,128]{1,0:T(4,128)} %negs_ref.1, s32[1,4]{1,0:T(1,128)} %lengths_ref.1, bf16[4096,512]{1,0:T(8,128)(2,1)} %table_hbm.1, bf16[4,512,128]{2,1,0:T(8,128)(2,1)} %w_in_hbm.1, ...), custom_call_target="tpu_custom_call" | custom-call | tf_op jit(solution)/shard_map/layer/pallas_call | solution.py:833
  126.8 10.1 %add_rows.1 = (f32[4096,512]{1,0:T(8,128)}, f32[2048,128]{1,0:T(8,128)}, f32[128,512]{1,0:T(8,128)}) custom-call(s32[128,128]{1,0:T(8,128)} %get-tuple-element.10.ids_hbm, bf16[512,512]{1,0:T(8,128)(2,1)} %get-tuple-element.11.rows_hbm, bf16[2560,128]{1,0:T(8,128)(2,1)} %get-tuple-element.12.weight_hbm, bf16[4096,512]{1,0:T(8,128)(2,1)} %get-tuple-element.13.part_ref), custom_call_target="tpu_custom_call" | custom-call | tf_op jit(solution)/shard_map/add_rows/pallas_call | solution.py:963

commit v6 on v5

--- a/solution.py
+++ b/solution.py
@@ -176,11 +176,18 @@
             c.wait_recv()
             d.start()
 
-    def finish(self):
-        for c in self.first[2:] + self.second:
-            c.wait_recv()
+    def arrived(self, half):
+        self.first[3 - half].wait_recv()
+        self.second[half].wait_recv()
+
+    def sent(self):
         for c in self.first + self.second:
             c.wait_send()
+
+    def finish(self):
+        self.arrived(0)
+        self.arrived(1)
+        self.sent()
 
 
 class Scatter:
@@ -227,17 +234,24 @@
             ).astype(BF)
             self.second[i].start()
 
-    def finish(self):
+    def half(self, i):
         h = self.h
-        for c in self.first[2:] + self.second:
-            c.wait_recv()
+        self.first[3 - i].wait_recv()
+        self.second[i].wait_recv()
+
+        def got(j):
+            return self.land[j * h : (j + 1) * h].astype(F32)
+
+        return got(3 - i) + got(4 + i)
+
+    def sent(self):
         for c in self.first + self.second:
             c.wait_send()
 
-        def got(i):
-            return self.land[i * h : (i + 1) * h].astype(F32)
-
-        return got(3) + got(4), got(2) + got(5)
+    def finish(self):
+        halves = self.half(0), self.half(1)
+        self.sent()
+        return halves
 
 
 def slots_of(ids):
@@ -612,9 +626,11 @@
     segment = users.segment(t_row)
     valid = users.segment(t_row + 1) == segment
     users_of = [jnp.where(segment == u, 1.0, 0.0) for u in range(4)]
-    gates.finish()
+    gates.arrived(0)
 
     for b in range(4):
+        if b == 2:
+            gates.arrived(1)
         at = slice(b * Q, (b + 1) * Q)
         gated = jnp.concatenate(
             [gated_ref[h * 1024 + b * Q : h * 1024 + (b + 1) * Q, :] for h in range(4)], axis=1
@@ -689,7 +705,7 @@
     rest_ref[Q : Q + 8, :] = jnp.where(iota((8, 1), 0) == 0, d_follow[Q - 1 : Q, :], 0.0)
     dkey_ref[...] = jnp.zeros_like(dkey_ref)
     dvalue_ref[...] = jnp.zeros_like(dvalue_ref)
-    halves = gate_sum.finish()
+    halves = [gate_sum.half(0)]
 
     def attend_back(b):
         at = slice(b * Q, (b + 1) * Q)
@@ -710,6 +726,7 @@
     attend_back(0)
     attend_back(1)
     w_out_sum.forward()
+    halves.append(gate_sum.half(1))
     attend_back(2)
     attend_back(3)
 
@@ -820,6 +837,8 @@
         move.wait()
     for c in totals + hist.first + hist.second:
         c.wait_send()
+    gates.sent()
+    gate_sum.sent()
     wait_rows(request_ref, OWNERS - 1, all_send.at[0])
     wait_rows(hist_out, (OWNERS - 1) * 16, all_send.at[3])
     wait_rows(neg_out, (OWNERS - 1) * 16, all_send.at[4])
@@ -930,36 +949,67 @@
     return mm(put, rows_ref[slot * 128 : (slot + 4) * 128, :])
 
 
-def add_kernel(ids_hbm, rows_hbm, weight_hbm, part_ref, out_ref, w_in_ref, w_out_ref, ids_ref, rows_ref, weight_ref, sems):
-    tile = out_ref.shape[0]
-    step = pl.program_id(0)
-
-    @pl.when(step == 0)
-    def _():
-        moves = [
-            pltpu.make_async_copy(ids_hbm, ids_ref, sems.at[0]),
-            pltpu.make_async_copy(rows_hbm, rows_ref, sems.at[1]),
-            pltpu.make_async_copy(weight_hbm, weight_ref, sems.at[2]),
-        ]
-        for move in moves:
-            move.start()
-        for move in moves:
-            move.wait()
-
-    out_ref[...] = part_ref[...].astype(F32) + put_rows(ids_ref, rows_ref, step * tile, 0, tile)
-    w_in_ref[...] = weight_ref[pl.ds(pl.multiple_of(step * 256, 256), 256), :].astype(F32)
+TILES = 8
+
+
+def add_kernel(
+    ids_hbm,
+    rows_hbm,
+    weight_hbm,
+    part_hbm,
+    out_hbm,
+    w_in_hbm,
+    w_out_hbm,
+    ids_ref,
+    rows_ref,
+    weight_ref,
+    part_ref,
+    out_ref,
+    w_in_ref,
+    w_out_ref,
+    in_sems,
+    part_sems,
+    out_sems,
+    w_sems,
+):
+    tile = ROWS // TILES
+    moves = [
+        pltpu.make_async_copy(ids_hbm, ids_ref, in_sems.at[0]),
+        pltpu.make_async_copy(rows_hbm, rows_ref, in_sems.at[1]),
+        pltpu.make_async_copy(weight_hbm, weight_ref, in_sems.at[2]),
+    ]
+    parts, outs = [], []
+    for i in range(TILES):
+        at = pl.ds(i * tile, tile)
+        parts.append(pltpu.make_async_copy(part_hbm.at[at], part_ref.at[at], part_sems.at[i]))
+        outs.append(pltpu.make_async_copy(out_ref.at[at], out_hbm.at[at], out_sems.at[i]))
+    for move in moves + parts:
+        move.start()
+    moves[0].wait()
+    moves[1].wait()
+    for i in range(TILES):
+        at = pl.ds(i * tile, tile)
+        parts[i].wait()
+        out_ref[at, :] = part_ref[at, :].astype(F32) + put_rows(ids_ref, rows_ref, i * tile, 0, tile)
+        outs[i].start()
+    moves[2].wait()
+    w_in_ref[...] = weight_ref[0:2048, :].astype(F32)
     w_out_ref[...] = jnp.concatenate(
-        [
-            weight_ref[pl.ds(pl.multiple_of(2048 + c * 128 + step * 16, 16), 16), :]
-            for c in range(4)
-        ],
-        axis=1,
+        [weight_ref[2048 + c * 128 : 2048 + (c + 1) * 128, :] for c in range(4)], axis=1
     ).astype(F32)
+    weights = [
+        pltpu.make_async_copy(w_in_ref, w_in_hbm, w_sems.at[0]),
+        pltpu.make_async_copy(w_out_ref, w_out_hbm, w_sems.at[1]),
+    ]
+    for move in weights:
+        move.start()
+    for move in outs + weights:
+        move.wait()
 
 
 def add_rows(ids, rows, weight, part):
-    tile = 512
     anywhere = pl.BlockSpec(memory_space=pl.ANY)
+    sem = pltpu.SemaphoreType.DMA
     return pl.pallas_call(
         add_kernel,
         out_shape=[
@@ -967,18 +1017,20 @@
             jax.ShapeDtypeStruct((2048, DH), F32),
             jax.ShapeDtypeStruct((DH, D), F32),
         ],
-        grid=(ROWS // tile,),
-        in_specs=[anywhere] * 3 + [pl.BlockSpec((tile, D), lambda i: (i, 0))],
-        out_specs=[
-            pl.BlockSpec((tile, D), lambda i: (i, 0)),
-            pl.BlockSpec((256, DH), lambda i: (i, 0)),
-            pl.BlockSpec((16, D), lambda i: (i, 0)),
-        ],
+        in_specs=[anywhere] * 4,
+        out_specs=[anywhere] * 3,
         scratch_shapes=[
             pltpu.VMEM((128, 128), jnp.int32),
             pltpu.VMEM((CAP_H * OWNERS, D), BF),
             pltpu.VMEM((2560, 128), BF),
-            pltpu.SemaphoreType.DMA((3,)),
+            pltpu.VMEM((ROWS, D), BF),
+            pltpu.VMEM((ROWS, D), F32),
+            pltpu.VMEM((2048, DH), F32),
+            pltpu.VMEM((DH, D), F32),
+            sem((3,)),
+            sem((TILES,)),
+            sem((TILES,)),
+            sem((2,)),
         ],
         compiler_params=pltpu.CompilerParams(vmem_limit_bytes=56 * 1024 * 1024),
         name="add_rows",

time: 137 us -> 134 us (0.978)
  Pallas kernels: 136 us -> 133 us
    pallas_call x1, Pallas kernels: 10.1 us -> 7.07 us  [add_rows(): pl.pallas_call(add_kernel, out_shape=[jax.ShapeDtypeStruct((ROWS, D), F32...]
where the time goes in v6:
time: 134 us
  Pallas kernels  133 us (99%)
    pallas_call x1, Pallas kernels, layer(): pl.pallas_call(layer_kernel, out_shape=[jax.ShapeDtypeStruct((128, 128),...  126 us
    pallas_call x1, Pallas kernels, add_rows(): pl.pallas_call(add_kernel, out_shape=[jax.ShapeDtypeStruct((ROWS, D), F32...  7.07 us

profile of v6, /device:TPU:1, one launch (start us, length us, event | category | flops | bytes accessed | tf_op | source)
XLA Modules:
  0.0 133.6 jit_solution(12842351996300093284)
XLA Ops:
  0.6 125.7 %layer.1 = (s32[128,128]{1,0:T(8,128)}, bf16[512,512]{1,0:T(8,128)(2,1)}, bf16[2560,128]{1,0:T(8,128)(2,1)}, bf16[4096,512]{1,0:T(8,128)(2,1)}) custom-call(s32[1,256]{1,0:T(1,128)} %bitcast.2, s32[4,128]{1,0:T(4,128)} %negs_ref.1, s32[1,4]{1,0:T(1,128)} %lengths_ref.1, bf16[4096,512]{1,0:T(8,128)(2,1)} %table_hbm.1, bf16[4,512,128]{2,1,0:T(8,128)(2,1)} %w_in_hbm.1, ...), custom_call_target="tpu_custom_call" | custom-call | tf_op jit(solution)/shard_map/layer/pallas_call | solution.py:852
  126.4 7.1 %add_rows.1 = (f32[4096,512]{1,0:T(8,128)}, f32[2048,128]{1,0:T(8,128)}, f32[128,512]{1,0:T(8,128)}) custom-call(s32[128,128]{1,0:T(8,128)} %get-tuple-element.10.ids_hbm, bf16[512,512]{1,0:T(8,128)(2,1)} %get-tuple-element.11.rows_hbm, bf16[2560,128]{1,0:T(8,128)(2,1)} %get-tuple-element.12.weight_hbm, bf16[4096,512]{1,0:T(8,128)(2,1)} %get-tuple-element.13.part_hbm), custom_call_target="tpu_custom_call" | custom-call | tf_op jit(solution)/shard_map/add_rows/pallas_call | solution.py:1013

commit v7 on v6

--- a/solution.py
+++ b/solution.py
@@ -72,18 +72,14 @@
         do(z * 8 + y * 2 + core, x)
 
 
-def each_dp(dp, tx, do):
-    z, y, near = coordinates(dp, tx)
-    mine, other = near[0][0], near[4][0]
+def each_chip(dp, tx, do):
+    z, y, _ = coordinates(dp, tx)
 
     def one(i, carry):
-        base = plane_base(z, y, lax.rem(i * 7, 16))
-        do(base + mine)
-        do(base + other)
+        do(plane_base(z, y, lax.rem(i * 7, 16)))
         return carry
 
     lax.fori_loop(1, 16, one, 0)
-    do(z * 8 + y * 2 + other)
 
 
 def signal(sem, dp, x):
@@ -127,13 +123,15 @@
     pltpu.make_async_copy(ref.at[pl.ds(0, count)], ref.at[pl.ds(0, count)], sem).wait()
 
 
-class Ring:
+class Group:
     def __init__(self, dp, tx, send_sems, recv_sems):
-        self.dp = dp
-        self.tx = tx
-        self.right = lax.rem(tx + 1, 4)
-        self.left = lax.rem(tx + 3, 4)
-        self.far = lax.rem(tx + 2, 4)
+        p, q = lax.rem(tx, 2), lax.rem(dp, 2)
+        self.chip = dp - q
+        self.first_x = tx - p
+        self.role = p * 2 + q
+        self.core = p * 2 + 1 - q
+        self.over = (1 - p) * 2 + q
+        self.cross = (1 - p) * 2 + 1 - q
         self.send_sems = send_sems
         self.recv_sems = recv_sems
 
@@ -143,41 +141,45 @@
             dst_ref=dst,
             send_sem=self.send_sems.at[slot],
             recv_sem=self.recv_sems.at[slot],
-            device_id=(self.dp, to),
+            device_id=(self.chip + lax.rem(to, 2), self.first_x + lax.div(to, 2)),
             device_id_type=MESH,
         )
 
 
 class Gather:
-    def __init__(self, ring, buf, block):
+    def __init__(self, group, buf, block):
         h = block // 2
-        r = ring
+        g = group
 
         def part(t, half):
             return buf.at[pl.ds(pl.multiple_of(t * block + half * h, h), h)]
 
-        self.first = [
-            r.copy(part(r.tx, 0), part(r.tx, 0), 0, r.right),
-            r.copy(part(r.tx, 1), part(r.tx, 1), 1, r.left),
-            r.copy(part(r.tx, 1), part(r.tx, 1), 2, r.right),
-            r.copy(part(r.tx, 0), part(r.tx, 0), 3, r.left),
+        self.first = [g.copy(part(g.role, i), part(g.role, i), i, g.over) for i in range(2)] + [
+            g.copy(part(g.role, i), part(g.role, i), 2 + i, g.core) for i in range(2)
         ]
         self.second = [
-            r.copy(part(r.left, 0), part(r.left, 0), 4, r.right),
-            r.copy(part(r.right, 1), part(r.right, 1), 5, r.left),
+            g.copy(part(g.over, i), part(g.over, i), 4 + i, g.core) for i in range(2)
         ]
 
+    def start_half(self, half):
+        self.first[half].start()
+        self.first[2 + half].start()
+
     def start(self):
-        for c in self.first:
-            c.start()
+        self.start_half(0)
+        self.start_half(1)
 
     def forward(self):
         for c, d in zip(self.first[:2], self.second):
             c.wait_recv()
             d.start()
 
+    def near(self):
+        for c in self.first[2:]:
+            c.wait_recv()
+
     def arrived(self, half):
-        self.first[3 - half].wait_recv()
+        self.first[2 + half].wait_recv()
         self.second[half].wait_recv()
 
     def sent(self):
@@ -191,25 +193,21 @@
 
 
 class Scatter:
-    def __init__(self, ring, part, land, onward, block):
+    def __init__(self, group, part, land, onward, block):
         h = block // 2
-        r = ring
+        g = group
         self.h = h
-        self.ring = r
+        self.group = g
         self.part = part
         self.land = land
         self.onward = onward
         self.block = block
 
-        self.first = [
-            r.copy(self.at(r.far, 0), self.slot(0), 0, r.right),
-            r.copy(self.at(r.far, 1), self.slot(1), 1, r.left),
-            r.copy(self.at(r.right, 1), self.slot(2), 2, r.right),
-            r.copy(self.at(r.left, 0), self.slot(3), 3, r.left),
+        self.first = [g.copy(self.at(g.cross, i), self.slot(i), i, g.core) for i in range(2)] + [
+            g.copy(self.at(g.core, i), self.slot(2 + i), 2 + i, g.core) for i in range(2)
         ]
         self.second = [
-            r.copy(onward.at[pl.ds(0, h)], self.slot(4), 4, r.right),
-            r.copy(onward.at[pl.ds(h, h)], self.slot(5), 5, r.left),
+            g.copy(onward.at[pl.ds(i * h, h)], self.slot(4 + i), 4 + i, g.over) for i in range(2)
         ]
 
     def at(self, t, half):
@@ -221,28 +219,36 @@
     def slot(self, i):
         return self.land.at[pl.ds(i * self.h, self.h)]
 
+    def start_half(self, half):
+        self.first[half].start()
+        self.first[2 + half].start()
+
     def start(self):
-        for c in self.first:
-            c.start()
+        self.start_half(0)
+        self.start_half(1)
+
+    def forward_half(self, i):
+        h = self.h
+        self.first[i].wait_recv()
+        self.onward[i * h : (i + 1) * h] = (
+            self.land[i * h : (i + 1) * h].astype(F32)
+            + self.part[self.span(self.group.over, i)].astype(F32)
+        ).astype(BF)
+        self.second[i].start()
 
     def forward(self):
-        h = self.h
-        for i, t in enumerate((self.ring.right, self.ring.left)):
-            self.first[i].wait_recv()
-            self.onward[i * h : (i + 1) * h] = (
-                self.land[i * h : (i + 1) * h].astype(F32) + self.part[self.span(t, i)].astype(F32)
-            ).astype(BF)
-            self.second[i].start()
+        self.forward_half(0)
+        self.forward_half(1)
 
     def half(self, i):
         h = self.h
-        self.first[3 - i].wait_recv()
+        self.first[2 + i].wait_recv()
         self.second[i].wait_recv()
 
         def got(j):
             return self.land[j * h : (j + 1) * h].astype(F32)
 
-        return got(3 - i) + got(4 + i)
+        return got(2 + i) + got(4 + i)
 
     def sent(self):
         for c in self.first + self.second:
@@ -386,7 +392,7 @@
 
 class Users:
     def __init__(self, lengths_ref):
-        self.lengths = [lengths_ref[0, u] for u in range(4)]
+        self.lengths = [lengths_ref[0:1, u : u + 1] for u in range(4)]
         self.ends = []
         end = 0
         for length in self.lengths:
@@ -408,7 +414,6 @@
 
 VM = pl.BlockSpec(memory_space=pltpu.VMEM)
 HB = pl.BlockSpec(memory_space=pl.ANY)
-SM = pl.BlockSpec(memory_space=pltpu.SMEM)
 Q = 256
 KEYS = 768
 SCALE = DH**-0.5
@@ -426,6 +431,10 @@
     rows_out,
     weight_out,
     table_out,
+    lengths_mine,
+    ids_own,
+    negs_own,
+    lengths_own,
     table_ref,
     request_ref,
     arrived_ref,
@@ -485,51 +494,83 @@
     ring_recv,
     total_send,
     total_recv,
+    move_send,
+    move_recv,
 ):
     dp, tx = position()
     barrier = pltpu.get_barrier_semaphore()
     greet_planes(barrier, dp, tx)
-    loads = [pltpu.make_async_copy(table_hbm, table_ref, load_sems.at[0])]
-    for j in range(4):
-        loads.append(
-            pltpu.make_async_copy(
-                w_in_hbm.at[j], w_in_ref.at[:, j * DH : (j + 1) * DH], load_sems.at[1 + j]
-            )
-        )
-    loads.append(
-        pltpu.make_async_copy(
-            w_out_hbm, w_out_ref.at[pl.ds(pl.multiple_of(tx * DH, DH), DH)], load_sems.at[5]
-        )
-    )
-    for load in loads:
-        load.start()
-
-    def ring(i):
-        return Ring(dp, tx, ring_send.at[i], ring_recv.at[i])
-
-    right, left, far = ring(0).right, ring(0).left, ring(0).far
+    load = pltpu.make_async_copy(table_hbm, table_ref, load_sems.at[0])
+    load.start()
+    lengths_mine[...] = jnp.zeros_like(lengths_mine)
+    lengths_mine[:, 0:4] = lengths_ref[...]
+
+    def group(i):
+        return Group(dp, tx, ring_send.at[i], ring_recv.at[i])
+
+    here = group(0)
+    role, chip, p, q = here.role, here.chip, lax.rem(tx, 2), lax.rem(dp, 2)
+    after = lax.rem(role + 1, 4)
+    group_dp = chip + lax.div(tx, 2)
 
     def rows_of(b, n=Q):
         return pl.ds(pl.multiple_of(b * n, n), n)
 
-    ids, negs = ids_ref[...], neg_row(negs_ref)
+    to_dp, to_x = chip + p, 2 * q + lax.div(tx, 2)
+    moved = [
+        (ids_ref, ids_own),
+        (negs_ref, negs_own),
+        (lengths_mine, lengths_own),
+        (w_out_hbm, w_out_ref.at[rows_of(tx, DH)]),
+    ] + [(w_in_hbm.at[j], w_in_ref.at[:, j * DH : (j + 1) * DH]) for j in range(4)]
+    stays = role == tx
+
+    def remote(i):
+        return pltpu.make_async_remote_copy(
+            src_ref=moved[i][0],
+            dst_ref=moved[i][1],
+            send_sem=move_send.at[i],
+            recv_sem=move_recv.at[i],
+            device_id=(to_dp, to_x),
+            device_id_type=MESH,
+        )
+
+    def moved_in(i):
+        at = w_out_ref.at[rows_of(role, DH)] if i == 3 else moved[i][1]
+        pltpu.make_async_copy(at, at, move_recv.at[i]).wait()
+
+    pl.semaphore_wait(barrier, 22)
+    greet_again(met_sem, dp, tx)
+
+    @pl.when(stays)
+    def _():
+        for i, (src, dst) in enumerate(moved):
+            pltpu.make_async_copy(src, dst, move_recv.at[i]).start()
+
+    @pl.when(jnp.logical_not(stays))
+    def _():
+        for i in range(len(moved)):
+            remote(i).start()
+
+    for i in range(3):
+        moved_in(i)
+
+    ids, negs = ids_own[...], neg_row(negs_own)
     holder_h, hits_h, before_h = slots_of(ids)
     holder_n, hits_n, before_n = slots_of(negs)
     wanted = wanted_rows(ids, hits_h, before_h, 0) + wanted_rows(negs, hits_n, before_n, CAP_H)
-    pl.semaphore_wait(barrier, 22)
-    greet_again(met_sem, dp, tx)
     request_ref[:, 0, :] = wanted.astype(jnp.int32) - 1
     slot_h = holder_h * CAP_H + before_h
     slot_n = holder_n * CAP_N + before_n
 
     pl.semaphore_wait(met_sem, 7)
     spread_all(request_ref, arrived_ref, 1, all_send.at[0], all_recv.at[0], dp, tx)
-    for load in loads:
-        load.wait()
-    w_outs = Gather(ring(1), w_out_ref, DH)
+    load.wait()
+    moved_in(3)
+    w_outs = Gather(group(1), w_out_ref, DH)
     w_outs.start()
     slot_h_col, slot_n_col = as_column(slot_h), as_column(slot_n)
-    users = Users(lengths_ref)
+    users = Users(lengths_own)
     wait_rows(arrived_ref, OWNERS - 1, all_recv.at[0])
 
     arrived = arrived_ref[:, 0, :]
@@ -541,8 +582,8 @@
     gather_rows(table_ref, jnp.concatenate(columns[4:8], axis=0), picked_ref, 512)
 
     wait_rows(hist_in, (OWNERS - 1) * 16, all_recv.at[1])
-    emb_ref[rows_of(tx), :] = take_slots(hist_in, slot_h_col, CAP_H)
-    hist = Gather(ring(0), emb_ref, Q)
+    emb_ref[rows_of(role), :] = take_slots(hist_in, slot_h_col, CAP_H)
+    hist = Gather(group(0), emb_ref, Q)
     hist.start()
 
     def project(b):
@@ -558,18 +599,19 @@
     hist.forward()
     spread_chunks(picked_ref, neg_out, 512, CAP_N)
     spread_all(neg_out, neg_in, 16, all_send.at[2], all_recv.at[2], dp, tx)
-    project(tx)
-    for c in hist.first[2:]:
-        c.wait_recv()
-    project(left)
-    project(right)
+    for i in range(4, 8):
+        moved_in(i)
+    project(role)
+    hist.near()
+    project(here.core)
+    project(here.over)
     for c in hist.second:
         c.wait_recv()
-    project(far)
+    project(here.cross)
 
     arrived_t_ref[...] = jnp.transpose(arrived.astype(F32)).astype(jnp.int32)
 
-    mine = pl.multiple_of(tx * 1024, 1024)
+    mine = pl.multiple_of(role * 1024, 1024)
 
     def keys_of(b):
         low = max(b - 2, 0)
@@ -595,15 +637,13 @@
         factor_ref[at, :] = jnp.broadcast_to(factor, (Q, DH))
         gated_ref[pl.ds(mine + b * Q, Q), :] = (mixed * proj_ref[at, 0:128].astype(F32)).astype(BF)
 
-    gates = Gather(ring(2), gated_ref, 1024)
+    gates = Gather(group(2), gated_ref, 1024)
     attend(0)
     attend(1)
-    gates.first[0].start()
-    gates.first[3].start()
+    gates.start_half(0)
     attend(2)
     attend(3)
-    gates.first[1].start()
-    gates.first[2].start()
+    gates.start_half(1)
 
     wait_rows(neg_in, (OWNERS - 1) * 16, all_recv.at[2])
     neg_ref[...] = take_slots(neg_in, slot_n_col, CAP_N)
@@ -614,10 +654,10 @@
     w_outs.finish()
     arrived_t_ref[...] = jnp.transpose(arrived.astype(F32)).astype(jnp.int32)
 
-    emb_f = emb_ref[rows_of(tx), :].astype(F32)
+    emb_f = emb_ref[rows_of(role), :].astype(F32)
     follow = jnp.where(
         iota((Q, 1), 0) == Q - 1,
-        emb_ref[rows_of(right), :].astype(F32)[0:1, :],
+        emb_ref[rows_of(after), :].astype(F32)[0:1, :],
         pltpu.roll(emb_f, Q - 1, 0),
     )
     follow_factor = unit_factor(follow)
@@ -646,16 +686,16 @@
             [grown[u * DH : (u + 1) * DH, :] * users_of[u][:, at] for u in range(4)], axis=0
         )
         grown_ref[:, at] = grown
-        total_ref[tx, :, at] = jnp.sum(grown, axis=0, keepdims=True)
-
-    y_unit_f = y_unit_ref[rows_of(tx), :].astype(F32)
+        total_ref[role, :, at] = jnp.sum(grown, axis=0, keepdims=True)
+
+    y_unit_f = y_unit_ref[rows_of(role), :].astype(F32)
     grown_pos = jnp.exp(sharpness * row_sum(y_unit_f * follow_unit))
-    own_lanes = pl.ds(pl.multiple_of(tx * Q, Q), Q)
+    own_lanes = pl.ds(pl.multiple_of(role * Q, Q), Q)
     grown_pos_row = jnp.transpose(jnp.broadcast_to(grown_pos, (Q, DH)))[0:1, :]
-    total_ref[tx, :, own_lanes] += grown_pos_row
+    total_ref[role, :, own_lanes] += grown_pos_row
     totals = [
-        Ring(dp, tx, total_send, total_recv).copy(total_ref.at[tx], total_ref.at[tx], i, to)
-        for i, to in enumerate((right, left, far))
+        Group(dp, tx, total_send, total_recv).copy(total_ref.at[role], total_ref.at[role], i, to)
+        for i, to in enumerate((here.over, here.cross, here.core))
     ]
     for c in totals:
         c.start()
@@ -666,12 +706,12 @@
     scaled_own = jnp.transpose(jnp.broadcast_to(whole_ref[:, own_lanes], (DH, Q)))[:, 0:1]
     d_pos = jnp.where(scaled_own > 0.0, scaled_own * grown_pos - sharpness, 0.0)
     d_unit_pos = d_pos * follow_unit
-    gate_sum = Scatter(ring(3), dgated_ref, dgated_land, dgated_on, 1024)
+    gate_sum = Scatter(group(3), dgated_ref, dgated_land, dgated_on, 1024)
     for b in range(4):
         at = slice(b * Q, (b + 1) * Q)
         shares = (grown_ref[:, at] * whole_ref[:, at]).astype(BF)
         shares_ref[:, at] = shares
-        d_unit = mm_tn(shares, unit_ref[...]) + jnp.where(tx == b, d_unit_pos, 0.0)
+        d_unit = mm_tn(shares, unit_ref[...]) + jnp.where(role == b, d_unit_pos, 0.0)
         d_rows = unit_back(d_unit, y_ref[at, :], y_factor_ref[at, :][:, 0:1])
         drows_ref[at, :] = d_rows
         d_gated = mm_nt(d_rows.astype(BF), w_out_ref[...]).astype(BF)
@@ -680,10 +720,9 @@
                 :, h * DH : (h + 1) * DH
             ]
         if b == 1:
-            gate_sum.first[0].start()
-            gate_sum.first[3].start()
-    gate_sum.first[1].start()
-    gate_sum.first[2].start()
+            gate_sum.start_half(0)
+    gate_sum.start_half(1)
+    gate_sum.forward()
 
     d_neg = unit_back(
         mm(shares_ref[...], y_unit_ref[...]),
@@ -692,13 +731,12 @@
     )
     wait_rows(neg_out, (OWNERS - 1) * 16, all_send.at[2])
     put_slots(d_neg.astype(BF), slot_n, neg_out, CAP_N)
-    gate_sum.forward()
     spread_all(neg_out, neg_back, 16, all_send.at[4], all_recv.at[4], dp, tx)
     for h in range(4):
         dout_part[h * DH : (h + 1) * DH, :] = mm_tn(
             gated_ref[h * 1024 : (h + 1) * 1024, :], drows_ref[...].astype(BF)
         ).astype(BF)
-    w_out_sum = Scatter(ring(4), dout_part, dout_land, dout_on, DH)
+    w_out_sum = Scatter(group(4), dout_part, dout_land, dout_on, DH)
     w_out_sum.start()
     d_follow = unit_back(d_pos * y_unit_f, follow, follow_factor)
     rest_ref[0:Q, :] = jnp.where(iota((Q, 1), 0) == 0, 0.0, pltpu.roll(d_follow, 1, 0))
@@ -747,51 +785,62 @@
         d_normed = mm_nt(d_pre, w_in_ref[...]).astype(BF).astype(F32)
         return normal_back(d_normed, normed, factor) + drows_ref[at, :]
 
-    emb_sum = Scatter(ring(5), demb_ref, emb_land, emb_on, Q)
-    demb_ref[rows_of(far), :] = project_back(far).astype(BF)
+    emb_sum = Scatter(group(5), demb_ref, emb_land, emb_on, Q)
+    def send_part(b):
+        next_first = jnp.where((iota((Q, 1), 0) == 0) & (b == after), rest_ref[Q : Q + 1, :], 0.0)
+        demb_ref[rows_of(b), :] = (project_back(b) + next_first).astype(BF)
+
+    send_part(here.cross)
     emb_sum.first[0].start()
     emb_sum.first[1].start()
-    d_right = project_back(right)
-    demb_ref[rows_of(right), :] = (
-        d_right + jnp.where(iota((Q, 1), 0) == 0, rest_ref[Q : Q + 1, :], 0.0)
-    ).astype(BF)
+    send_part(here.over)
+    emb_sum.forward()
+    send_part(here.core)
     emb_sum.first[2].start()
-    demb_ref[rows_of(left), :] = project_back(left).astype(BF)
     emb_sum.first[3].start()
-    rest_ref[0:Q, :] += project_back(tx)
-    emb_sum.forward()
+    rest_ref[0:Q, :] += project_back(role)
 
     d_win = mm_tn(normed_ref[...], dpre_ref[...]).astype(BF)
     first, second = w_out_sum.finish()
-    d_wout = jnp.concatenate([first, second], axis=0) + dout_part[rows_of(tx, DH), :].astype(F32)
+    d_wout = jnp.concatenate([first, second], axis=0) + dout_part[rows_of(role, DH), :].astype(F32)
     for j in range(4):
         weight_ref[j * D : (j + 1) * D, :] = d_win[:, j * DH : (j + 1) * DH]
         weight_ref[2048 + j * DH : 2048 + (j + 1) * DH, :] = d_wout[
             :, j * DH : (j + 1) * DH
         ].astype(BF)
-    own = pl.ds(pl.multiple_of(dp * PIECE, 16), PIECE)
-
-    def out_piece(pd):
+    own = pl.ds(pl.multiple_of(group_dp * PIECE, 16), PIECE)
+
+    def out_piece(base, other):
+        to = base + other
         pltpu.make_async_remote_copy(
-            src_ref=weight_ref.at[pl.ds(pl.multiple_of(pd * PIECE, 16), PIECE)],
+            src_ref=weight_ref.at[pl.ds(pl.multiple_of(to * PIECE, 16), PIECE)],
             dst_ref=weight_in.at[own],
             send_sem=all_send.at[5],
             recv_sem=all_recv.at[5],
-            device_id=(pd, tx),
+            device_id=(base + q, 2 * other + p),
             device_id_type=MESH,
         ).start()
 
-    def back_piece(pd):
+    def back_piece(to):
         pltpu.make_async_remote_copy(
             src_ref=weight_mine,
             dst_ref=weight_sum.at[own],
             send_sem=all_send.at[6],
             recv_sem=all_recv.at[6],
-            device_id=(pd, tx),
+            device_id=(to, role),
             device_id_type=MESH,
         ).start()
 
-    each_dp(dp, tx, out_piece)
+    def out_pieces(base):
+        out_piece(base, 0)
+        out_piece(base, 1)
+
+    def back_pieces(base):
+        back_piece(base)
+        back_piece(base + 1)
+
+    each_chip(dp, tx, out_pieces)
+    out_piece(chip, 1 - lax.div(tx, 2))
     weight_in[own] = weight_ref[own]
 
     wait_rows(neg_back, (OWNERS - 1) * 16, all_recv.at[4])
@@ -817,15 +866,36 @@
     for i in range(1, N_DP):
         total = total + weight_in[i * PIECE : (i + 1) * PIECE, :].astype(F32)
     weight_mine[...] = total.astype(BF)
-    weight_sum[own] = total.astype(BF)
-    each_dp(dp, tx, back_piece)
+    each_chip(dp, tx, back_pieces)
+    back_piece(chip + 1 - q)
+
+    @pl.when(stays)
+    def _():
+        weight_sum[own] = weight_mine[...]
+
+    @pl.when(jnp.logical_not(stays))
+    def _():
+        back_piece(dp)
+
 
     lax.fori_loop(4, 8, add_negatives, 0)
     keep = pltpu.make_async_copy(table_ref, table_out, load_sems.at[3])
     keep.start()
     wait_rows(hist_back, (OWNERS - 1) * 16, all_recv.at[3])
     gather_chunks(hist_back, picked_ref, 0, CAP_H)
-    wait_rows(weight_sum, (N_DP - 1) * PIECE, all_recv.at[6])
+
+    @pl.when(stays)
+    def _():
+        wait_rows(weight_sum, (N_DP - 1) * PIECE, all_recv.at[6])
+        wait_rows(weight_in, (N_DP - 1) * PIECE, all_send.at[6])
+
+    @pl.when(jnp.logical_not(stays))
+    def _():
+        wait_rows(weight_sum, N_DP * PIECE, all_recv.at[6])
+        wait_rows(weight_in, N_DP * PIECE, all_send.at[6])
+        for i in range(len(moved)):
+            remote(i).wait_send()
+
     results = [
         pltpu.make_async_copy(arrived_t_ref, ids_out, load_sems.at[0]),
         pltpu.make_async_copy(picked_ref.at[0:512], rows_out, load_sems.at[1]),
@@ -843,7 +913,6 @@
     wait_rows(hist_out, (OWNERS - 1) * 16, all_send.at[3])
     wait_rows(neg_out, (OWNERS - 1) * 16, all_send.at[4])
     wait_rows(weight_in, (N_DP - 1) * PIECE, all_send.at[5])
-    wait_rows(weight_in, (N_DP - 1) * PIECE, all_send.at[6])
 
 
 def layer(ids, negs, lengths, table, w_in, w_out):
@@ -857,9 +926,13 @@
             jax.ShapeDtypeStruct((2560, 128), BF),
             jax.ShapeDtypeStruct((ROWS, D), BF),
         ],
-        in_specs=[VM, VM, SM, HB, HB, HB],
+        in_specs=[VM, VM, VM, HB, HB, HB],
         out_specs=[HB] * 4,
         scratch_shapes=[
+            vm((1, 128), jnp.int32),
+            vm((1, 256), jnp.int32),
+            vm((4, 128), jnp.int32),
+            vm((1, 128), jnp.int32),
             vm((ROWS, D), BF),
             vm((OWNERS, 1, 128), jnp.int32),
             vm((OWNERS, 1, 128), jnp.int32),
@@ -919,6 +992,8 @@
             sem((6, 6)),
             sem((3,)),
             sem((3,)),
+            sem((8,)),
+            sem((8,)),
         ],
         compiler_params=pltpu.CompilerParams(
             collective_id=0, has_side_effects=True, vmem_limit_bytes=56 * 1024 * 1024

time: 134 us -> 138 us (1.030)
  Pallas kernels: 133 us -> 137 us
    pallas_call x1, Pallas kernels: 126 us -> 130 us  [layer(): pl.pallas_call(layer_kernel, out_shape=[jax.ShapeDtypeStruct((128, 128),...]
where the time goes in v7:
time: 138 us
  Pallas kernels  137 us (99%)
    pallas_call x1, Pallas kernels, layer(): pl.pallas_call(layer_kernel, out_shape=[jax.ShapeDtypeStruct((128, 128),...  130 us
    pallas_call x1, Pallas kernels, add_rows(): pl.pallas_call(add_kernel, out_shape=[jax.ShapeDtypeStruct((ROWS, D), F32...  7.06 us

profile of v7, /device:TPU:1, one launch (start us, length us, event | category | flops | bytes accessed | tf_op | source)
XLA Modules:
  0.0 138.3 jit_solution(9292581081157883179)
XLA Ops:
  0.6 130.4 %layer.1 = (s32[128,128]{1,0:T(8,128)}, bf16[512,512]{1,0:T(8,128)(2,1)}, bf16[2560,128]{1,0:T(8,128)(2,1)}, bf16[4096,512]{1,0:T(8,128)(2,1)}) custom-call(s32[1,256]{1,0:T(1,128)} %bitcast.2, s32[4,128]{1,0:T(4,128)} %negs_ref.1, s32[1,4]{1,0:T(1,128)} %lengths_ref.1, bf16[4096,512]{1,0:T(8,128)(2,1)} %table_hbm.1, bf16[4,512,128]{2,1,0:T(8,128)(2,1)} %w_in_hbm.1, ...), custom_call_target="tpu_custom_call" | custom-call | tf_op jit(solution)/shard_map/layer/pallas_call | solution.py:921
  131.1 7.1 %add_rows.1 = (f32[4096,512]{1,0:T(8,128)}, f32[2048,128]{1,0:T(8,128)}, f32[128,512]{1,0:T(8,128)}) custom-call(s32[128,128]{1,0:T(8,128)} %get-tuple-element.10.ids_hbm, bf16[512,512]{1,0:T(8,128)(2,1)} %get-tuple-element.11.rows_hbm, bf16[2560,128]{1,0:T(8,128)(2,1)} %get-tuple-element.12.weight_hbm, bf16[4096,512]{1,0:T(8,128)(2,1)} %get-tuple-element.13.part_hbm), custom_call_target="tpu_custom_call" | custom-call | tf_op jit(solution)/shard_map/add_rows/pallas_call | solution.py:1088

commit v8 on v7

--- a/solution.py
+++ b/solution.py
@@ -542,16 +542,18 @@
     pl.semaphore_wait(barrier, 22)
     greet_again(met_sem, dp, tx)
 
-    @pl.when(stays)
-    def _():
-        for i, (src, dst) in enumerate(moved):
-            pltpu.make_async_copy(src, dst, move_recv.at[i]).start()
-
-    @pl.when(jnp.logical_not(stays))
-    def _():
-        for i in range(len(moved)):
-            remote(i).start()
-
+    def move(which):
+        @pl.when(stays)
+        def _():
+            for i in which:
+                pltpu.make_async_copy(*moved[i], move_recv.at[i]).start()
+
+        @pl.when(jnp.logical_not(stays))
+        def _():
+            for i in which:
+                remote(i).start()
+
+    move(range(3))
     for i in range(3):
         moved_in(i)
 
@@ -566,20 +568,20 @@
     pl.semaphore_wait(met_sem, 7)
     spread_all(request_ref, arrived_ref, 1, all_send.at[0], all_recv.at[0], dp, tx)
     load.wait()
-    moved_in(3)
-    w_outs = Gather(group(1), w_out_ref, DH)
-    w_outs.start()
     slot_h_col, slot_n_col = as_column(slot_h), as_column(slot_n)
     users = Users(lengths_own)
     wait_rows(arrived_ref, OWNERS - 1, all_recv.at[0])
+    move(range(3, 8))
 
     arrived = arrived_ref[:, 0, :]
     columns = [arrived[:, k : k + 1] for k in range(CAP_H + CAP_N)]
     gather_rows(table_ref, jnp.concatenate(columns[0:4], axis=0), picked_ref, 0)
     spread_chunks(picked_ref, hist_out, 0, CAP_H)
     spread_all(hist_out, hist_in, 16, all_send.at[1], all_recv.at[1], dp, tx)
-    w_outs.forward()
     gather_rows(table_ref, jnp.concatenate(columns[4:8], axis=0), picked_ref, 512)
+    moved_in(3)
+    w_outs = Gather(group(1), w_out_ref, DH)
+    w_outs.start()
 
     wait_rows(hist_in, (OWNERS - 1) * 16, all_recv.at[1])
     emb_ref[rows_of(role), :] = take_slots(hist_in, slot_h_col, CAP_H)
@@ -595,6 +597,7 @@
         proj_ref[at, :] = (pre * gate).astype(BF)
         slope_ref[at, :] = gate * (1.0 + pre * (1.0 - gate))
 
+    w_outs.forward()
     gather_rows(table_ref, jnp.concatenate(columns[8:12], axis=0), picked_ref, 1024)
     hist.forward()
     spread_chunks(picked_ref, neg_out, 512, CAP_N)

time: 138 us -> 137 us (level)
  no operation moved by 1% of the time
where the time goes in v8:
time: 137 us
  Pallas kernels  136 us (99%)
    pallas_call x1, Pallas kernels, layer(): pl.pallas_call(layer_kernel, out_shape=[jax.ShapeDtypeStruct((128, 128),...  129 us
    pallas_call x1, Pallas kernels, add_rows(): pl.pallas_call(add_kernel, out_shape=[jax.ShapeDtypeStruct((ROWS, D), F32...  7.06 us

profile of v8, /device:TPU:1, one launch (start us, length us, event | category | flops | bytes accessed | tf_op | source)
XLA Modules:
  0.0 137.2 jit_solution(13230994484595486086)
XLA Ops:
  0.6 129.3 %layer.1 = (s32[128,128]{1,0:T(8,128)}, bf16[512,512]{1,0:T(8,128)(2,1)}, bf16[2560,128]{1,0:T(8,128)(2,1)}, bf16[4096,512]{1,0:T(8,128)(2,1)}) custom-call(s32[1,256]{1,0:T(1,128)} %bitcast.2, s32[4,128]{1,0:T(4,128)} %negs_ref.1, s32[1,4]{1,0:T(1,128)} %lengths_ref.1, bf16[4096,512]{1,0:T(8,128)(2,1)} %table_hbm.1, bf16[4,512,128]{2,1,0:T(8,128)(2,1)} %w_in_hbm.1, ...), custom_call_target="tpu_custom_call" | custom-call | tf_op jit(solution)/shard_map/layer/pallas_call | solution.py:924
  130.0 7.1 %add_rows.1 = (f32[4096,512]{1,0:T(8,128)}, f32[2048,128]{1,0:T(8,128)}, f32[128,512]{1,0:T(8,128)}) custom-call(s32[128,128]{1,0:T(8,128)} %get-tuple-element.10.ids_hbm, bf16[512,512]{1,0:T(8,128)(2,1)} %get-tuple-element.11.rows_hbm, bf16[2560,128]{1,0:T(8,128)(2,1)} %get-tuple-element.12.weight_hbm, bf16[4096,512]{1,0:T(8,128)(2,1)} %get-tuple-element.13.part_hbm), custom_call_target="tpu_custom_call" | custom-call | tf_op jit(solution)/shard_map/add_rows/pallas_call | solution.py:1091

commit v9 on v6

--- a/solution.py
+++ b/solution.py
@@ -485,6 +485,7 @@
     ring_recv,
     total_send,
     total_recv,
+    keep_sems,
 ):
     dp, tx = position()
     barrier = pltpu.get_barrier_semaphore()
@@ -797,14 +798,21 @@
     wait_rows(neg_back, (OWNERS - 1) * 16, all_recv.at[4])
     gather_chunks(neg_back, picked_ref, 512, CAP_N)
 
-    def add_negatives(i, carry):
-        at = pl.ds(pl.multiple_of(i * 512, 512), 512)
+    keeps = [
+        pltpu.make_async_copy(
+            table_ref.at[pl.ds(i * 512, 512)], table_out.at[pl.ds(i * 512, 512)], keep_sems.at[i]
+        )
+        for i in range(8)
+    ]
+
+    def add_negatives(i):
         total = put_rows(arrived_t_ref, picked_ref, i * 512, 4, 512)
         total = total + put_rows(arrived_t_ref, picked_ref, i * 512, 8, 512)
-        table_ref[at, :] = total.astype(BF)
-        return carry
-
-    lax.fori_loop(0, 4, add_negatives, 0)
+        table_ref[i * 512 : (i + 1) * 512, :] = total.astype(BF)
+        keeps[i].start()
+
+    for i in range(4):
+        add_negatives(i)
 
     first, second = emb_sum.finish()
     d_hist = rest_ref[0:Q, :] + jnp.concatenate([first, second], axis=0)
@@ -820,9 +828,8 @@
     weight_sum[own] = total.astype(BF)
     each_dp(dp, tx, back_piece)
 
-    lax.fori_loop(4, 8, add_negatives, 0)
-    keep = pltpu.make_async_copy(table_ref, table_out, load_sems.at[3])
-    keep.start()
+    for i in range(4, 8):
+        add_negatives(i)
     wait_rows(hist_back, (OWNERS - 1) * 16, all_recv.at[3])
     gather_chunks(hist_back, picked_ref, 0, CAP_H)
     wait_rows(weight_sum, (N_DP - 1) * PIECE, all_recv.at[6])
@@ -833,7 +840,7 @@
     ]
     for move in results:
         move.start()
-    for move in results + [keep]:
+    for move in results + keeps:
         move.wait()
     for c in totals + hist.first + hist.second:
         c.wait_send()
@@ -919,6 +926,7 @@
             sem((6, 6)),
             sem((3,)),
             sem((3,)),
+            sem((8,)),
         ],
         compiler_params=pltpu.CompilerParams(
             collective_id=0, has_side_effects=True, vmem_limit_bytes=56 * 1024 * 1024

time: 134 us -> 134 us (level)
  no operation moved by 1% of the time
where the time goes in v9:
time: 134 us
  Pallas kernels  133 us (99%)
    pallas_call x1, Pallas kernels, layer(): pl.pallas_call(layer_kernel, out_shape=[jax.ShapeDtypeStruct((128, 128),...  126 us
    pallas_call x1, Pallas kernels, add_rows(): pl.pallas_call(add_kernel, out_shape=[jax.ShapeDtypeStruct((ROWS, D), F32...  7.06 us

profile of v9, /device:TPU:1, one launch (start us, length us, event | category | flops | bytes accessed | tf_op | source)
XLA Modules:
  0.0 133.7 jit_solution(6597830491852502382)
XLA Ops:
  0.6 125.8 %layer.1 = (s32[128,128]{1,0:T(8,128)}, bf16[512,512]{1,0:T(8,128)(2,1)}, bf16[2560,128]{1,0:T(8,128)(2,1)}, bf16[4096,512]{1,0:T(8,128)(2,1)}) custom-call(s32[1,256]{1,0:T(1,128)} %bitcast.2, s32[4,128]{1,0:T(4,128)} %negs_ref.1, s32[1,4]{1,0:T(1,128)} %lengths_ref.1, bf16[4096,512]{1,0:T(8,128)(2,1)} %table_hbm.1, bf16[4,512,128]{2,1,0:T(8,128)(2,1)} %w_in_hbm.1, ...), custom_call_target="tpu_custom_call" | custom-call | tf_op jit(solution)/shard_map/layer/pallas_call | solution.py:859
  126.4 7.1 %add_rows.1 = (f32[4096,512]{1,0:T(8,128)}, f32[2048,128]{1,0:T(8,128)}, f32[128,512]{1,0:T(8,128)}) custom-call(s32[128,128]{1,0:T(8,128)} %get-tuple-element.10.ids_hbm, bf16[512,512]{1,0:T(8,128)(2,1)} %get-tuple-element.11.rows_hbm, bf16[2560,128]{1,0:T(8,128)(2,1)} %get-tuple-element.12.weight_hbm, bf16[4096,512]{1,0:T(8,128)(2,1)} %get-tuple-element.13.part_hbm), custom_call_target="tpu_custom_call" | custom-call | tf_op jit(solution)/shard_map/add_rows/pallas_call | solution.py:1021
